TPU v7x, 32 devices: a whole 2x2x4 slice. The times are simulated.
32 devices in a mesh: row: 8 (over y, x, core), col: 4 (over z).
Axes of the slice: x: 2, y: 2, z: 4, core: 2. Of those that a mesh axis runs over, the one named last changes fastest.
Arguments:
- tokens: bfloat16 [8192, 2048], P(('row', 'col')), may hold values from -6 to 6
- seq_lens: int32 [8, 3], P('row'), may hold values from 1 to 512, 1024 in all within a row
- attn_gain: bfloat16 [2048], replicated, may hold values from 0.099609375 to 1.8984375
- query_weight: bfloat16 [2048, 2048], P('row', 'col'), may hold values from -0.125 to 0.125
- keyvalue_weight: bfloat16 [2048, 8, 128], P('row', 'col'), may hold values from -0.125 to 0.125
- output_weight: bfloat16 [2048, 2048], P('row', 'col'), may hold values from -0.5 to 0.5
- mlp_gain: bfloat16 [2048], replicated, may hold values from 0.099609375 to 1.8984375
- hidden_weight: bfloat16 [2048, 2, 8192], P('row', None, 'col'), may hold values from -0.125 to 0.125
- down_weight: bfloat16 [2048, 8192], P('row', 'col'), may hold values from -0.09375 to 0.09375
- out_grad: bfloat16 [8192, 2048], P(('row', 'col')), may hold values from -6 to 6
Outputs:
- block_out: bfloat16 [8192, 2048], P(('row', 'col'))
- grad_tokens: bfloat16 [8192, 2048], P(('row', 'col'))
- grad_attn_gain: float32 [2048], replicated
- grad_query: float32 [2048, 2048], P('row', 'col')
- grad_keyvalue: float32 [2048, 8, 128], P('row', 'col')
- grad_output: float32 [2048, 2048], P('row', 'col')
- grad_mlp_gain: float32 [2048], replicated
- grad_hidden: float32 [2048, 2, 8192], P('row', None, 'col')
- grad_down: float32 [2048, 8192], P('row', 'col')
Inputs may be any that keep to these rules, and one draw needn't show every extreme that they name: Each row of seq_lens belongs to one block of 1024 tokens, sums to 1024, and its largest entry is 512.
All inputs are finite; a program needn't handle non-finite values.
Results may differ from a plain program's by a relative error of at most 0.023.
Values may be sent and summed in bfloat16 or wider, within the bound.
A program may use at most 256 MiB of HBM per device.

v0:
```python
import jax
import jax.numpy as jnp
from jax import lax
from jax.sharding import PartitionSpec as P

HD = 64


epsilon = 1e-05
rope_base = 500000.0
blocked = -1e30


def rope_tables(position):
    indices = jnp.arange(HD // 2, dtype=jnp.float32)
    frequency = rope_base ** (-(indices * 2.0 / HD))
    wavelen = 2.0 * jnp.pi / frequency
    smooth = (8192.0 / wavelen - 1.0) / 3.0
    scaled = jnp.where(
        wavelen > 8192.0, frequency / 32.0, (1.0 - smooth) * frequency / 32.0 + smooth * frequency
    )
    frequency = jnp.where(wavelen < 2048.0, frequency, scaled)
    angles = position.astype(jnp.float32)[:, None] * frequency[None, :]
    return (jnp.cos(angles), jnp.sin(angles))


def rotate(values, cosine, sinusoid):
    halfway = values.shape[-1] // 2
    former = values[..., :halfway]
    latter = values[..., halfway:]
    cos_wide = cosine[:, None, :]
    sin_wide = sinusoid[:, None, :]
    return jnp.concatenate(
        [former * cos_wide - latter * sin_wide, latter * cos_wide + former * sin_wide], axis=-1
    )


def normalize(values, gain):
    scale = lax.rsqrt(jnp.mean(values * values, axis=1, keepdims=True) + epsilon)
    return ((values * scale * gain).astype(jnp.bfloat16), scale)


def norm_back(grad_in, values, scale, gain):
    weighted = grad_in * gain
    inner_sum = jnp.mean(weighted * values, axis=1, keepdims=True)
    return (
        scale * weighted - values * (scale * scale * scale) * inner_sum,
        jnp.sum(grad_in * values * scale, axis=0),
    )


def against(left, right):
    return lax.dot_general(
        left, right, (((1,), (1,)), ((), ())), preferred_element_type=jnp.float32
    )


def over_rows(left, right):
    return lax.dot_general(
        left, right, (((0,), (0,)), ((), ())), preferred_element_type=jnp.float32
    )


def spread(values):
    return lax.all_gather(values, "col", axis=0, tiled=True)


def block_mask(segment, row_begin, finish):
    indices = jnp.arange(finish, dtype=jnp.int32)
    same_seq = segment[row_begin:finish, None] == segment[None, :finish]
    return same_seq & (indices[None, :] <= indices[row_begin:finish, None])


def attention_forward(queries, key_rows, values, segment, block_rows):
    row_total = queries.shape[0]
    factor = HD ** (-0.5)
    outputs = []
    lse_list = []
    for row_begin in range(0, row_total, block_rows):
        finish = row_begin + block_rows
        allowed = block_mask(segment, row_begin, finish)
        scores = (
            jnp.einsum(
                "qkgd,skd->kgqs",
                queries[row_begin:finish],
                key_rows[:finish],
                preferred_element_type=jnp.float32,
            )
            * factor
        )
        scores = jnp.where(allowed[None, None], scores, blocked)
        summit = jnp.max(scores, axis=3, keepdims=True)
        weights = jnp.exp(scores - summit)
        totals = jnp.sum(weights, axis=3, keepdims=True)
        chances = (weights / totals).astype(jnp.bfloat16)
        outputs.append(
            jnp.einsum(
                "kgqs,skd->qkgd", chances, values[:finish], preferred_element_type=jnp.float32
            )
        )
        lse_list.append(summit + jnp.log(totals))
    return (jnp.concatenate(outputs, 0), lse_list)


def attention_backward(queries, key_rows, values, segment, block_rows, lse_list, grad_mixed):
    row_total = queries.shape[0]
    factor = HD ** (-0.5)
    grad_query = []
    grad_key = jnp.zeros(key_rows.shape, jnp.float32)
    grad_value = jnp.zeros(values.shape, jnp.float32)
    for number, row_begin in enumerate(range(0, row_total, block_rows)):
        finish = row_begin + block_rows
        allowed = block_mask(segment, row_begin, finish)
        scores = (
            jnp.einsum(
                "qkgd,skd->kgqs",
                queries[row_begin:finish],
                key_rows[:finish],
                preferred_element_type=jnp.float32,
            )
            * factor
        )
        scores = jnp.where(allowed[None, None], scores, blocked)
        chances = jnp.exp(scores - lse_list[number])
        rounded = chances.astype(jnp.bfloat16)
        grad_block = grad_mixed[row_begin:finish]
        grad_chance = jnp.einsum(
            "qkgd,skd->kgqs", grad_block, values[:finish], preferred_element_type=jnp.float32
        )
        centre = jnp.sum(chances * grad_chance, axis=3, keepdims=True)
        grad_score = (chances * (grad_chance - centre)).astype(jnp.bfloat16)
        grad_query.append(
            jnp.einsum(
                "kgqs,skd->qkgd", grad_score, key_rows[:finish], preferred_element_type=jnp.float32
            )
            * factor
        )
        grad_key = grad_key.at[:finish].add(
            jnp.einsum(
                "kgqs,qkgd->skd",
                grad_score,
                queries[row_begin:finish],
                preferred_element_type=jnp.float32,
            )
            * factor
        )
        grad_value = grad_value.at[:finish].add(
            jnp.einsum("kgqs,qkgd->skd", rounded, grad_block, preferred_element_type=jnp.float32)
        )
    return (jnp.concatenate(grad_query, 0), grad_key, grad_value)


def shards(
    tokens,
    seq_lens,
    attn_gain,
    query_weight,
    keyvalue_weight,
    output_weight,
    mlp_gain,
    hidden_weight,
    down_weight,
    out_grad,
):
    local_rows = tokens.shape[0]
    row_count = local_rows * lax.axis_size("col")
    block_rows = min(512, row_count)
    lengths = seq_lens[0]
    finish = jnp.cumsum(lengths)
    indices = jnp.arange(row_count, dtype=jnp.int32)
    passed = indices[:, None] >= finish[None, :]
    segment = jnp.sum(passed.astype(jnp.int32), axis=1, dtype=jnp.int32)
    position = indices - jnp.sum(jnp.where(passed, lengths[None, :], 0), axis=1, dtype=jnp.int32)
    cosine, sinusoid = rope_tables(position)
    gain_first = attn_gain.astype(jnp.float32)
    gain_second = mlp_gain.astype(jnp.float32)
    full_query, full_keyvalue, full_output, full_hidden, full_down = (
        lax.all_gather(query_weight, "row", axis=0, tiled=True),
        lax.all_gather(keyvalue_weight, "row", axis=0, tiled=True),
        lax.all_gather(output_weight, "row", axis=0, tiled=True),
        lax.all_gather(hidden_weight, "row", axis=0, tiled=True),
        lax.all_gather(down_weight, "row", axis=0, tiled=True),
    )
    model_width = full_query.shape[0]
    head_count = full_query.shape[1] // HD
    pair_count = full_keyvalue.shape[1]
    group_size = head_count // pair_count
    hidden_count = full_down.shape[1]
    inputs = tokens.astype(jnp.float32)
    normal_in, scale_in = normalize(inputs, gain_first)
    rows_in = spread(normal_in)
    queries = jnp.dot(rows_in, full_query, preferred_element_type=jnp.float32).reshape(
        row_count, head_count, HD
    )
    keyvals = jnp.dot(
        rows_in,
        full_keyvalue.reshape(model_width, pair_count * 2 * HD),
        preferred_element_type=jnp.float32,
    ).reshape(row_count, pair_count, 2, HD)
    queries = (
        rotate(queries, cosine, sinusoid)
        .astype(jnp.bfloat16)
        .reshape(row_count, pair_count, group_size, HD)
    )
    key_rows = rotate(keyvals[:, :, 0], cosine, sinusoid).astype(jnp.bfloat16)
    values = keyvals[:, :, 1].astype(jnp.bfloat16)
    mixed_heads, lse_list = attention_forward(queries, key_rows, values, segment, block_rows)
    mixed_heads = mixed_heads.astype(jnp.bfloat16).reshape(row_count, head_count * HD)
    attended = lax.psum_scatter(
        against(mixed_heads, full_output).astype(jnp.bfloat16),
        "col",
        scatter_dimension=0,
        tiled=True,
    ).astype(jnp.float32)
    hidden_in = inputs + attended
    normal_mid, scale_mid = normalize(hidden_in, gain_second)
    rows_mid = spread(normal_mid)
    flat_hidden = full_hidden.reshape(model_width, 2 * hidden_count)
    gate_up = jnp.dot(rows_mid, flat_hidden, preferred_element_type=jnp.float32)
    gate_part = gate_up[:, :hidden_count]
    up_part = gate_up[:, hidden_count:]
    sigmoid_gate = jax.nn.sigmoid(gate_part)
    silu_gate = gate_part * sigmoid_gate
    gated_act = (silu_gate * up_part).astype(jnp.bfloat16)
    block_out = hidden_in + lax.psum_scatter(
        against(gated_act, full_down).astype(jnp.bfloat16), "col", scatter_dimension=0, tiled=True
    ).astype(jnp.float32)
    full_query, full_keyvalue, full_output, full_hidden, full_down = (
        lax.all_gather(query_weight, "row", axis=0, tiled=True),
        lax.all_gather(keyvalue_weight, "row", axis=0, tiled=True),
        lax.all_gather(output_weight, "row", axis=0, tiled=True),
        lax.all_gather(hidden_weight, "row", axis=0, tiled=True),
        lax.all_gather(down_weight, "row", axis=0, tiled=True),
    )
    flat_hidden = full_hidden.reshape(model_width, 2 * hidden_count)
    rows_grad = spread(out_grad)
    grad_gated = jnp.dot(rows_grad, full_down, preferred_element_type=jnp.float32)
    grad_down_part = over_rows(rows_grad, gated_act)
    grad_gate = grad_gated * up_part * sigmoid_gate * (1.0 + gate_part * (1.0 - sigmoid_gate))
    grad_up = grad_gated * silu_gate
    grad_gate_up = jnp.concatenate([grad_gate, grad_up], axis=1).astype(jnp.bfloat16)
    grad_hidden_part = over_rows(rows_mid, grad_gate_up).reshape(model_width, 2, hidden_count)
    grad_mid = lax.psum_scatter(
        against(grad_gate_up, flat_hidden).astype(jnp.bfloat16),
        "col",
        scatter_dimension=0,
        tiled=True,
    ).astype(jnp.float32)
    back_mid, gain_mid_part = norm_back(grad_mid, hidden_in, scale_mid, gain_second)
    grad_hidden_in = out_grad.astype(jnp.float32) + back_mid
    rows_attn = spread(grad_hidden_in.astype(jnp.bfloat16))
    grad_mixed = jnp.dot(rows_attn, full_output, preferred_element_type=jnp.float32).astype(
        jnp.bfloat16
    )
    grad_output_part = over_rows(rows_attn, mixed_heads)
    grad_q_rot, grad_k_rot, grad_value = attention_backward(
        queries,
        key_rows,
        values,
        segment,
        block_rows,
        lse_list,
        grad_mixed.reshape(row_count, pair_count, group_size, HD),
    )
    grad_query = (
        rotate(grad_q_rot.reshape(row_count, head_count, HD), cosine, -sinusoid)
        .astype(jnp.bfloat16)
        .reshape(row_count, head_count * HD)
    )
    grad_key = rotate(grad_k_rot, cosine, -sinusoid)
    grad_keyval = (
        jnp.stack([grad_key, grad_value], axis=2)
        .astype(jnp.bfloat16)
        .reshape(row_count, pair_count * 2 * HD)
    )
    grad_query_part = over_rows(rows_in, grad_query)
    grad_keyvalue_part = over_rows(rows_in, grad_keyval).reshape(model_width, pair_count, 2 * HD)
    flat_keyvalue = full_keyvalue.reshape(model_width, pair_count * 2 * HD)
    grad_in = lax.psum_scatter(
        (against(grad_query, full_query) + against(grad_keyval, flat_keyvalue)).astype(
            jnp.bfloat16
        ),
        "col",
        scatter_dimension=0,
        tiled=True,
    ).astype(jnp.float32)
    back_in, gain_in_part = norm_back(grad_in, inputs, scale_in, gain_first)
    grad_tokens = (grad_hidden_in + back_in).astype(jnp.bfloat16)
    gain_in_sum, gain_mid_sum = lax.psum((gain_in_part, gain_mid_part), ("row", "col"))
    sum_query, sum_keyvalue, sum_output, sum_hidden, sum_down = (
        lax.psum_scatter(
            grad_query_part.astype(jnp.bfloat16), "row", scatter_dimension=0, tiled=True
        ).astype(jnp.float32),
        lax.psum_scatter(
            grad_keyvalue_part.astype(jnp.bfloat16), "row", scatter_dimension=0, tiled=True
        ).astype(jnp.float32),
        lax.psum_scatter(
            grad_output_part.astype(jnp.bfloat16), "row", scatter_dimension=0, tiled=True
        ).astype(jnp.float32),
        lax.psum_scatter(
            grad_hidden_part.astype(jnp.bfloat16), "row", scatter_dimension=0, tiled=True
        ).astype(jnp.float32),
        lax.psum_scatter(
            grad_down_part.astype(jnp.bfloat16), "row", scatter_dimension=0, tiled=True
        ).astype(jnp.float32),
    )
    return (
        block_out.astype(jnp.bfloat16),
        grad_tokens,
        gain_in_sum,
        sum_query,
        sum_keyvalue,
        sum_output,
        gain_mid_sum,
        sum_hidden,
        sum_down,
    )


def solution(mesh):
    return jax.shard_map(
        shards,
        mesh=mesh,
        in_specs=(
            P(("row", "col"), None),
            P("row", None),
            P(),
            P("row", "col"),
            P("row", "col", None),
            P("row", "col"),
            P(),
            P("row", None, "col"),
            P("row", "col"),
            P(("row", "col"), None),
        ),
        out_specs=(
            P(("row", "col"), None),
            P(("row", "col"), None),
            P(),
            P("row", "col"),
            P("row", "col", None),
            P("row", "col"),
            P(),
            P("row", None, "col"),
            P("row", "col"),
        ),
        check_vma=False,
    )
```

profile of v0, /device:TPU:0, one launch (start us, length us, event | category | flops | bytes accessed | tf_op | source)
XLA Modules:
  0.0 1390.3 jit_solution(14106508200416905413)
XLA Ops:
  17.5 18.7 %all-gather.12.cloned.1.call-done = bf16[2048,2,128]{2,1,0:T(2,128)(2,1)} async-done(((bf16[256,2,128]{2,1,0:T(2,128)(2,1)}), bf16[2048,2,128]{2,1,0:T(2,128)(2,1)}) %all-gather.12.cloned.1.call-update) | async-done | bytes 1048592 | tf_op jit(solution)/shard_map/all_gather | solution.py:179
  38.2 80.9 %all-gather.10.cloned.1.call-done = bf16[1024,2048]{1,0:T(8,128)(2,1)} async-done(((bf16[256,2048]{1,0:T(8,128)(2,1)}), bf16[1024,2048]{1,0:T(8,128)(2,1)}) %all-gather.10.cloned.1.call-update) | async-done | bytes 4194320 | tf_op jit(solution)/shard_map/all_gather | solution.py:65
  123.5 23.9 %all-gather.14.cloned.1.call-done = bf16[2048,512]{1,0:T(8,128)(2,1)} async-done(((bf16[256,512]{1,0:T(8,128)(2,1)}), bf16[2048,512]{1,0:T(8,128)(2,1)}) %all-gather.14.cloned.1.call-update) | async-done | bytes 2097168 | tf_op jit(solution)/shard_map/all_gather | solution.py:178
  157.8 7.7 fusion.91
  165.6 8.4 fusion.3
  197.0 76.3 %reduce-scatter.9.cloned.1.call-done = bf16[256,2048]{1,0:T(8,128)(2,1)} async-done(((bf16[1024,2048]{1,0:T(8,128)(2,1)}), bf16[256,2048]{1,0:T(8,128)(2,1)}) %reduce-scatter.9.cloned.1.call-update) | async-done | bytes 1048592 | tf_op jit(solution)/shard_map/reduce_scatter | solution.py:209
  279.1 86.5 %all-gather.20.cloned.1.call-done = bf16[2048,2,2048]{2,1,0:T(2,128)(2,1)} async-done(((bf16[256,2,2048]{2,1,0:T(2,128)(2,1)}), bf16[2048,2,2048]{2,1,0:T(2,128)(2,1)}) %all-gather.20.cloned.1.call-update) | async-done | bytes 16777232 | tf_op jit(solution)/shard_map/all_gather | solution.py:181
  365.6 17.7 %copy.90 = bf16[256,8,2,2048]{3,1,2,0:T(8,128)(2,1)} copy(bf16[256,8,2,2048]{3,2,1,0:T(2,128)(2,1)} %bitcast.193) | data formatting | bytes 33554432
  383.3 65.3 %all-gather.18.cloned.1.call-done = bf16[1024,2048]{1,0:T(8,128)(2,1)} async-done(((bf16[256,2048]{1,0:T(8,128)(2,1)}), bf16[1024,2048]{1,0:T(8,128)(2,1)}) %all-gather.18.cloned.1.call-update) | async-done | bytes 4194320 | tf_op jit(solution)/shard_map/all_gather | solution.py:65
  448.6 23.5 %fusion.95 = f32[1024,4096]{1,0:T(8,128)} fusion(bf16[1024,2048]{1,0:T(8,128)(2,1)} %all-gather.18.cloned.1.call-done, bf16[2048,4096]{1,0:T(8,128)(2,1)} %bitcast.194), kind=kOutput, calls=%fused_computation.162 | convolution fusion | flops 17179869184 | bytes 37748736 | tf_op jit(solution)/shard_map/dot_general | solution.py:219
  472.1 57.5 %all-gather.24.cloned.1.call-done = bf16[1024,2048]{1,0:T(8,128)(2,1)} async-done(((bf16[256,2048]{1,0:T(8,128)(2,1)}), bf16[1024,2048]{1,0:T(8,128)(2,1)}) %all-gather.24.cloned.1.call-update) | async-done | bytes 4194320 | tf_op jit(solution)/shard_map/all_gather | solution.py:65
  529.6 55.0 %all-gather.22.cloned.1.call-done = bf16[2048,2048]{1,0:T(8,128)(2,1)} async-done(((bf16[256,2048]{1,0:T(8,128)(2,1)}), bf16[2048,2048]{1,0:T(8,128)(2,1)}) %all-gather.22.cloned.1.call-update) | async-done | bytes 8388624 | tf_op jit(solution)/shard_map/all_gather | solution.py:182
  584.6 21.0 %multiply_convert_fusion.1 = (bf16[1024,2048]{1,0:T(8,128)(2,1)S(1)}, bf16[1024,2048]{1,0:T(8,128)(2,1)}, bf16[1024,2048]{1,0:T(8,128)(2,1)}) fusion(f32[1024,4096]{1,0:T(8,128)} %fusion.95, bf16[1024,2048]{1,0:T(8,128)(2,1)} %all-gather.24.cloned.1.call-done, bf16[2048,2048]{1,0:T(8,128)(2,1)} %all-gather.22.cloned.1.call-done), kind=kOutput, calls=%fused_computation.25 | convolution fusion | flops 8621391872 | bytes 41943040 | tf_op jit(solution)/shard_map/dot_general | solution.py:237
  607.6 22.8 %fusion.24 = bf16[1024,2048]{1,0:T(8,128)(2,1)} fusion(bf16[2048,4096]{1,0:T(8,128)(2,1)} %bitcast.195, bf16[1024,2048]{1,0:T(8,128)(2,1)} %get-tuple-element.118, bf16[1024,2048]{1,0:T(8,128)(2,1)S(1)} %get-tuple-element.117), kind=kOutput, calls=%fused_computation.48 | convolution fusion | flops 17198743552 | bytes 29360128 | tf_op jit(solution)/shard_map/dot_general | solution.py:53
  630.5 76.9 %reduce-scatter.13.cloned.1.call-done = bf16[256,2048]{1,0:T(8,128)(2,1)} async-done(((bf16[1024,2048]{1,0:T(8,128)(2,1)}), bf16[256,2048]{1,0:T(8,128)(2,1)}) %reduce-scatter.13.cloned.1.call-update) | async-done | bytes 1048592 | tf_op jit(solution)/shard_map/reduce_scatter | solution.py:243
  713.7 25.5 %convolution_convert_fusion = bf16[2048,4096]{1,0:T(8,128)(2,1)} fusion(bf16[1024,2048]{1,0:T(8,128)(2,1)} %all-gather.18.cloned.1.call-done, bf16[1024,2048]{1,0:T(8,128)(2,1)} %get-tuple-element.118, bf16[1024,2048]{1,0:T(8,128)(2,1)} %copy-done.51), kind=kOutput, calls=%fused_computation.9 | convolution fusion | flops 17205035008 | bytes 29360128 | tf_op jit(solution)/shard_map/dot_general | solution.py:59
  739.2 27.9 %convert_element_type.187 = bf16[2048,2,2048]{2,1,0:T(2,128)(2,1)} reshape(bf16[2048,4096]{1,0:T(8,128)(2,1)} %convolution_convert_fusion) | data formatting | bytes 33554432 | tf_op jit(solution)/shard_map/convert_element_type | solution.py:301
  767.1 14.6 %convert_bitcast_fusion = bf16[2048,2048]{0,1:T(8,128)(2,1)} fusion(bf16[1024,2048]{1,0:T(8,128)(2,1)} %get-tuple-element.119, bf16[1024,2048]{1,0:T(8,128)(2,1)} %all-gather.24.cloned.1.call-done), kind=kOutput, calls=%fused_computation.20 | convolution fusion | flops 8594128896 | bytes 16777216 | tf_op jit(solution)/shard_map/dot_general | solution.py:59
  782.6 12.5 all-gather.26.cloned.1.call-done
  800.4 9.5 fusion.7
  809.9 7.7 fusion.9
  821.0 8.5 fusion
  829.5 10.8 fusion.2
  888.2 14.1 %convolution_convert_fusion.1 = bf16[1024,2048]{1,0:T(8,128)(2,1)} fusion(bf16[1024,2048]{1,0:T(8,128)(2,1)} %get-tuple-element.119, bf16[2048,2048]{1,0:T(8,128)(2,1)} %all-gather.22.cloned.1.call-done), kind=kOutput, calls=%fused_computation.49 | convolution fusion | flops 8592031744 | bytes 16777216 | tf_op jit(solution)/shard_map/dot_general | solution.py:53
  904.3 110.7 %all-reduce.6.cloned.1.call-done = bf16[2048,2,2048]{2,1,0:T(2,128)(2,1)} async-done(((bf16[2048,2,2048]{2,1,0:T(2,128)(2,1)}), bf16[2048,2,2048]{2,1,0:T(2,128)(2,1)}) %all-reduce.6.cloned.1.call-update) | async-done | bytes 16777232
  1021.1 69.1 %reduce-scatter.23.cloned.1.call-done = bf16[256,2048]{0,1:T(8,128)(2,1)} async-done(((bf16[2048,2048]{0,1:T(8,128)(2,1)}), bf16[256,2048]{0,1:T(8,128)(2,1)}) %reduce-scatter.23.cloned.1.call-update) | async-done | bytes 1048592 | tf_op jit(solution)/shard_map/reduce_scatter | solution.py:303
  1092.8 37.1 %reduce-scatter.19.cloned.1.call-done = bf16[256,2,128]{2,0,1:T(8,128)(2,1)} async-done(((bf16[2048,2,128]{2,0,1:T(8,128)(2,1)}), bf16[256,2,128]{2,0,1:T(8,128)(2,1)}) %reduce-scatter.19.cloned.1.call-update) | async-done | bytes 131088 | tf_op jit(solution)/shard_map/reduce_scatter | solution.py:294
  1131.6 42.7 %reduce-scatter.21.cloned.1.call-done = bf16[256,512]{1,0:T(8,128)(2,1)} async-done(((bf16[2048,512]{1,0:T(8,128)(2,1)}), bf16[256,512]{1,0:T(8,128)(2,1)}) %reduce-scatter.21.cloned.1.call-update) | async-done | bytes 262160 | tf_op jit(solution)/shard_map/reduce_scatter | solution.py:297
  1176.1 43.0 %reduce-scatter.17.cloned.1.call-done = bf16[256,512]{1,0:T(8,128)(2,1)} async-done(((bf16[2048,512]{1,0:T(8,128)(2,1)}), bf16[256,512]{1,0:T(8,128)(2,1)}) %reduce-scatter.17.cloned.1.call-update) | async-done | bytes 262160 | tf_op jit(solution)/shard_map/reduce_scatter | solution.py:291
  1220.8 77.1 %reduce-scatter.15.cloned.1.call-done = bf16[256,2048]{1,0:T(8,128)(2,1)} async-done(((bf16[1024,2048]{1,0:T(8,128)(2,1)}), bf16[256,2048]{1,0:T(8,128)(2,1)}) %reduce-scatter.15.cloned.1.call-update) | async-done | bytes 1048592 | tf_op jit(solution)/shard_map/reduce_scatter | solution.py:279
  1299.8 43.2 %all-reduce.3 = (f32[2048]{0:T(1024)}, f32[2048]{0:T(1024)}) all-reduce(f32[2048]{0:T(1024)S(1)} %get-tuple-element.111, f32[2048]{0:T(1024)S(1)} %copy-done.33), channel_id=1, replica_groups=mesh['row'=8,'col'=4] {'row','col'}, use_global_device_ids=true, to_apply=%region_18.19 | all-reduce | flops 4096 | bytes 32768 | tf_op jit(solution)/shard_map/psum | solution.py:289
  1343.0 35.6 %reduce-scatter.11.cloned.1.call-done = bf16[256,2048]{1,0:T(8,128)(2,1)} async-done(((bf16[1024,2048]{1,0:T(8,128)(2,1)}), bf16[256,2048]{1,0:T(8,128)(2,1)}) %reduce-scatter.11.cloned.1.call-update) | async-done | bytes 1048592 | tf_op jit(solution)/shard_map/reduce_scatter | solution.py:225
  (224 shorter events, 142.5 us)
Async XLA Ops:
  7.2 28.9 %all-gather.12.cloned.1.call-start = ((), (), s32[]{:S(2)}) async-start(), calls=%async_computation.9 | async-start | bytes 1179648 | tf_op jit(solution)/shard_map/all_gather | solution.py:179
  7.9 111.1 %all-gather.10.cloned.1.call-start = ((), (), s32[]{:S(2)}) async-start(), calls=%async_computation.8 | async-start | bytes 5242880 | tf_op jit(solution)/shard_map/all_gather | solution.py:65
  13.9 133.5 %all-gather.14.cloned.1.call-start = ((), (), s32[]{:S(2)}) async-start(), calls=%async_computation.10 | async-start | bytes 2359296 | tf_op jit(solution)/shard_map/all_gather | solution.py:178
  14.6 175.0 %all-gather.16.cloned.1.call-start = ((), (), s32[]{:S(2)}) async-start(), calls=%async_computation.11 | async-start | bytes 2359296 | tf_op jit(solution)/shard_map/all_gather | solution.py:180
  15.2 258.1 %reduce-scatter.9.cloned.1.call-start = ((), (), s32[]{:S(2)}) async-start(), calls=%async_computation.12 | async-start | bytes 5242880 | tf_op jit(solution)/shard_map/reduce_scatter | solution.py:209
  196.4 169.2 %all-gather.20.cloned.1.call-start = ((), (), s32[]{:S(2)}) async-start(), calls=%async_computation.14 | async-start | bytes 18874368 | tf_op jit(solution)/shard_map/all_gather | solution.py:181
  197.0 251.7 %all-gather.18.cloned.1.call-start = ((), (), s32[]{:S(2)}) async-start(), calls=%async_computation.13 | async-start | bytes 5242880 | tf_op jit(solution)/shard_map/all_gather | solution.py:65
  197.0 512.9 %copy-start.21 = (f32[2048]{0:T(1024)}, f32[2048]{0:T(1024)S(1)}, u32[]{:S(2)}) copy-start(f32[2048]{0:T(1024)S(1)} %convert_element_type.159) | copy-start | bytes 24580
  275.0 435.0 %copy-start.34 = (f32[256]{0:T(256)}, f32[256]{0:T(256)S(1)}, u32[]{:S(2)}) copy-start(f32[256]{0:T(256)S(1)} %get-tuple-element.142) | copy-start | bytes 3076
  275.0 435.0 %copy-start.38 = (f32[256]{0:T(256)}, f32[256]{0:T(256)S(1)}, u32[]{:S(2)}) copy-start(f32[256]{0:T(256)S(1)} %get-tuple-element.141) | copy-start | bytes 3076
  277.6 252.0 %all-gather.24.cloned.1.call-start = ((), (), s32[]{:S(2)}) async-start(), calls=%async_computation.17 | async-start | bytes 5242880 | tf_op jit(solution)/shard_map/all_gather | solution.py:65
  278.3 306.2 %all-gather.22.cloned.1.call-start = ((), (), s32[]{:S(2)}) async-start(), calls=%async_computation.15 | async-start | bytes 9437184 | tf_op jit(solution)/shard_map/all_gather | solution.py:182
  279.1 428.3 %reduce-scatter.13.cloned.1.call-start = ((), (), s32[]{:S(2)}) async-start(), calls=%async_computation.18 | async-start | bytes 5242880 | tf_op jit(solution)/shard_map/reduce_scatter | solution.py:243
  630.5 164.5 %all-gather.26.cloned.1.call-start = ((), (), s32[]{:S(2)}) async-start(), calls=%async_computation.19 | async-start | bytes 5242880 | tf_op jit(solution)/shard_map/all_gather | solution.py:65
  713.6 301.4 %all-reduce.6.cloned.1.call-start = ((), (), s32[]{:S(2)}) async-start(), calls=%async_computation.25 | async-start | bytes 33554432
  767.1 323.1 %reduce-scatter.23.cloned.1.call-start = ((), (), s32[]{:S(2)}) async-start(), calls=%async_computation.24 | async-start | bytes 9437184 | tf_op jit(solution)/shard_map/reduce_scatter | solution.py:303
  781.8 348.0 %reduce-scatter.19.cloned.1.call-start = ((), (), s32[]{:S(2)}) async-start(), calls=%async_computation.22 | async-start | bytes 1179648 | tf_op jit(solution)/shard_map/reduce_scatter | solution.py:294
  859.8 314.5 %reduce-scatter.21.cloned.1.call-start = ((), (), s32[]{:S(2)}) async-start(), calls=%async_computation.23 | async-start | bytes 2359296 | tf_op jit(solution)/shard_map/reduce_scatter | solution.py:297
  865.9 353.1 %reduce-scatter.17.cloned.1.call-start = ((), (), s32[]{:S(2)}) async-start(), calls=%async_computation.21 | async-start | bytes 2359296 | tf_op jit(solution)/shard_map/reduce_scatter | solution.py:291
  880.4 417.6 %reduce-scatter.15.cloned.1.call-start = ((), (), s32[]{:S(2)}) async-start(), calls=%async_computation.20 | async-start | bytes 5242880 | tf_op jit(solution)/shard_map/reduce_scatter | solution.py:279
  887.9 490.6 %reduce-scatter.11.cloned.1.call-start = ((), (), s32[]{:S(2)}) async-start(), calls=%async_computation.16 | async-start | bytes 5242880 | tf_op jit(solution)/shard_map/reduce_scatter | solution.py:225
  904.3 393.7 %copy-start.1 = (bf16[256,2048]{1,0:T(8,128)(2,1)S(1)}, bf16[256,2048]{1,0:T(8,128)(2,1)}, u32[]{:S(2)}) copy-start(bf16[256,2048]{1,0:T(8,128)(2,1)} %param.22) | copy-start | bytes 3145732
  904.3 393.7 %copy-start.28 = (f32[2048]{0:T(1024)S(1)}, f32[2048]{0:T(1024)}, u32[]{:S(2)}) copy-start(f32[2048]{0:T(1024)} %copy-done.27) | copy-start | bytes 24580
  904.3 393.7 %copy-start.37 = (f32[256]{0:T(256)S(1)}, f32[256]{0:T(256)}, u32[]{:S(2)}) copy-start(f32[256]{0:T(256)} %copy-done.36) | copy-start | bytes 3076
  1021.1 278.7 %copy-start.33 = (f32[2048]{0:T(1024)S(1)}, f32[2048]{0:T(1024)}, u32[]{:S(2)}) copy-start(f32[2048]{0:T(1024)} %get-tuple-element.109) | copy-start | bytes 24580
  1021.1 357.5 %copy-start.4 = (bf16[256,2048]{1,0:T(8,128)(2,1)S(1)}, bf16[256,2048]{1,0:T(8,128)(2,1)}, u32[]{:S(2)}) copy-start(bf16[256,2048]{1,0:T(8,128)(2,1)} %reduce-scatter.9.cloned.1.call-done) | copy-start | bytes 3145732
  1021.1 357.5 %copy-start.6 = (bf16[256,2048]{1,0:T(8,128)(2,1)S(1)}, bf16[256,2048]{1,0:T(8,128)(2,1)}, u32[]{:S(2)}) copy-start(bf16[256,2048]{1,0:T(8,128)(2,1)} %param.31) | copy-start | bytes 3145732
  1021.1 357.5 %copy-start.22 = (f32[2048]{0:T(1024)S(1)}, f32[2048]{0:T(1024)}, u32[]{:S(2)}) copy-start(f32[2048]{0:T(1024)} %copy-done.21) | copy-start | bytes 24580
  1021.1 357.5 %copy-start.35 = (f32[256]{0:T(256)S(1)}, f32[256]{0:T(256)}, u32[]{:S(2)}) copy-start(f32[256]{0:T(256)} %copy-done.34) | copy-start | bytes 3076
  1021.1 357.4 %copy-start.39 = (f32[256]{0:T(256)S(1)}, f32[256]{0:T(256)}, u32[]{:S(2)}) copy-start(f32[256]{0:T(256)} %copy-done.38) | copy-start | bytes 3076
  1021.1 357.4 %copy-start.41 = (f32[256]{0:T(256)S(1)}, f32[256]{0:T(256)}, u32[]{:S(2)}) copy-start(f32[256]{0:T(256)} %copy-done.40) | copy-start | bytes 3076
  1021.1 357.4 %copy-start.42 = (f32[256]{0:T(256)S(1)}, f32[256]{0:T(256)}, u32[]{:S(2)}) copy-start(f32[256]{0:T(256)} %get-tuple-element.139) | copy-start | bytes 3076
  (46 other events, 699.4 us)
Sparse Core Ops, SparseCore 0:
  9.9 26.1 all-gather.11
  38.3 80.7 all-gather.9
  121.0 26.4 all-gather.13
  149.2 27.8 all-gather.15
  196.5 76.7 reduce-scatter.8
  275.2 90.3 all-gather.19
  367.8 80.7 all-gather.17
  450.3 79.2 all-gather.23
  531.6 52.9 all-gather.21
  630.6 76.7 reduce-scatter.12
  713.7 81.2 all-gather.25
  798.7 216.3 all-reduce.5
  1018.9 71.2 reduce-scatter.22
  1093.8 35.9 reduce-scatter.18
  1133.0 41.2 reduce-scatter.20
  1177.7 41.2 reduce-scatter.16
  1221.2 76.7 reduce-scatter.14
  1300.2 78.3 reduce-scatter.10
where the time goes:
time: 1400 us; the launch traced here: 1390 us
  waiting for transfers between devices  973 us (70%)
  matrix products  227 us (16%)
  other arithmetic  66.1 us (5%)
  local copies, waits for them, and re-layouts  64.2 us (5%)
  blocking collectives  43.2 us (3%)
  between operations  16.2 us (1%)
    all_gather x4, waiting for transfers between devices, spread(): return lax.all_gather(values, 'col', axis=0, tiled=True)  216 us
    unnamed x19, waiting for transfers between devices  115 us
    all_gather x1, waiting for transfers between devices, shards(): lax.all_gather(hidden_weight, 'row', axis=0, tiled=True)  86.5 us
    reduce_scatter x1, waiting for transfers between devices, shards(): lax.psum_scatter((against(grad_query, full_query) + against(grad_keyval,...  77.1 us
    reduce_scatter x1, waiting for transfers between devices, shards(): lax.psum_scatter(against(grad_gate_up, flat_hidden).astype(jnp.bfloat16),...  76.9 us
    reduce_scatter x1, waiting for transfers between devices, shards(): lax.psum_scatter(against(mixed_heads, full_output).astype(jnp.bfloat16),...  76.3 us
    reduce_scatter x1, waiting for transfers between devices, shards(): lax.psum_scatter(grad_down_part.astype(jnp.bfloat16), 'row', scatter_dime...  69.1 us
    all_gather x1, waiting for transfers between devices, shards(): lax.all_gather(down_weight, 'row', axis=0, tiled=True)  55 us
  transfers between devices with their start and end apart: 18, of which 17 were waited for; matrix products, arithmetic and copies ran while one was open for 21% of the time, Pallas kernels for 0%

commit v1 on v0

v1 whole, which is shorter than its diff:
```python
import functools

import jax
import jax.numpy as jnp
from jax import lax
from jax.experimental import pallas as pl
from jax.experimental.pallas import tpu as pltpu
from jax.sharding import PartitionSpec as P

HD = 64
SEQ_MAX = 512
MESH = pl.DeviceIdType.MESH
ANY = pl.BlockSpec(memory_space=pl.ANY)

epsilon = 1e-05
rope_base = 500000.0
blocked = -1e30
bf16 = jnp.bfloat16
f32 = jnp.float32


def plane_sizes(row_count):
    cores = 2 if row_count % 2 == 0 else 1
    chips = row_count // cores
    first = 2 if chips % 2 == 0 else 1
    return first, chips // first, cores


class Place:
    def __init__(self, row_count, col_count):
        self.rows, self.cols = row_count, col_count
        self.sizes = plane_sizes(row_count)
        na, nb, nk = self.sizes
        self.row = lax.axis_index("row")
        self.col = lax.axis_index("col")
        self.at = (self.row // (nb * nk), (self.row // nk) % nb, self.row % nk)

    def row_of(self, at):
        _, nb, nk = self.sizes
        return (at[0] * nb + at[1]) * nk + at[2]

    def chip_of(self, at):
        return at[0] * self.sizes[1] + at[1]

    def moved(self, axis, step, at=None):
        at = list(self.at if at is None else at)
        size = self.sizes[axis]
        at[axis] = lax.rem(at[axis] + (step % size), size)
        return tuple(at)

    def device(self, axis, step):
        return (self.row_of(self.moved(axis, step)), self.col)

    def greet(self, plane, line):
        barrier = pltpu.get_barrier_semaphore()
        count = 0
        if plane:
            for axis in range(3):
                size = self.sizes[axis]
                for step in {1 % size, (size - 1) % size} - {0}:
                    pl.semaphore_signal(
                        barrier, inc=1, device_id=self.device(axis, step), device_id_type=MESH
                    )
                    count += 1
        if line and self.cols > 1:
            for step, there in self.line_ways():

                @pl.when(there)
                def _(step=step):
                    pl.semaphore_signal(
                        barrier, inc=1, device_id=(self.row, self.col + step), device_id_type=MESH
                    )

        if line and self.cols > 1:
            last = self.cols - 1
            count = count + jnp.minimum(self.col, 1) + jnp.minimum(last - self.col, 1)
        if not isinstance(count, int) or count:
            pl.semaphore_wait(barrier, count)

    def line_ways(self):
        return ((1, self.col < self.cols - 1), (-1, self.col > 0))


def when(condition, action):
    if condition is None:
        action()
    else:
        pl.when(condition)(action)


def remote(src, dst, send_sem, recv_sem, device):
    return pltpu.make_async_remote_copy(
        src_ref=src,
        dst_ref=dst,
        send_sem=send_sem,
        recv_sem=recv_sem,
        device_id=device,
        device_id_type=MESH,
    )


class LineGather:
    def __init__(self, place, own, block, send_sems, recv_sems):
        self.place, self.own, self.block = place, own, block
        self.sends, self.recvs = send_sems, recv_sems

    def copy(self, way, step, origin):
        place = self.place
        source = self.own if step == 1 else self.block(origin)
        return remote(
            source,
            self.block(origin),
            self.sends.at[way, step - 1],
            self.recvs.at[way, step - 1],
            (place.row, place.col + (1, -1)[way]),
        )

    def sends_at(self, way, step):
        col, last = self.place.col, self.place.cols - 1
        if way == 0:
            return (col >= step - 1) & (col < last), col - (step - 1)
        return (col + step - 1 <= last) & (col > 0), col + (step - 1)

    def gets_at(self, way, step):
        col, last = self.place.col, self.place.cols - 1
        if way == 0:
            return col >= step, col - step
        return col + step <= last, col + step

    def send(self, way, step):
        condition, origin = self.sends_at(way, step)
        when(condition, lambda: self.copy(way, step, origin).start())

    def receive(self, way, step):
        condition, origin = self.gets_at(way, step)

        def action():
            self.copy(way, step, origin).wait_recv()

        when(condition, action)
        if step < self.place.cols - 1:
            self.send(way, step + 1)

    def finish(self):
        for step in range(1, self.place.cols):
            for way in (0, 1):
                condition, origin = self.sends_at(way, step)
                when(condition, lambda: self.copy(way, step, origin).wait_send())


class PlaneGather:
    def __init__(self, place, block, send_sems, recv_sems):
        self.place, self.block = place, block
        self.sends, self.recvs = send_sems, recv_sems

    @staticmethod
    def sem_count(sizes):
        na, nb, _ = sizes
        return 2 * na * nb - 1

    def axes(self, half):
        return (1, 0) if half == 0 else (0, 1)

    def counts(self, half):
        first, second = self.axes(half)
        return self.place.sizes[first], self.place.sizes[second]

    def origin(self, half, i, j, core_step=0):
        first, second = self.axes(half)
        at = self.place.moved(first, -i)
        at = self.place.moved(second, -j, at)
        if core_step:
            at = self.place.moved(2, 1, at)
        return self.place.row_of(at)

    def copy(self, half, kind, i, j):
        np_, nq = self.counts(half)
        if kind == 0:
            number, device = i - 1, self.place.device(self.axes(half)[0], 1)
        elif kind == 1:
            number = (np_ - 1) + i * (nq - 1) + (j - 1)
            device = self.place.device(self.axes(half)[1], 1)
        else:
            number = (np_ * nq - 1) + i * nq + j
            device = self.place.device(2, 1)
        return number, device

    def sender(self, half, kind, i, j):
        number, device = self.copy(half, kind, i, j)
        oi, oj = (i - 1, j) if kind == 0 else ((i, j - 1) if kind == 1 else (i, j))
        ref = self.block(self.origin(half, oi, oj), half)
        return remote(ref, ref, self.sends.at[half, number], self.recvs.at[half, number], device)

    def receiver(self, half, kind, i, j):
        number, device = self.copy(half, kind, i, j)
        ref = self.block(self.origin(half, i, j, 1 if kind == 2 else 0), half)
        return remote(ref, ref, self.sends.at[half, number], self.recvs.at[half, number], device)

    def all_copies(self):
        for half in (0, 1):
            np_, nq = self.counts(half)
            for i in range(1, np_):
                yield half, 0, i, 0
            for i in range(np_):
                for j in range(1, nq):
                    yield half, 1, i, j
            if self.place.sizes[2] > 1:
                for i in range(np_):
                    for j in range(nq):
                        yield half, 2, i, j

    def share(self, half, i, j):
        if self.place.sizes[2] > 1:
            self.sender(half, 2, i, j).start()

    def first(self):
        for half in (0, 1):
            if self.counts(half)[0] > 1:
                self.sender(half, 0, 1, 0).start()
        for half in (0, 1):
            self.share(half, 0, 0)

    def second(self):
        for half in (0, 1):
            np_, nq = self.counts(half)
            for i in range(np_):
                if i > 0:
                    self.receiver(half, 0, i, 0).wait_recv()
                    if i < np_ - 1:
                        self.sender(half, 0, i + 1, 0).start()
                if nq > 1:
                    self.sender(half, 1, i, 1).start()
                if i > 0:
                    self.share(half, i, 0)

    def third(self):
        for half in (0, 1):
            np_, nq = self.counts(half)
            for j in range(1, nq):
                for i in range(np_):
                    self.receiver(half, 1, i, j).wait_recv()
                    if j < nq - 1:
                        self.sender(half, 1, i, j + 1).start()
                    self.share(half, i, j)

    def finish(self):
        for copy in self.all_copies():
            self.sender(*copy).wait_send()
            if copy[1] == 2:
                self.receiver(*copy).wait_recv()


def gather_kernel(sizes, count, *refs):
    row_count, col_count = sizes
    own = refs[:count]
    own_act = refs[count]
    full = refs[count + 1 : 2 * count + 1]
    full_act = refs[2 * count + 1]
    local_sems, zs, zr, ps, pr = refs[2 * count + 2 :]
    place = Place(row_count, col_count)
    place.greet(True, True)
    deep = own[0].shape[0]
    half_deep = deep // 2
    token_rows = own_act.shape[0]

    lines = [
        LineGather(
            place,
            own[n],
            lambda j, n=n: full[n].at[j, pl.ds(place.row * deep, deep)],
            zs.at[n],
            zr.at[n],
        )
        for n in range(count)
    ]
    acts = LineGather(
        place,
        own_act,
        lambda j: full_act.at[pl.ds(j * token_rows, token_rows)],
        zs.at[count],
        zr.at[count],
    )

    def keep(n):
        target = (
            full[n].at[place.col, pl.ds(place.row * deep, deep)]
            if n < count
            else full_act.at[pl.ds(place.col * token_rows, token_rows)]
        )
        return pltpu.make_async_copy(own[n] if n < count else own_act, target, local_sems.at[n])

    for n in range(count + 1):
        keep(n).start()
    for line in lines + [acts]:
        for way in (0, 1):
            line.send(way, 1)
    for n in range(count + 1):
        keep(n).wait()

    def inside(n, col):
        return PlaneGather(
            place,
            lambda row, half: full[n].at[
                col, pl.ds(row * deep + half * half_deep, half_deep)
            ],
            ps.at[n, col],
            pr.at[n, col],
        )

    slots = [(0, 0)] + [(way, step) for step in range(1, col_count) for way in (0, 1)]
    entries = [(way, step, n) for way, step in slots for n in range(count)]

    def at_entry(entry):
        way, step, n = entry
        if step == 0:
            return None, place.col
        return lines[n].gets_at(way, step)

    for number in range(len(entries) + 2):
        if number < len(entries):
            way, step, n = entries[number]
            condition, col = at_entry(entries[number])
            if step > 0:
                lines[n].receive(way, step)
            when(condition, lambda: inside(n, col).first())
        if 1 <= number <= len(entries):
            condition, col = at_entry(entries[number - 1])
            m = entries[number - 1][2]
            when(condition, lambda: inside(m, col).second())
        if 2 <= number:
            condition, col = at_entry(entries[number - 2])
            m = entries[number - 2][2]
            when(condition, lambda: inside(m, col).third())
        if number < len(entries):
            way, step, n = entries[number]
            if step > 1 and way == 1 and n == count - 1:
                for other in (0, 1):
                    acts.receive(other, step - 1)
    for other in (0, 1):
        acts.receive(other, col_count - 1)
    for entry in entries:
        condition, col = at_entry(entry)
        m = entry[2]
        when(condition, lambda: inside(m, col).finish())
    for line in lines + [acts]:
        line.finish()


def gather_all(weights, act, row_count, col_count):
    count = len(weights)
    sizes = plane_sizes(row_count)
    deep = weights[0].shape[0]
    steps = max(col_count - 1, 1)
    plane_sems = (count, col_count, 2, PlaneGather.sem_count(sizes))
    moved = sum(w.size for w in weights) * row_count * col_count * 2
    return pl.pallas_call(
        functools.partial(gather_kernel, (row_count, col_count), count),
        out_shape=[
            jax.ShapeDtypeStruct((col_count, row_count * deep, w.shape[1]), bf16) for w in weights
        ]
        + [jax.ShapeDtypeStruct((col_count * act.shape[0], act.shape[1]), bf16)],
        in_specs=[ANY] * (count + 1),
        out_specs=[ANY] * (count + 1),
        scratch_shapes=[
            pltpu.SemaphoreType.DMA((count + 1,)),
            pltpu.SemaphoreType.DMA((count + 1, 2, steps)),
            pltpu.SemaphoreType.DMA((count + 1, 2, steps)),
            pltpu.SemaphoreType.DMA(plane_sems),
            pltpu.SemaphoreType.DMA(plane_sems),
        ],
        compiler_params=pltpu.CompilerParams(collective_id=0, has_side_effects=True),
        cost_estimate=pl.CostEstimate(flops=0, bytes_accessed=moved, transcendentals=0),
        name="gather_weights",
    )(*weights, act)


def line_gather_kernel(sizes, own, full, local_sem, sends, recvs):
    place = Place(*sizes)
    place.greet(False, True)
    rows = own.shape[0]
    line = LineGather(place, own, lambda j: full.at[pl.ds(j * rows, rows)], sends, recvs)
    for way in (0, 1):
        line.send(way, 1)
    keep = pltpu.make_async_copy(own, full.at[pl.ds(place.col * rows, rows)], local_sem)
    keep.start()
    for step in range(1, place.cols):
        for way in (0, 1):
            line.receive(way, step)
    keep.wait()
    line.finish()


def line_gather(own, row_count, col_count, collective_id):
    steps = max(col_count - 1, 1)
    return pl.pallas_call(
        functools.partial(line_gather_kernel, (row_count, col_count)),
        out_shape=jax.ShapeDtypeStruct((col_count * own.shape[0], own.shape[1]), own.dtype),
        in_specs=[ANY],
        out_specs=ANY,
        scratch_shapes=[
            pltpu.SemaphoreType.DMA,
            pltpu.SemaphoreType.DMA((2, steps)),
            pltpu.SemaphoreType.DMA((2, steps)),
        ],
        compiler_params=pltpu.CompilerParams(collective_id=collective_id, has_side_effects=True),
        cost_estimate=pl.CostEstimate(
            flops=0, bytes_accessed=own.size * 2 * col_count, transcendentals=0
        ),
        name="gather_line",
    )(own)


def add_rows(target, source):
    rows = target.shape[0]
    piece = 32 if rows % 32 == 0 else 16

    def body(n, carry):
        at = pl.ds(pl.multiple_of(n * piece, piece), piece)
        target[at] = (target[at].astype(f32) + source[at].astype(f32)).astype(target.dtype)
        return carry

    lax.fori_loop(0, rows // piece, body, 0)


class LineSum:
    def __init__(self, place, own, held, send_sems, recv_sems):
        self.place, self.own, self.held = place, own, held
        self.sends, self.recvs = send_sems, recv_sems

    def target(self, way, distance):
        col, last = self.place.col, self.place.cols - 1
        if way == 0:
            return col + distance <= last, col + distance
        return col >= distance, col - distance

    def gets(self, way, distance):
        col, last = self.place.col, self.place.cols - 1
        there, _ = self.target(way, distance)
        return there & ((col > 0) if way == 0 else (col < last))

    def copy(self, way, distance, source):
        return remote(
            source,
            self.held.at[way, distance - 1],
            self.sends.at[way, distance - 1],
            self.recvs.at[way, distance - 1],
            (self.place.row, self.place.col + (1, -1)[way]),
        )

    def arrived(self, way, distance):
        ref = self.held.at[way, distance]
        return remote(
            ref,
            ref,
            self.sends.at[way, distance],
            self.recvs.at[way, distance],
            (self.place.row, self.place.col + (1, -1)[way]),
        )

    def step(self, way, distance):
        condition, col = self.target(way, distance)
        if distance < self.place.cols - 1:

            def add():
                self.arrived(way, distance).wait_recv()
                add_rows(self.own(col), self.held.at[way, distance])

            when(self.gets(way, distance), add)
        when(condition, lambda: self.copy(way, distance, self.own(col)).start())

    def last(self, out):
        if self.place.cols > 1:
            for way in (0, 1):
                when(self.gets(way, 0), lambda: self.arrived(way, 0).wait_recv())
        own = self.own(self.place.col)
        rows = own.shape[0]
        piece = 32 if rows % 32 == 0 else 16
        has = [self.gets(way, 0) for way in (0, 1)]

        def body(n, carry):
            at = pl.ds(pl.multiple_of(n * piece, piece), piece)
            total = own[at].astype(f32)
            if self.place.cols > 1:
                for way in (0, 1):
                    term = self.held[way, 0, at].astype(f32)
                    total = total + jnp.where(has[way], term, 0.0)
            out[at] = total.astype(out.dtype)
            return carry

        lax.fori_loop(0, rows // piece, body, 0)

    def finish(self):
        for distance in range(1, self.place.cols):
            for way in (0, 1):
                condition, col = self.target(way, distance)
                when(condition, lambda: self.copy(way, distance, self.own(col)).wait_send())


def line_sum_kernel(sizes, terms, out, held, sends, recvs):
    place = Place(*sizes)
    place.greet(False, True)
    rows = out.shape[0]
    line = LineSum(
        place, lambda j: terms.at[pl.ds(pl.multiple_of(j * rows, rows), rows)], held, sends, recvs
    )
    for distance in range(place.cols - 1, 0, -1):
        for way in (0, 1):
            line.step(way, distance)
    line.last(out)
    line.finish()


def line_sum(terms, row_count, col_count, collective_id):
    steps = max(col_count - 1, 1)
    rows, width = terms.shape[0] // col_count, terms.shape[1]
    return pl.pallas_call(
        functools.partial(line_sum_kernel, (row_count, col_count)),
        out_shape=jax.ShapeDtypeStruct((rows, width), f32),
        in_specs=[pl.BlockSpec(memory_space=pltpu.VMEM)],
        out_specs=pl.BlockSpec(memory_space=pltpu.VMEM),
        scratch_shapes=[
            pltpu.VMEM((2, steps, rows, width), bf16),
            pltpu.SemaphoreType.DMA((2, steps)),
            pltpu.SemaphoreType.DMA((2, steps)),
        ],
        compiler_params=pltpu.CompilerParams(
            collective_id=collective_id, has_side_effects=True, vmem_limit_bytes=48 << 20
        ),
        cost_estimate=pl.CostEstimate(
            flops=terms.size, bytes_accessed=terms.size * 2, transcendentals=0
        ),
        name="sum_line",
    )(terms)


class PlaneSum:
    def __init__(self, place, acc, held_core, held_second, held_first, sems):
        self.place, self.acc = place, acc
        self.held = (held_first, held_second, held_core)
        self.sends, self.recvs = sems
        self.half_deep = acc.shape[1] // 2

    @staticmethod
    def counts_of(sizes):
        na, nb, _ = sizes
        return max(na, nb) - 1, max((na - 1) * nb, (nb - 1) * na)

    @staticmethod
    def sem_count(sizes):
        na, nb, _ = sizes
        return na * nb - 1

    def axes(self, half):
        return (1, 0) if half == 0 else (0, 1)

    def counts(self, half):
        first, second = self.axes(half)
        return self.place.sizes[first], self.place.sizes[second]

    def part(self, half, i, j):
        first, second = self.axes(half)
        at = self.place.moved(second, j, self.place.moved(first, i))
        return self.acc.at[
            self.place.chip_of(at), pl.ds(half * self.half_deep, self.half_deep)
        ]

    def copy(self, half, kind, step, i):
        np_, nq = self.counts(half)
        if kind == 1:
            number = (step - 1) * np_ + i
            source = self.part(half, i, nq - step)
            target = self.held[1].at[half, number]
            sem = number
        else:
            source = self.part(half, np_ - step, 0)
            target = self.held[0].at[half, step - 1]
            sem = (nq - 1) * np_ + step - 1
        device = self.place.device(self.axes(half)[1 if kind == 1 else 0], 1)
        return remote(source, target, self.sends.at[half, sem], self.recvs.at[half, sem], device)

    def add(self, half, kind, step, i):
        np_, nq = self.counts(half)
        self.copy(half, kind, step, i).wait_recv()
        if kind == 1:
            add_rows(
                self.part(half, i, nq - step - 1), self.held[1].at[half, (step - 1) * np_ + i]
            )
        else:
            add_rows(self.part(half, np_ - step - 1, 0), self.held[0].at[half, step - 1])

    def first(self):
        for half in (0, 1):
            np_, nq = self.counts(half)
            if nq > 1:
                for i in range(np_ - 1, -1, -1):
                    self.copy(half, 1, 1, i).start()

    def second(self):
        for half in (0, 1):
            np_, nq = self.counts(half)
            for step in range(1, nq):
                for i in range(np_ - 1, -1, -1):
                    self.add(half, 1, step, i)
                    if step < nq - 1:
                        self.copy(half, 1, step + 1, i).start()
                    elif i == np_ - 1 and np_ > 1:
                        self.copy(half, 0, 1, 0).start()
            if nq == 1 and np_ > 1:
                self.copy(half, 0, 1, 0).start()

    def third(self):
        for half in (0, 1):
            np_, _ = self.counts(half)
            for step in range(1, np_):
                self.add(half, 0, step, 0)
                if step < np_ - 1:
                    self.copy(half, 0, step + 1, 0).start()

    def finish(self):
        for half in (0, 1):
            np_, nq = self.counts(half)
            for step in range(1, nq):
                for i in range(np_):
                    self.copy(half, 1, step, i).wait_send()
            for step in range(1, np_):
                self.copy(half, 0, step, 0).wait_send()


def sum_kernel(sizes, count, *refs):
    row_count, col_count = sizes
    terms = refs[:count]
    act_terms = refs[count]
    outs = refs[count + 1 : 2 * count + 1]
    act_out = refs[2 * count + 1]
    refs = refs[2 * count + 2 :]
    per = [refs[6 * n : 6 * n + 6] for n in range(count)]
    act_held, load_sems, cs, cr, ps, pr, zs, zr = refs[6 * count :]
    place = Place(row_count, col_count)
    cores = place.sizes[2]
    core = place.at[2]
    token_rows = act_out.shape[0]

    slots = [(way, step) for step in range(col_count - 1, 0, -1) for way in (0, 1)] + [(0, 0)]
    entries = [(way, step, n) for way, step in slots for n in range(count)]

    acts = LineSum(
        place,
        lambda j: act_terms.at[pl.ds(pl.multiple_of(j * token_rows, token_rows), token_rows)],
        act_held,
        zs.at[count],
        zr.at[count],
    )
    acc = [per[n][0] for n in range(count)]
    lines = [
        LineSum(
            place,
            lambda j, n=n: acc[n].at[j, place.chip_of(place.at)],
            per[n][4],
            zs.at[n],
            zr.at[n],
        )
        for n in range(count)
    ]

    def at_entry(entry):
        way, step, n = entry
        if step == 0:
            return None, place.col
        return lines[n].target(way, step)

    def load(n, col):
        return pltpu.make_async_copy(
            terms[n].at[col, :, core], acc[n].at[col], load_sems.at[n, col]
        )

    def share(n, col):
        return remote(
            terms[n].at[col, :, lax.rem(core + 1, cores)],
            per[n][1].at[col],
            cs.at[n, col],
            cr.at[n, col],
            place.device(2, 1),
        )

    def inside(n, col):
        return PlaneSum(
            place,
            acc[n].at[col],
            per[n][1].at[col],
            per[n][2].at[col],
            per[n][3].at[col],
            (ps.at[n, col], pr.at[n, col]),
        )

    for entry in entries:
        condition, col = at_entry(entry)
        n = entry[2]
        when(condition, lambda: load(n, col).start())
    place.greet(True, True)
    if cores > 1:
        for entry in entries:
            condition, col = at_entry(entry)
            n = entry[2]
            when(condition, lambda: share(n, col).start())
    for way in (0, 1):
        if col_count > 1:
            acts.step(way, col_count - 1)

    def start(n, col):
        load(n, col).wait()
        if cores > 1:
            share(n, col).wait_recv()
            for chip in range(acc[n].shape[1]):
                add_rows(acc[n].at[col, chip], per[n][1].at[col, chip])
        inside(n, col).first()

    for number in range(len(entries) + 2):
        if number < len(entries):
            condition, col = at_entry(entries[number])
            n = entries[number][2]
            when(condition, lambda: start(n, col))
        if 1 <= number <= len(entries):
            condition, col = at_entry(entries[number - 1])
            n = entries[number - 1][2]
            when(condition, lambda: inside(n, col).second())
        if 2 <= number:
            way, step, n = entries[number - 2]
            condition, col = at_entry(entries[number - 2])
            when(condition, lambda: inside(n, col).third())
            if step > 0:
                lines[n].step(way, step)
            else:
                lines[n].last(per[n][5])
                pltpu.make_async_copy(per[n][5], outs[n], load_sems.at[n, place.col]).start()
        if number < len(entries):
            way, step, n = entries[number]
            if 1 < step and way == 1 and n == count - 1:
                for other in (0, 1):
                    acts.step(other, step - 1)
    acts.last(act_out)
    for n in range(count):
        pltpu.make_async_copy(per[n][5], outs[n], load_sems.at[n, place.col]).wait()
    for entry in entries:
        condition, col = at_entry(entry)
        n = entry[2]

        def done():
            if cores > 1:
                share(n, col).wait_send()
            inside(n, col).finish()

        when(condition, done)
    for line in lines + [acts]:
        line.finish()


def sum_all(terms, act_terms, row_count, col_count, act_type):
    count = len(terms)
    sizes = plane_sizes(row_count)
    na, nb, nk = sizes
    chips = na * nb
    deep = terms[0].shape[1] // row_count
    steps = max(col_count - 1, 1)
    firsts, seconds = PlaneSum.counts_of(sizes)
    widths = [t.shape[2] for t in terms]
    token_rows = act_terms.shape[0] // col_count
    scratch = []
    for width in widths:
        scratch += [
            pltpu.VMEM((col_count, chips, deep, width), bf16),
            pltpu.VMEM((col_count, chips, deep, width), bf16),
            pltpu.VMEM((col_count, 2, max(seconds, 1), deep // 2, width), bf16),
            pltpu.VMEM((col_count, 2, max(firsts, 1), deep // 2, width), bf16),
            pltpu.VMEM((2, steps, deep, width), bf16),
            pltpu.VMEM((deep, width), f32),
        ]
    plane_sems = (count, col_count, 2, max(PlaneSum.sem_count(sizes), 1))
    scratch += [
        pltpu.VMEM((2, steps, token_rows, act_terms.shape[1]), bf16),
        pltpu.SemaphoreType.DMA((count, col_count)),
        pltpu.SemaphoreType.DMA((count, col_count)),
        pltpu.SemaphoreType.DMA((count, col_count)),
        pltpu.SemaphoreType.DMA(plane_sems),
        pltpu.SemaphoreType.DMA(plane_sems),
        pltpu.SemaphoreType.DMA((count + 1, 2, steps)),
        pltpu.SemaphoreType.DMA((count + 1, 2, steps)),
    ]
    vmem = pl.BlockSpec(memory_space=pltpu.VMEM)
    return pl.pallas_call(
        functools.partial(sum_kernel, (row_count, col_count), count),
        out_shape=[jax.ShapeDtypeStruct((deep, width), f32) for width in widths]
        + [jax.ShapeDtypeStruct((token_rows, act_terms.shape[1]), act_type)],
        in_specs=[ANY] * count + [vmem],
        out_specs=[ANY] * count + [vmem],
        scratch_shapes=scratch,
        compiler_params=pltpu.CompilerParams(
            collective_id=1, has_side_effects=True, vmem_limit_bytes=60 << 20
        ),
        cost_estimate=pl.CostEstimate(
            flops=0, bytes_accessed=sum(t.size for t in terms) * 4, transcendentals=0
        ),
        name="sum_weights",
    )(
        *[t.reshape(col_count, chips, nk, deep, t.shape[2]) for t in terms],
        act_terms,
    )


def rope_tables(position):
    indices = jnp.arange(HD // 2, dtype=f32)
    frequency = rope_base ** (-(indices * 2.0 / HD))
    wavelen = 2.0 * jnp.pi / frequency
    smooth = (8192.0 / wavelen - 1.0) / 3.0
    scaled = jnp.where(
        wavelen > 8192.0, frequency / 32.0, (1.0 - smooth) * frequency / 32.0 + smooth * frequency
    )
    frequency = jnp.where(wavelen < 2048.0, frequency, scaled)
    angles = position.astype(f32)[:, None] * frequency[None, :]
    return (jnp.cos(angles), jnp.sin(angles))


def rotate(values, cosine, sinusoid):
    halfway = values.shape[-1] // 2
    former = values[..., :halfway]
    latter = values[..., halfway:]
    cos_wide = cosine[:, None, :]
    sin_wide = sinusoid[:, None, :]
    return jnp.concatenate(
        [former * cos_wide - latter * sin_wide, latter * cos_wide + former * sin_wide], axis=-1
    )


def normalize(values, gain):
    scale = lax.rsqrt(jnp.mean(values * values, axis=1, keepdims=True) + epsilon)
    return ((values * scale * gain).astype(bf16), scale)


def norm_back(grad_in, values, scale, gain):
    weighted = grad_in * gain
    inner_sum = jnp.mean(weighted * values, axis=1, keepdims=True)
    return (
        scale * weighted - values * (scale * scale * scale) * inner_sum,
        jnp.sum(grad_in * values * scale, axis=0),
    )


def against(left, right):
    return lax.dot_general(left, right, (((1,), (1,)), ((), ())), preferred_element_type=f32)


def over_rows(left, right):
    return lax.dot_general(left, right, (((0,), (0,)), ((), ())), preferred_element_type=f32)


def matmul(left, right):
    return jnp.dot(left, right, preferred_element_type=f32)


def shift(values, step, col_count):
    if step > 0:
        pairs = [(i, i + step) for i in range(col_count - step)]
    else:
        pairs = [(i, i + step) for i in range(-step, col_count)]
    return lax.ppermute(values, "col", pairs)


def shards(
    tokens,
    seq_lens,
    attn_gain,
    query_weight,
    keyvalue_weight,
    output_weight,
    mlp_gain,
    hidden_weight,
    down_weight,
    out_grad,
):
    row_count, col_count = lax.axis_size("row"), lax.axis_size("col")
    local = tokens.shape[0]
    block_rows = local * col_count
    col = lax.axis_index("col")
    deep = query_weight.shape[0]
    width = tokens.shape[1]
    query_width = query_weight.shape[1]
    pairs = keyvalue_weight.shape[1]
    heads = query_width // HD
    group = heads // pairs
    hidden = down_weight.shape[1]
    back = min(-(-(SEQ_MAX - 1) // local), col_count - 1)

    lengths = seq_lens[0]
    finish = jnp.cumsum(lengths)
    indices = jnp.arange(block_rows, dtype=jnp.int32)
    passed = indices[:, None] >= finish[None, :]
    segment = jnp.sum(passed.astype(jnp.int32), axis=1, dtype=jnp.int32)
    position = indices - jnp.sum(jnp.where(passed, lengths[None, :], 0), axis=1, dtype=jnp.int32)
    own_position = lax.dynamic_slice(position, (col * local,), (local,))
    own_segment = lax.dynamic_slice(segment, (col * local,), (local,))
    padded = jnp.concatenate([jnp.full((back * local,), -1, jnp.int32), segment])
    key_segment = lax.dynamic_slice(padded, (col * local,), ((back + 1) * local,))
    key_index = jnp.arange((back + 1) * local, dtype=jnp.int32) - back * local
    query_index = jnp.arange(local, dtype=jnp.int32)
    allowed = (own_segment[:, None] == key_segment[None, :]) & (
        key_index[None, :] <= query_index[:, None]
    )
    cosine, sinusoid = rope_tables(own_position)
    gain_first = attn_gain.astype(f32)
    gain_second = mlp_gain.astype(f32)

    full_hidden = lax.all_gather(
        hidden_weight.reshape(deep, 2 * hidden), "row", axis=0, tiled=True
    )
    full_down = lax.all_gather(down_weight, "row", axis=0, tiled=True)

    first_weight = jnp.concatenate(
        [query_weight, keyvalue_weight.reshape(deep, pairs * 2 * HD)], axis=1
    )
    full_first, full_output, rows_grad = gather_all(
        [first_weight, output_weight], out_grad, row_count, col_count
    )

    inputs = tokens.astype(f32)
    normal_in, scale_in = normalize(inputs, gain_first)
    projected = jnp.stack([matmul(normal_in, full_first[z]) for z in range(col_count)])
    queries = (
        rotate(projected[:, :, :query_width].reshape(col_count, local, heads, HD), cosine, sinusoid)
        .astype(bf16)
        .reshape(col_count, local, pairs, group, HD)
    )
    keyvals = projected[:, :, query_width:].reshape(col_count, local, pairs, 2, HD)
    keyvals = jnp.stack(
        [rotate(keyvals[:, :, :, 0], cosine, sinusoid), keyvals[:, :, :, 1]], axis=3
    ).astype(bf16)
    chunks = [keyvals]
    for _ in range(back):
        chunks.insert(0, shift(chunks[0], 1, col_count))
    all_keyvals = jnp.concatenate(chunks, axis=1)
    key_rows, values = all_keyvals[:, :, :, 0], all_keyvals[:, :, :, 1]

    factor = HD ** (-0.5)
    scores = jnp.einsum("ztkgd,zskd->zkgts", queries, key_rows, preferred_element_type=f32) * factor
    scores = jnp.where(allowed, scores, blocked)
    summit = jnp.max(scores, axis=-1, keepdims=True)
    weights = jnp.exp(scores - summit)
    totals = jnp.sum(weights, axis=-1, keepdims=True)
    chances = weights / totals
    rounded = chances.astype(bf16)
    mixed = (
        jnp.einsum("zkgts,zskd->ztkgd", rounded, values, preferred_element_type=f32)
        .astype(bf16)
        .reshape(col_count, local, query_width)
    )
    attended = sum(against(mixed[z], full_output[z]) for z in range(col_count))
    hidden_in = inputs + attended
    normal_mid, scale_mid = normalize(hidden_in, gain_second)

    rows_mid = line_gather(normal_mid, row_count, col_count, 2)
    gate_up = matmul(rows_mid, full_hidden)
    gate_part = gate_up[:, :hidden]
    up_part = gate_up[:, hidden:]
    sigmoid_gate = jax.nn.sigmoid(gate_part)
    silu_gate = gate_part * sigmoid_gate
    gated_act = (silu_gate * up_part).astype(bf16)
    grad_gated = matmul(rows_grad, full_down)
    grad_gate = grad_gated * up_part * sigmoid_gate * (1.0 + gate_part * (1.0 - sigmoid_gate))
    grad_up = grad_gated * silu_gate
    grad_gate_up = jnp.concatenate([grad_gate, grad_up], axis=1).astype(bf16)
    grad_mid = line_sum(
        against(grad_gate_up, full_hidden).astype(bf16), row_count, col_count, 3
    )
    out_terms = against(gated_act, full_down).astype(bf16)
    grad_down_part = over_rows(rows_grad, gated_act).astype(bf16)
    grad_hidden_part = over_rows(rows_mid, grad_gate_up).astype(bf16)
    sum_hidden = lax.psum_scatter(grad_hidden_part, "row", scatter_dimension=0, tiled=True)
    sum_down = lax.psum_scatter(grad_down_part, "row", scatter_dimension=0, tiled=True)

    back_mid, gain_mid_part = norm_back(grad_mid, hidden_in, scale_mid, gain_second)
    grad_hidden_in = out_grad.astype(f32) + back_mid
    grad_low = grad_hidden_in.astype(bf16)
    grad_mixed = jnp.stack(
        [matmul(grad_low, full_output[z]).astype(bf16) for z in range(col_count)]
    ).reshape(col_count, local, pairs, group, HD)
    grad_output_part = jnp.stack(
        [over_rows(grad_low, mixed[z]).astype(bf16) for z in range(col_count)]
    )

    grad_chance = jnp.einsum("ztkgd,zskd->zkgts", grad_mixed, values, preferred_element_type=f32)
    centre = jnp.sum(chances * grad_chance, axis=-1, keepdims=True)
    grad_score = (chances * (grad_chance - centre)).astype(bf16)
    grad_query = (
        jnp.einsum("zkgts,zskd->ztkgd", grad_score, key_rows, preferred_element_type=f32) * factor
    )
    grad_key = (
        jnp.einsum("zkgts,ztkgd->zskd", grad_score, queries, preferred_element_type=f32) * factor
    )
    grad_value = jnp.einsum("zkgts,ztkgd->zskd", rounded, grad_mixed, preferred_element_type=f32)
    grad_keyval = jnp.stack([grad_key, grad_value], axis=3)
    carried = None
    for number in range(back + 1):
        part = grad_keyval[:, number * local : (number + 1) * local]
        if carried is not None:
            part = part + carried.astype(f32)
        if number < back:
            carried = shift(part.astype(bf16), -1, col_count)
    grad_query = rotate(
        grad_query.reshape(col_count, local, heads, HD), cosine, -sinusoid
    ).reshape(col_count, local, query_width)
    grad_keyval = jnp.stack(
        [rotate(part[:, :, :, 0], cosine, -sinusoid), part[:, :, :, 1]], axis=3
    ).reshape(col_count, local, pairs * 2 * HD)
    grad_first = jnp.concatenate([grad_query, grad_keyval], axis=2).astype(bf16)
    grad_first_part = jnp.stack(
        [over_rows(normal_in, grad_first[z]).astype(bf16) for z in range(col_count)]
    )
    sum_first, sum_output, out_sum = sum_all(
        [grad_first_part, grad_output_part], out_terms, row_count, col_count, f32
    )
    block_out = hidden_in + out_sum
    grad_in = sum(against(grad_first[z], full_first[z]) for z in range(col_count))
    back_in, gain_in_part = norm_back(grad_in, inputs, scale_in, gain_first)
    grad_tokens = (grad_hidden_in + back_in).astype(bf16)
    gain_in_sum, gain_mid_sum = lax.psum((gain_in_part, gain_mid_part), ("row", "col"))
    return (
        block_out.astype(bf16),
        grad_tokens,
        gain_in_sum,
        sum_first[:, :query_width],
        sum_first[:, query_width:].reshape(deep, pairs, 2 * HD),
        sum_output,
        gain_mid_sum,
        sum_hidden.astype(f32).reshape(deep, 2, hidden),
        sum_down.astype(f32),
    )


def solution(mesh):
    return jax.shard_map(
        shards,
        mesh=mesh,
        in_specs=(
            P(("row", "col"), None),
            P("row", None),
            P(),
            P("row", "col"),
            P("row", "col", None),
            P("row", "col"),
            P(),
            P("row", None, "col"),
            P("row", "col"),
            P(("row", "col"), None),
        ),
        out_specs=(
            P(("row", "col"), None),
            P(("row", "col"), None),
            P(),
            P("row", "col"),
            P("row", "col", None),
            P("row", "col"),
            P(),
            P("row", None, "col"),
            P("row", "col"),
        ),
        check_vma=False,
    )
```

time: 1400 us -> 927 us (0.66)
  waiting for transfers between devices: 973 us -> 20.2 us
  Pallas kernels: 0 us -> 513 us
  local copies, waits for them, and re-layouts: 64.2 us -> 27.8 us
    pallas_call x0 -> x4, Pallas kernels: none -> 513 us  [the longest x1 254 us: gather_all(): pl.pallas_call(functools.partial(gather_kernel, (row_count, col_count), c...]
    reduce_scatter x8 -> x2, waiting for transfers between devices: 458 us -> 0.01 us  [the longest x1 0.01 us: shards(): lax.psum_scatter(grad_down_part, 'row', scatter_dimension=0, tiled=True)]
    all_gather x9 -> x2, waiting for transfers between devices: 400 us -> 0.02 us  [the longest x1 0.02 us: shards(): lax.all_gather(hidden_weight.reshape(deep, 2 * hidden), 'row', axis=0, ti...]
    unnamed x19 -> x4, waiting for transfers between devices: 115 us -> 0.74 us
    convert_element_type x2 -> x4, local copies, waits for them, and re-layouts: 27.9 us -> 2.57 us  [shards(): matmul(grad_low, full_output[z]).astype(bf16)]
    unnamed x125 -> x117, local copies, waits for them, and re-layouts: 35.5 us -> 11.4 us
    ppermute x0 -> x4, waiting for transfers between devices: none -> 19.4 us  [shift(): return lax.ppermute(values, 'col', pairs)]
    another operation x5 -> x13, other arithmetic: 0.92 us -> 16.6 us  [the longest x1 5.86 us: shards(): jnp.stack([over_rows(normal_in, grad_first[z]).astype(bf16) for z in rang...]
  transfers between devices with their start and end apart: 18 -> 8, of which waited for: 17 -> 3; matrix products, arithmetic and copies ran while one was open for 21% -> 28% of each run, Pallas kernels for 0% -> 56%
where the time goes in v1:
time: 927 us; the launch traced here: 919 us
  Pallas kernels  513 us (55%)
  matrix products  232 us (25%)
  other arithmetic  52.6 us (6%)
  blocking collectives  46.9 us (5%)
  local copies, waits for them, and re-layouts  27.8 us (3%)
  waiting for transfers between devices  20.2 us (2%)
  between operations  15.1 us (2%)
  starting transfers between devices  11 us (1%)
    pallas_call x1, Pallas kernels, gather_all(): pl.pallas_call(functools.partial(gather_kernel, (row_count, col_count), c...  254 us
    pallas_call x1, Pallas kernels, sum_all(): pl.pallas_call(functools.partial(sum_kernel, (row_count, col_count), coun...  123 us
    pallas_call x1, Pallas kernels, line_gather(): pl.pallas_call(functools.partial(line_gather_kernel, (row_count, col_coun...  68.8 us
    pallas_call x1, Pallas kernels, line_sum(): pl.pallas_call(functools.partial(line_sum_kernel, (row_count, col_count))...  68.4 us
    dot_general x10, matrix products, matmul(): return jnp.dot(left, right, preferred_element_type=f32)  65.9 us
    dot_general x10, matrix products, against(): lax.dot_general(left, right, (((1,), (1,)), ((), ())), preferred_element_...  57.6 us
    psum x1, blocking collectives, shards(): lax.psum((gain_in_part, gain_mid_part), ('row', 'col'))  46.9 us
    dot_general x10, matrix products, over_rows(): lax.dot_general(left, right, (((0,), (0,)), ((), ())), preferred_element_...  46.7 us
  transfers between devices with their start and end apart: 8, of which 3 were waited for; matrix products, arithmetic and copies ran while one was open for 28% of the time, Pallas kernels for 56%

profile of v1, /device:TPU:0, one launch (start us, length us, event | category | flops | bytes accessed | tf_op | source)
XLA Modules:
  0.0 919.4 jit_solution(628877365724192127)
XLA Ops:
  7.2 3.9 copy.73
  13.6 253.6 %gather_weights.1 = (bf16[4,2048,768]{2,1,0:T(8,128)(2,1)}, bf16[4,2048,512]{2,1,0:T(8,128)(2,1)}, bf16[1024,2048]{1,0:T(8,128)(2,1)}) custom-call(bf16[256,768]{1,0:T(8,128)(2,1)} %pad_maximum_fusion.18.refs_0_, bf16[256,512]{1,0:T(8,128)(2,1)} %refs_1_.1, bf16[256,2048]{1,0:T(8,128)(2,1)} %refs_2_.1), custom_call_target="tpu_custom_call" | custom-call | bytes 20971520 | tf_op jit(solution)/shard_map/gather_weights/pallas_call | solution.py:356
  267.3 3.1 fusion.100
  270.3 3.9 fusion.97
  283.6 7.2 collective-permute-done
  290.8 5.4 collective-permute-start.1
  305.4 14.2 %fusion.159 = (f32[4,2,4,256]{3,2,1,0:T(4,128)S(1)}, f32[4,2,4,256,768]{3,4,2,1,0:T(8,128)}) fusion(pred[256,768]{0,1:T(8,128)(4,1)} %fusion.121, bf16[4,768,2,2,64]{1,4,2,0,3:T(8,128)(2,1)S(1)} %maximum_maximum_fusion, bf16[4,256,2,4,32]{1,4,3,2,0:T(8,128)(2,1)} %bitcast.266, bf16[4,256,2,4,32]{1,4,3,2,0:T(8,128)(2,1)S(1)} %bitcast.264), kind=kOutput, calls=%fused_computation.212 | convolution fusion | flops 832570112 | bytes 27230208 | tf_op jit(solution)/shard_map/sub | solution.py:945
  319.6 10.7 %fusion.88 = bf16[4,256,2,4,64]{1,4,3,2,0:T(8,128)(2,1)} fusion(bf16[4,768,2,2,64]{1,4,2,0,3:T(8,128)(2,1)S(1)} %maximum_maximum_fusion, f32[4,2,4,256,768]{3,4,2,1,0:T(8,128)} %get-tuple-element.54, f32[4,2,4,256]{3,2,1,0:T(4,128)S(1)} %get-tuple-element.53), kind=kOutput, calls=%fused_computation.131 | convolution fusion | flops 818413568 | bytes 27033600 | tf_op jit(solution)/shard_map/zkgts,zskd->ztkgd/dot_general | solution.py:950
  338.4 68.8 %gather_line.1 = bf16[1024,2048]{1,0:T(8,128)(2,1)} custom-call(bf16[256,2048]{1,0:T(8,128)(2,1)} %multiply_convert_fusion.3.own), custom_call_target="tpu_custom_call" | custom-call | bytes 4194304 | tf_op jit(solution)/shard_map/gather_line/pallas_call | solution.py:395
  407.3 23.8 %fusion.160 = f32[1024,4096]{1,0:T(8,128)} fusion(bf16[1024,2048]{1,0:T(8,128)(2,1)} %gather_line.1, bf16[2048,4096]{1,0:T(8,128)(2,1)} %all-gather.5.cloned.1.call-done), kind=kOutput, calls=%fused_computation.213 | convolution fusion | flops 17179869184 | bytes 37748736 | tf_op jit(solution)/shard_map/dot_general | solution.py:856
  431.1 21.8 %multiply_convert_fusion.2 = (bf16[1024,2048]{1,0:T(8,128)(2,1)}, bf16[1024,2048]{1,0:T(8,128)(2,1)}, bf16[1024,2048]{1,0:T(8,128)(2,1)}) fusion(f32[1024,4096]{1,0:T(8,128)} %fusion.160, bf16[1024,2048]{1,0:T(8,128)(2,1)} %get-tuple-element.17, bf16[2048,2048]{1,0:T(8,128)(2,1)} %all-gather.3.cloned.1.call-done), kind=kOutput, calls=%fused_computation.19 | convolution fusion | flops 8621391872 | bytes 41943040 | tf_op jit(solution)/shard_map/dot_general | solution.py:856
  452.8 13.5 %convolution_convert_fusion.1 = bf16[2048,2048]{1,0:T(8,128)(2,1)} fusion(bf16[1024,2048]{1,0:T(8,128)(2,1)S(1)} %copy-done.51, bf16[1024,2048]{1,0:T(8,128)(2,1)} %get-tuple-element.33), kind=kOutput, calls=%fused_computation.22 | convolution fusion | flops 8594128896 | bytes 16777216 | tf_op jit(solution)/shard_map/dot_general | solution.py:852
  466.4 25.5 %convolution_convert_fusion = bf16[2048,4096]{1,0:T(8,128)(2,1)} fusion(bf16[1024,2048]{1,0:T(8,128)(2,1)} %gather_line.1, bf16[1024,2048]{1,0:T(8,128)(2,1)} %get-tuple-element.32, bf16[1024,2048]{1,0:T(8,128)(2,1)} %get-tuple-element.31), kind=kOutput, calls=%fused_computation.9 | convolution fusion | flops 17205035008 | bytes 29360128 | tf_op jit(solution)/shard_map/dot_general | solution.py:852
  492.0 23.9 %fusion.14.terms = bf16[1024,2048]{1,0:T(8,128)(2,1)} fusion(bf16[2048,4096]{1,0:T(8,128)(2,1)} %all-gather.5.cloned.1.call-done, bf16[1024,2048]{1,0:T(8,128)(2,1)} %get-tuple-element.32, bf16[1024,2048]{1,0:T(8,128)(2,1)} %get-tuple-element.31), kind=kOutput, calls=%fused_computation.34 | convolution fusion | flops 17198743552 | bytes 29360128 | tf_op jit(solution)/shard_map/dot_general | solution.py:848
  515.9 68.4 %sum_line.1 = f32[256,2048]{1,0:T(8,128)S(1)} custom-call(bf16[1024,2048]{1,0:T(8,128)(2,1)} %fusion.14.terms), custom_call_target="tpu_custom_call" | custom-call | flops 2097152 | bytes 4194304 | tf_op jit(solution)/shard_map/sum_line/pallas_call | solution.py:516
  592.8 3.1 fusion.103
  597.2 3.2 fusion.106
  601.5 17.8 %fusion.1 = (f32[4,2,4,256]{3,2,1,0:T(4,128)S(1)}, f32[4,2,768,256,4]{3,2,4,1,0:T(8,128)}) fusion(f32[4,2,4,256,768]{3,4,2,1,0:T(8,128)} %get-tuple-element.54, f32[4,2,4,256]{3,2,1,0:T(4,128)S(1)} %copy-done.46, bf16[1,256,2,4,64]{1,4,3,2,0:T(8,128)(2,1)S(1)} %bitcast.269, bf16[1,256,2,4,64]{1,4,3,2,0:T(8,128)(2,1)S(1)} %bitcast.271, ...), kind=kOutput, calls=%fused_computation.3 | convolution fusion | flops 828366848 | bytes 52232192 | tf_op jit(solution)/shard_map/ztkgd,zskd->zkgts/dot_general | solution.py:988
  619.4 17.3 %fusion.3 = bf16[4,2,4,256,768]{3,4,2,1,0:T(8,128)(2,1)S(1)} fusion(f32[4,2,768,256,4]{3,2,4,1,0:T(8,128)} %get-tuple-element.58, f32[4,2,4,256]{3,2,1,0:T(4,128)S(1)} %get-tuple-element.57, f32[4,2,4,256,768]{3,4,2,1,0:T(8,128)} %get-tuple-element.54, f32[4,2,4,256]{3,2,1,0:T(4,128)S(1)} %copy-done.46), kind=kLoop, calls=%fused_computation.5 | loop fusion | flops 25165824 | bytes 62980096 | tf_op jit(solution)/shard_map/convert_element_type | solution.py:990
  636.7 4.7 copy-done
  641.4 6.3 fusion.81
  647.6 10.9 %fusion.82 = f32[4,768,2,1,64]{1,4,2,0,3:T(8,128)S(1)} fusion(bf16[1,256,2,4,64]{1,4,3,2,0:T(8,128)(2,1)S(1)} %bitcast.270, bf16[1,256,2,4,64]{1,4,3,2,0:T(8,128)(2,1)} %bitcast.272, bf16[1,256,2,4,64]{1,4,3,2,0:T(8,128)(2,1)} %bitcast.276, bf16[1,256,2,4,64]{1,4,3,2,0:T(8,128)(2,1)} %bitcast.274, f32[4,2,4,256,768]{3,4,2,1,0:T(8,128)} %get-tuple-element.54, ...), kind=kOutput, calls=%fused_computation.129 | convolution fusion | flops 819462144 | bytes 27820032 | tf_op jit(solution)/shard_map/zkgts,ztkgd->zskd/dot_general | solution.py:997
  664.5 14.2 %convolution_convert_fusion.2.refs_2_ = bf16[1024,2048]{1,0:T(8,128)(2,1)} fusion(bf16[1024,2048]{1,0:T(8,128)(2,1)} %get-tuple-element.33, bf16[2048,2048]{1,0:T(8,128)(2,1)} %all-gather.3.cloned.1.call-done), kind=kOutput, calls=%fused_computation.35 | convolution fusion | flops 8592031744 | bytes 16777216 | tf_op jit(solution)/shard_map/dot_general | solution.py:848
  678.7 3.9 pad_maximum_fusion.2.refs_1_
  688.3 10.1 %collective-permute-done.3 = bf16[4,256,2,2,64]{1,4,2,0,3:T(8,128)(2,1)S(1)} collective-permute-done((bf16[4,256,2,2,64]{1,4,2,0,3:T(8,128)(2,1)S(1)}, bf16[4,256,2,2,64]{1,4,2,0,3:T(8,128)(2,1)S(1)}, u32[]{:S(2)}, u32[]{:S(2)}) %collective-permute-start.3) | collective-permute-done | bytes 524320 | tf_op jit(solution)/shard_map/ppermute | solution.py:864
  704.4 5.9 pad_maximum_fusion.refs_0_
  710.3 122.7 %sum_weights.1 = (f32[256,768]{1,0:T(8,128)}, f32[256,512]{1,0:T(8,128)}, f32[256,2048]{1,0:T(8,128)}) custom-call(bf16[4,4,2,256,768]{4,3,2,1,0:T(8,128)(2,1)} %pad_maximum_fusion.refs_0_, bf16[4,4,2,256,512]{4,3,2,1,0:T(8,128)(2,1)} %pad_maximum_fusion.2.refs_1_, bf16[1024,2048]{1,0:T(8,128)(2,1)} %convolution_convert_fusion.2.refs_2_), custom_call_target="tpu_custom_call" | custom-call | bytes 41943040 | tf_op jit(solution)/shard_map/sum_weights/pallas_call | solution.py:789
  839.6 3.0 fusion.41
  842.5 3.0 fusion.44
  845.5 5.4 fusion.59
  850.9 46.9 %all-reduce.1 = (f32[2048]{0:T(1024)}, f32[2048]{0:T(1024)}) all-reduce(f32[2048]{0:T(1024)} %get-tuple-element.23, f32[2048]{0:T(1024)} %get-tuple-element.21), channel_id=1, replica_groups=mesh['row'=8,'col'=4] {'row','col'}, use_global_device_ids=true, to_apply=%region_11.12 | all-reduce | flops 4096 | bytes 32768 | tf_op jit(solution)/shard_map/psum | solution.py:1023
  905.2 6.6 reshape.271
  (205 shorter events, 71.9 us)
Async XLA Ops:
  7.2 400.1 %all-gather.5.cloned.1.call-start = ((), (), s32[]{:S(2)}) async-start(), calls=%async_computation.3 | async-start | bytes 18874368 | tf_op jit(solution)/shard_map/all_gather | solution.py:911
  11.2 419.9 %all-gather.3.cloned.1.call-start = ((), (), s32[]{:S(2)}) async-start(), calls=%async_computation.2 | async-start | bytes 9437184 | tf_op jit(solution)/shard_map/all_gather | solution.py:914
  11.9 890.5 %reduce-scatter.5.cloned.1.call-start = ((), (), s32[]{:S(2)}) async-start(), calls=%async_computation.5 | async-start | bytes 9437184 | tf_op jit(solution)/shard_map/reduce_scatter | solution.py:976
  12.8 262.5 %copy-start.43 = (f32[256]{0:T(256)}, f32[256]{0:T(256)S(1)}, u32[]{:S(2)}) copy-start(f32[256]{0:T(256)S(1)} %get-tuple-element.50) | copy-start | bytes 3076
  12.8 262.5 %copy-start.35 = (f32[2048]{0:T(1024)}, f32[2048]{0:T(1024)S(1)}, u32[]{:S(2)}) copy-start(f32[2048]{0:T(1024)S(1)} %convert_element_type.116) | copy-start | bytes 24580
  278.8 20.2 %copy-start.32 = (f32[256,32]{0,1:T(8,128)}, f32[256,32]{0,1:T(8,128)S(1)}, u32[]{:S(2)}) copy-start(f32[256,32]{0,1:T(8,128)S(1)} %get-tuple-element.48) | copy-start | bytes 98308
  279.0 17.3 %copy-start.49 = (bf16[2048]{0:T(1024)(128)(2,1)S(1)}, bf16[2048]{0:T(1024)(128)(2,1)}, u32[]{:S(2)}) copy-start(bf16[2048]{0:T(1024)(128)(2,1)} %param.16) | copy-start | bytes 12292
  279.8 10.9 %collective-permute-start = (bf16[4,256,2,2,64]{1,4,2,0,3:T(8,128)(2,1)}, bf16[4,256,2,2,64]{1,4,2,0,3:T(8,128)(2,1)}, u32[]{:S(2)}, u32[]{:S(2)}) collective-permute-start(bf16[4,256,2,2,64]{1,4,2,0,3:T(8,128)(2,1)} %pad_maximum_fusion.15), channel_id=1, source_target_pairs={{0,1},{1,2},{2,3},{4,5},{5,6},{6,7},{8,9},{9,10},{10,11},{12,13},{... | collective-permute-start | bytes 1572872 | tf_op jit(solution)/shard_map/ppermute | solution.py:864
  290.8 13.1 %collective-permute-start.1 = (bf16[4,256,2,2,64]{1,4,2,0,3:T(8,128)(2,1)}, bf16[4,256,2,2,64]{1,4,2,0,3:T(8,128)(2,1)}, u32[]{:S(2)}, u32[]{:S(2)}) collective-permute-start(bf16[4,256,2,2,64]{1,4,2,0,3:T(8,128)(2,1)} %collective-permute-done), channel_id=1, source_target_pairs={{0,1},{1,2},{2,3},{4,5},{5,6},{6,7},{8,9},{9,10},{10,11},{12,13},{... | collective-permute-start | bytes 1572872 | tf_op jit(solution)/shard_map/ppermute | solution.py:864
  301.8 17.8 %copy-start.31 = (bf16[4,256,8,32]{1,3,2,0:T(8,128)(2,1)}, bf16[4,256,8,32]{1,3,2,0:T(8,128)(2,1)S(1)}, u32[]{:S(2)}) copy-start(bf16[4,256,8,32]{1,3,2,0:T(8,128)(2,1)S(1)} %get-tuple-element.36) | copy-start | bytes 1572868
  305.4 14.2 %copy-start.15 = (bf16[4,768,2,2,64]{1,4,2,0,3:T(8,128)(2,1)}, bf16[4,768,2,2,64]{1,4,2,0,3:T(8,128)(2,1)S(1)}, u32[]{:S(2)}) copy-start(bf16[4,768,2,2,64]{1,4,2,0,3:T(8,128)(2,1)S(1)} %maximum_maximum_fusion) | copy-start | bytes 4718596
  319.6 10.7 %copy-start.45 = (f32[4,2,4,256]{3,2,1,0:T(4,128)}, f32[4,2,4,256]{3,2,1,0:T(4,128)S(1)}, u32[]{:S(2)}) copy-start(f32[4,2,4,256]{3,2,1,0:T(4,128)S(1)} %get-tuple-element.53) | copy-start | bytes 98308
  319.6 14.8 %slice-start.3 = ((s8[8388608]{0:T(1024)(128)(4,1)}), s8[4194304]{0:T(1024)(128)(4,1)S(1)}, s32[]{:S(2)}) async-start(s8[8388608]{0:T(1024)(128)(4,1)} %bitcast.243), calls=%async_computation.9 | async-start | bytes 8388608
  319.6 14.8 %slice-start.4 = ((s8[8388608]{0:T(1024)(128)(4,1)}), s8[4194304]{0:T(1024)(128)(4,1)S(1)}, s32[]{:S(2)}) async-start(s8[8388608]{0:T(1024)(128)(4,1)} %bitcast.243), calls=%async_computation.10 | async-start | bytes 8388608
  337.0 248.6 %copy-start.1 = (f32[256,2048]{1,0:T(8,128)}, f32[256,2048]{1,0:T(8,128)S(1)}, u32[]{:S(2)}) copy-start(f32[256,2048]{1,0:T(8,128)S(1)} %get-tuple-element.56) | copy-start | bytes 6291460
  431.1 21.8 %copy-start.51 = (bf16[1024,2048]{1,0:T(8,128)(2,1)S(1)}, bf16[1024,2048]{1,0:T(8,128)(2,1)}, u32[]{:S(2)}) copy-start(bf16[1024,2048]{1,0:T(8,128)(2,1)} %get-tuple-element.17) | copy-start | bytes 12582916
  466.4 438.8 %reduce-scatter.3.cloned.1.call-start = ((), (), s32[]{:S(2)}) async-start(), calls=%async_computation.4 | async-start | bytes 18874368 | tf_op jit(solution)/shard_map/reduce_scatter | solution.py:975
  587.6 9.6 %copy-start.5 = (bf16[256,2048]{1,0:T(8,128)(2,1)}, bf16[256,2048]{1,0:T(8,128)(2,1)S(1)}, u32[]{:S(2)}) copy-start(bf16[256,2048]{1,0:T(8,128)(2,1)S(1)} %get-tuple-element.29) | copy-start | bytes 3145732
  592.8 8.7 copy-start.39
  597.1 22.2 %copy-start.40 = (bf16[256,512]{0,1:T(8,128)(2,1)}, bf16[256,512]{0,1:T(8,128)(2,1)S(1)}, u32[]{:S(2)}) copy-start(bf16[256,512]{0,1:T(8,128)(2,1)S(1)} %copy.54) | copy-start | bytes 786436
  601.5 17.8 %copy-start.41 = (bf16[256,512]{0,1:T(8,128)(2,1)}, bf16[256,512]{0,1:T(8,128)(2,1)S(1)}, u32[]{:S(2)}) copy-start(bf16[256,512]{0,1:T(8,128)(2,1)S(1)} %copy.55) | copy-start | bytes 786436
  647.6 10.9 %copy-start.7 = (f32[4,768,2,1,64]{1,4,2,0,3:T(8,128)S(1)}, f32[4,768,2,1,64]{1,4,2,0,3:T(8,128)}, u32[]{:S(2)}) copy-start(f32[4,768,2,1,64]{1,4,2,0,3:T(8,128)} %fusion.81) | copy-start | bytes 4718596
  658.5 24.0 %copy-start.9 = (f32[4,768,2,1,64]{1,4,2,0,3:T(8,128)}, f32[4,768,2,1,64]{1,4,2,0,3:T(8,128)S(1)}, u32[]{:S(2)}) copy-start(f32[4,768,2,1,64]{1,4,2,0,3:T(8,128)S(1)} %fusion.82) | copy-start | bytes 4718596
  659.5 23.1 %collective-permute-start.2 = (bf16[4,256,2,2,64]{1,4,2,0,3:T(8,128)(2,1)}, bf16[4,256,2,2,64]{1,4,2,0,3:T(8,128)(2,1)}, u32[]{:S(2)}, u32[]{:S(2)}) collective-permute-start(bf16[4,256,2,2,64]{1,4,2,0,3:T(8,128)(2,1)} %fusion.120), channel_id=1, source_target_pairs={{1,0},{2,1},{3,2},{5,4},{6,5},{7,6},{9,8},{10,9},{11,10},{13,12},{... | collective-permute-start | bytes 1572872 | tf_op jit(solution)/shard_map/ppermute | solution.py:864
  663.6 21.8 %slice-start = ((s8[12582912]{0:T(1024)(128)(4,1)}), s8[4194304]{0:T(1024)(128)(4,1)S(1)}, s32[]{:S(2)}) async-start(s8[12582912]{0:T(1024)(128)(4,1)} %bitcast.223), calls=%async_computation.6 | async-start | bytes 8388608
  664.4 21.1 %slice-start.1 = ((s8[12582912]{0:T(1024)(128)(4,1)}), s8[4194304]{0:T(1024)(128)(4,1)S(1)}, s32[]{:S(2)}) async-start(s8[12582912]{0:T(1024)(128)(4,1)} %bitcast.223), calls=%async_computation.7 | async-start | bytes 8388608
  664.4 21.1 %slice-start.2 = ((s8[12582912]{0:T(1024)(128)(4,1)}), s8[4194304]{0:T(1024)(128)(4,1)S(1)}, s32[]{:S(2)}) async-start(s8[12582912]{0:T(1024)(128)(4,1)} %bitcast.223), calls=%async_computation.8 | async-start | bytes 8388608
  683.9 14.5 %collective-permute-start.3 = (bf16[4,256,2,2,64]{1,4,2,0,3:T(8,128)(2,1)S(1)}, bf16[4,256,2,2,64]{1,4,2,0,3:T(8,128)(2,1)S(1)}, u32[]{:S(2)}, u32[]{:S(2)}) collective-permute-start(bf16[4,256,2,2,64]{1,4,2,0,3:T(8,128)(2,1)S(1)} %fusion.117), channel_id=1, source_target_pairs={{1,0},{2,1},{3,2},{5,4},{6,5},{7,6},{9,8},{10,9},{11,10},{13,12},{... | collective-permute-start | bytes 1572872 | tf_op jit(solution)/shard_map/ppermute | solution.py:864
  687.8 10.6 %copy-start.8 = (f32[4,768,2,1,64]{1,4,2,0,3:T(8,128)S(1)}, f32[4,768,2,1,64]{1,4,2,0,3:T(8,128)}, u32[]{:S(2)}) copy-start(f32[4,768,2,1,64]{1,4,2,0,3:T(8,128)} %fusion.81) | copy-start | bytes 4718596
  687.8 10.6 %copy-start.10 = (f32[4,768,2,1,64]{1,4,2,0,3:T(8,128)S(1)}, f32[4,768,2,1,64]{1,4,2,0,3:T(8,128)}, u32[]{:S(2)}) copy-start(f32[4,768,2,1,64]{1,4,2,0,3:T(8,128)} %copy-done.9) | copy-start | bytes 4718596
  845.5 52.3 %copy-start.2 = (f32[256,2048]{1,0:T(8,128)S(1)}, f32[256,2048]{1,0:T(8,128)}, u32[]{:S(2)}) copy-start(f32[256,2048]{1,0:T(8,128)} %copy-done.1) | copy-start | bytes 6291460
  850.9 49.9 %copy-start.47 = (f32[256]{0:T(256)S(1)}, f32[256]{0:T(256)}, u32[]{:S(2)}) copy-start(f32[256]{0:T(256)} %get-tuple-element.49) | copy-start | bytes 3076
  (33 other events, 105.3 us)
Sparse Core Ops, SparseCore 0:
  11.3 119.6 all-gather.4
  132.8 80.7 all-gather.2
  466.5 71.2 reduce-scatter.4
  541.7 115.9 reduce-scatter.2

commit v2 on v1

--- a/solution.py
+++ b/solution.py
@@ -253,15 +253,12 @@
 def gather_kernel(sizes, count, *refs):
     row_count, col_count = sizes
     own = refs[:count]
-    own_act = refs[count]
-    full = refs[count + 1 : 2 * count + 1]
-    full_act = refs[2 * count + 1]
-    local_sems, zs, zr, ps, pr = refs[2 * count + 2 :]
+    full = refs[count : 2 * count]
+    local_sems, zs, zr, ps, pr = refs[2 * count :]
     place = Place(row_count, col_count)
     place.greet(True, True)
     deep = own[0].shape[0]
     half_deep = deep // 2
-    token_rows = own_act.shape[0]
 
     lines = [
         LineGather(
@@ -273,28 +270,17 @@
         )
         for n in range(count)
     ]
-    acts = LineGather(
-        place,
-        own_act,
-        lambda j: full_act.at[pl.ds(j * token_rows, token_rows)],
-        zs.at[count],
-        zr.at[count],
-    )
-
     def keep(n):
-        target = (
-            full[n].at[place.col, pl.ds(place.row * deep, deep)]
-            if n < count
-            else full_act.at[pl.ds(place.col * token_rows, token_rows)]
+        return pltpu.make_async_copy(
+            own[n], full[n].at[place.col, pl.ds(place.row * deep, deep)], local_sems.at[n]
         )
-        return pltpu.make_async_copy(own[n] if n < count else own_act, target, local_sems.at[n])
-
-    for n in range(count + 1):
+
+    for n in range(count):
         keep(n).start()
-    for line in lines + [acts]:
+    for line in lines:
         for way in (0, 1):
             line.send(way, 1)
-    for n in range(count + 1):
+    for n in range(count):
         keep(n).wait()
 
     def inside(n, col):
@@ -331,22 +317,15 @@
             condition, col = at_entry(entries[number - 2])
             m = entries[number - 2][2]
             when(condition, lambda: inside(m, col).third())
-        if number < len(entries):
-            way, step, n = entries[number]
-            if step > 1 and way == 1 and n == count - 1:
-                for other in (0, 1):
-                    acts.receive(other, step - 1)
-    for other in (0, 1):
-        acts.receive(other, col_count - 1)
     for entry in entries:
         condition, col = at_entry(entry)
         m = entry[2]
         when(condition, lambda: inside(m, col).finish())
-    for line in lines + [acts]:
+    for line in lines:
         line.finish()
 
 
-def gather_all(weights, act, row_count, col_count):
+def gather_all(weights, row_count, col_count):
     count = len(weights)
     sizes = plane_sizes(row_count)
     deep = weights[0].shape[0]
@@ -357,21 +336,20 @@
         functools.partial(gather_kernel, (row_count, col_count), count),
         out_shape=[
             jax.ShapeDtypeStruct((col_count, row_count * deep, w.shape[1]), bf16) for w in weights
-        ]
-        + [jax.ShapeDtypeStruct((col_count * act.shape[0], act.shape[1]), bf16)],
-        in_specs=[ANY] * (count + 1),
-        out_specs=[ANY] * (count + 1),
+        ],
+        in_specs=[ANY] * count,
+        out_specs=[ANY] * count,
         scratch_shapes=[
-            pltpu.SemaphoreType.DMA((count + 1,)),
-            pltpu.SemaphoreType.DMA((count + 1, 2, steps)),
-            pltpu.SemaphoreType.DMA((count + 1, 2, steps)),
+            pltpu.SemaphoreType.DMA((count,)),
+            pltpu.SemaphoreType.DMA((count, 2, steps)),
+            pltpu.SemaphoreType.DMA((count, 2, steps)),
             pltpu.SemaphoreType.DMA(plane_sems),
             pltpu.SemaphoreType.DMA(plane_sems),
         ],
         compiler_params=pltpu.CompilerParams(collective_id=0, has_side_effects=True),
         cost_estimate=pl.CostEstimate(flops=0, bytes_accessed=moved, transcendentals=0),
         name="gather_weights",
-    )(*weights, act)
+    )(*weights)
 
 
 def line_gather_kernel(sizes, own, full, local_sem, sends, recvs):
@@ -626,15 +604,94 @@
                 self.copy(half, 0, step, 0).wait_send()
 
 
+class SmallSum:
+    def __init__(self, place, own, total, ring_held, line_held, ring_sems, line_sems):
+        self.place, self.own, self.total = place, own, total
+        self.held, self.sems = ring_held, ring_sems
+        self.line = LineGather(
+            place, total, lambda j: line_held.at[j], line_sems.at[0], line_sems.at[1]
+        )
+        self.line_held = line_held
+        self.stages = []
+        for axis in range(3):
+            for step in range(1, place.sizes[axis]):
+                self.stages.append(functools.partial(self.ring_send, axis, step))
+                self.stages.append(functools.partial(self.ring_receive, axis, step))
+            if place.sizes[axis] > 1:
+                self.stages.append(functools.partial(self.ring_add, axis))
+        self.stages.append(self.line_start)
+        for step in range(1, place.cols):
+            self.stages.append(functools.partial(self.line_step, step))
+        self.stages.append(self.line_add)
+
+    def begin(self):
+        self.total[...] = self.own[...]
+
+    def block(self, axis, step):
+        at = self.place.moved(axis, -step)[axis]
+        return self.held.at[axis, at]
+
+    def ring_copy(self, axis, step):
+        source = self.total if step == 1 else self.block(axis, step - 1)
+        target = self.held.at[axis, self.place.moved(axis, 1 - step)[axis]]
+        return remote(
+            source,
+            target,
+            self.sems.at[0, axis, step - 1],
+            self.sems.at[1, axis, step - 1],
+            self.place.device(axis, 1),
+        )
+
+    def ring_send(self, axis, step):
+        self.ring_copy(axis, step).start()
+
+    def ring_receive(self, axis, step):
+        ref = self.block(axis, step)
+        remote(
+            ref,
+            ref,
+            self.sems.at[0, axis, step - 1],
+            self.sems.at[1, axis, step - 1],
+            self.place.device(axis, 1),
+        ).wait_recv()
+
+    def ring_add(self, axis):
+        for step in range(1, self.place.sizes[axis]):
+            self.ring_copy(axis, step).wait_send()
+        own_at = self.place.at[axis]
+        total = None
+        for at in range(self.place.sizes[axis]):
+            term = jnp.where(own_at == at, self.total[...], self.held[axis, at])
+            total = term if total is None else total + term
+        self.total[...] = total
+
+    def line_start(self):
+        for way in (0, 1):
+            self.line.send(way, 1)
+
+    def line_step(self, step):
+        for way in (0, 1):
+            self.line.receive(way, step)
+
+    def line_add(self):
+        self.line.finish()
+        total = None
+        for at in range(self.place.cols):
+            term = jnp.where(self.place.col == at, self.total[...], self.line_held[at])
+            total = term if total is None else total + term
+        self.total[...] = total
+
+
 def sum_kernel(sizes, count, *refs):
     row_count, col_count = sizes
     terms = refs[:count]
-    act_terms = refs[count]
-    outs = refs[count + 1 : 2 * count + 1]
-    act_out = refs[2 * count + 1]
-    refs = refs[2 * count + 2 :]
+    act_terms, small = refs[count : count + 2]
+    outs = refs[count + 2 : 2 * count + 2]
+    act_out, small_out = refs[2 * count + 2 : 2 * count + 4]
+    refs = refs[2 * count + 4 :]
     per = [refs[6 * n : 6 * n + 6] for n in range(count)]
-    act_held, load_sems, cs, cr, ps, pr, zs, zr = refs[6 * count :]
+    act_held, load_sems, cs, cr, ps, pr, zs, zr = refs[6 * count : 6 * count + 8]
+    ring_held, line_held, ring_sems, line_sems = refs[6 * count + 8 :]
     place = Place(row_count, col_count)
     cores = place.sizes[2]
     core = place.at[2]
@@ -705,6 +762,9 @@
     for way in (0, 1):
         if col_count > 1:
             acts.step(way, col_count - 1)
+    smalls = SmallSum(place, small, small_out, ring_held, line_held, ring_sems, line_sems)
+    smalls.begin()
+    stages = list(smalls.stages)
 
     def start(n, col):
         load(n, col).wait()
@@ -737,6 +797,10 @@
             if 1 < step and way == 1 and n == count - 1:
                 for other in (0, 1):
                     acts.step(other, step - 1)
+        if stages:
+            stages.pop(0)()
+    for stage in stages:
+        stage()
     acts.last(act_out)
     for n in range(count):
         pltpu.make_async_copy(per[n][5], outs[n], load_sems.at[n, place.col]).wait()
@@ -754,7 +818,7 @@
         line.finish()
 
 
-def sum_all(terms, act_terms, row_count, col_count, act_type):
+def sum_all(terms, act_terms, small, row_count, col_count, act_type):
     count = len(terms)
     sizes = plane_sizes(row_count)
     na, nb, nk = sizes
@@ -784,14 +848,21 @@
         pltpu.SemaphoreType.DMA(plane_sems),
         pltpu.SemaphoreType.DMA((count + 1, 2, steps)),
         pltpu.SemaphoreType.DMA((count + 1, 2, steps)),
+        pltpu.VMEM((3, max(sizes)) + small.shape, f32),
+        pltpu.VMEM((col_count,) + small.shape, f32),
+        pltpu.SemaphoreType.DMA((2, 3, max(max(sizes) - 1, 1))),
+        pltpu.SemaphoreType.DMA((2, 2, steps)),
     ]
     vmem = pl.BlockSpec(memory_space=pltpu.VMEM)
     return pl.pallas_call(
         functools.partial(sum_kernel, (row_count, col_count), count),
         out_shape=[jax.ShapeDtypeStruct((deep, width), f32) for width in widths]
-        + [jax.ShapeDtypeStruct((token_rows, act_terms.shape[1]), act_type)],
-        in_specs=[ANY] * count + [vmem],
-        out_specs=[ANY] * count + [vmem],
+        + [
+            jax.ShapeDtypeStruct((token_rows, act_terms.shape[1]), act_type),
+            jax.ShapeDtypeStruct(small.shape, f32),
+        ],
+        in_specs=[ANY] * count + [vmem, vmem],
+        out_specs=[ANY] * count + [vmem, vmem],
         scratch_shapes=scratch,
         compiler_params=pltpu.CompilerParams(
             collective_id=1, has_side_effects=True, vmem_limit_bytes=60 << 20
@@ -803,6 +874,7 @@
     )(
         *[t.reshape(col_count, chips, nk, deep, t.shape[2]) for t in terms],
         act_terms,
+        small,
     )
 
 
@@ -908,17 +980,18 @@
     gain_first = attn_gain.astype(f32)
     gain_second = mlp_gain.astype(f32)
 
-    full_hidden = lax.all_gather(
-        hidden_weight.reshape(deep, 2 * hidden), "row", axis=0, tiled=True
-    )
-    full_down = lax.all_gather(down_weight, "row", axis=0, tiled=True)
+    rows_grad = lax.all_gather(out_grad, "col", axis=0, tiled=True)
 
     first_weight = jnp.concatenate(
         [query_weight, keyvalue_weight.reshape(deep, pairs * 2 * HD)], axis=1
     )
-    full_first, full_output, rows_grad = gather_all(
-        [first_weight, output_weight], out_grad, row_count, col_count
-    )
+    full_first, full_output = gather_all([first_weight, output_weight], row_count, col_count)
+
+    hidden_flat, down_flat, full_first = lax.optimization_barrier(
+        (hidden_weight.reshape(deep, 2 * hidden), down_weight, full_first)
+    )
+    full_hidden = lax.all_gather(hidden_flat, "row", axis=0, tiled=True)
+    full_down = lax.all_gather(down_flat, "row", axis=0, tiled=True)
 
     inputs = tokens.astype(f32)
     normal_in, scale_in = normalize(inputs, gain_first)
@@ -1013,14 +1086,15 @@
     grad_first_part = jnp.stack(
         [over_rows(normal_in, grad_first[z]).astype(bf16) for z in range(col_count)]
     )
-    sum_first, sum_output, out_sum = sum_all(
-        [grad_first_part, grad_output_part], out_terms, row_count, col_count, f32
-    )
-    block_out = hidden_in + out_sum
     grad_in = sum(against(grad_first[z], full_first[z]) for z in range(col_count))
     back_in, gain_in_part = norm_back(grad_in, inputs, scale_in, gain_first)
     grad_tokens = (grad_hidden_in + back_in).astype(bf16)
-    gain_in_sum, gain_mid_sum = lax.psum((gain_in_part, gain_mid_part), ("row", "col"))
+    gain_parts = jnp.concatenate([gain_in_part, gain_mid_part]).reshape(-1, 128)
+    sum_first, sum_output, out_sum, gain_sums = sum_all(
+        [grad_first_part, grad_output_part], out_terms, gain_parts, row_count, col_count, f32
+    )
+    block_out = hidden_in + out_sum
+    gain_in_sum, gain_mid_sum = gain_sums.reshape(2, width)
     return (
         block_out.astype(bf16),
         grad_tokens,

time: 927 us -> 870 us (0.939)
  blocking collectives: 46.9 us -> 0 us
  Pallas kernels: 513 us -> 476 us
  waiting for transfers between devices: 20.2 us -> 36.1 us
    pallas_call x1, Pallas kernels: 254 us -> 128 us  [gather_all(): pl.pallas_call(functools.partial(gather_kernel, (row_count, col_count), c...]
    pallas_call x1, Pallas kernels: 68.8 us -> 138 us  [line_gather(): pl.pallas_call(functools.partial(line_gather_kernel, (row_count, col_coun...]
    psum x1 -> x0, blocking collectives: 46.9 us -> none  [shards(): lax.psum((gain_in_part, gain_mid_part), ('row', 'col'))]
    pallas_call x1, Pallas kernels: 123 us -> 133 us  [sum_all(): pl.pallas_call(functools.partial(sum_kernel, (row_count, col_count), coun...]
  transfers between devices with their start and end apart: 8 -> 9, of which waited for: 3 -> 4; matrix products, arithmetic and copies ran while one was open for 28% -> 30% of each run, Pallas kernels for 56% -> 41%
where the time goes in v2:
time: 870 us; the launch traced here: 855 us
  Pallas kernels  476 us (55%)
  matrix products  229 us (26%)
  other arithmetic  53.7 us (6%)
  waiting for transfers between devices  36.1 us (4%)
  local copies, waits for them, and re-layouts  34.3 us (4%)
  between operations  15.1 us (2%)
  starting transfers between devices  10.8 us (1%)
    pallas_call x1, Pallas kernels, line_gather(): pl.pallas_call(functools.partial(line_gather_kernel, (row_count, col_coun...  138 us
    pallas_call x1, Pallas kernels, sum_all(): pl.pallas_call(functools.partial(sum_kernel, (row_count, col_count), coun...  133 us
    pallas_call x1, Pallas kernels, gather_all(): pl.pallas_call(functools.partial(gather_kernel, (row_count, col_count), c...  128 us
    pallas_call x1, Pallas kernels, line_sum(): pl.pallas_call(functools.partial(line_sum_kernel, (row_count, col_count))...  77 us
    dot_general x10, matrix products, matmul(): return jnp.dot(left, right, preferred_element_type=f32)  70.3 us
    dot_general x10, matrix products, against(): lax.dot_general(left, right, (((1,), (1,)), ((), ())), preferred_element_...  49.9 us
    dot_general x10, matrix products, over_rows(): lax.dot_general(left, right, (((0,), (0,)), ((), ())), preferred_element_...  45.6 us
    ppermute x4, waiting for transfers between devices, shift(): return lax.ppermute(values, 'col', pairs)  25.4 us
  transfers between devices with their start and end apart: 9, of which 4 were waited for; matrix products, arithmetic and copies ran while one was open for 30% of the time, Pallas kernels for 41%

profile of v2, /device:TPU:0, one launch (start us, length us, event | category | flops | bytes accessed | tf_op | source)
XLA Modules:
  0.0 854.8 jit_solution(13193731042181574528)
XLA Ops:
  8.2 3.8 copy.82
  12.8 127.6 %gather_weights.1 = (bf16[4,2048,768]{2,1,0:T(8,128)(2,1)}, bf16[4,2048,512]{2,1,0:T(8,128)(2,1)}) custom-call(bf16[256,768]{1,0:T(8,128)(2,1)} %pad_maximum_fusion.18.refs_0_, bf16[256,512]{1,0:T(8,128)(2,1)} %refs_1_.1), custom_call_target="tpu_custom_call" | custom-call | bytes 20971520 | tf_op jit(solution)/shard_map/gather_weights/pallas_call | solution.py:335
  142.8 3.5 fusion.104
  146.3 4.7 fusion.101
  161.0 9.8 %collective-permute-done = bf16[4,256,2,2,64]{1,4,2,0,3:T(8,128)(2,1)} collective-permute-done((bf16[4,256,2,2,64]{1,4,2,0,3:T(8,128)(2,1)}, bf16[4,256,2,2,64]{1,4,2,0,3:T(8,128)(2,1)}, u32[]{:S(2)}, u32[]{:S(2)}) %collective-permute-start) | collective-permute-done | bytes 524320 | tf_op jit(solution)/shard_map/ppermute | solution.py:936
  170.8 5.5 collective-permute-start.1
  179.2 3.3 subtract_convert_fusion.1
  182.5 4.1 collective-permute-done.1
  188.1 14.2 %fusion.163 = (f32[4,2,4,256]{3,2,1,0:T(4,128)S(1)}, f32[4,2,4,256,768]{3,4,2,1,0:T(8,128)}) fusion(pred[256,768]{0,1:T(8,128)(4,1)} %fusion.125, bf16[4,768,2,2,64]{1,4,2,0,3:T(8,128)(2,1)S(1)} %maximum_maximum_fusion, bf16[4,256,2,4,32]{1,4,3,2,0:T(8,128)(2,1)} %bitcast.287, bf16[4,256,2,4,32]{1,4,3,2,0:T(8,128)(2,1)S(1)} %bitcast.285), kind=kOutput, calls=%fused_computation.219 | convolution fusion | flops 832570112 | bytes 27230208 | tf_op jit(solution)/shard_map/sub | solution.py:1018
  202.4 11.1 %fusion.92 = bf16[4,256,2,4,64]{1,4,3,2,0:T(8,128)(2,1)} fusion(bf16[4,768,2,2,64]{1,4,2,0,3:T(8,128)(2,1)S(1)} %maximum_maximum_fusion, f32[4,2,4,256,768]{3,4,2,1,0:T(8,128)} %get-tuple-element.87, f32[4,2,4,256]{3,2,1,0:T(4,128)S(1)} %get-tuple-element.86), kind=kOutput, calls=%fused_computation.135 | convolution fusion | flops 818413568 | bytes 27033600 | tf_op jit(solution)/shard_map/zkgts,zskd->ztkgd/dot_general | solution.py:1023
  222.6 138.0 %gather_line.1 = bf16[1024,2048]{1,0:T(8,128)(2,1)} custom-call(bf16[256,2048]{1,0:T(8,128)(2,1)} %multiply_convert_fusion.1.own), custom_call_target="tpu_custom_call" | custom-call | bytes 4194304 | tf_op jit(solution)/shard_map/gather_line/pallas_call | solution.py:373
  360.7 23.8 %fusion.164 = f32[1024,4096]{0,1:T(8,128)} fusion(bf16[1024,2048]{1,0:T(8,128)(2,1)} %gather_line.1, bf16[2048,4096]{1,0:T(8,128)(2,1)} %all-gather.8.cloned.1.call-done), kind=kOutput, calls=%fused_computation.220 | convolution fusion | flops 17179869184 | bytes 37748736 | tf_op jit(solution)/shard_map/dot_general | solution.py:928
  384.5 9.2 %all-gather.4.cloned.1.call-done = bf16[2048,2048]{1,0:T(8,128)(2,1)} async-done(((bf16[256,2048]{1,0:T(8,128)(2,1)}), bf16[2048,2048]{1,0:T(8,128)(2,1)}) %all-gather.4.cloned.1.call-update) | async-done | bytes 8388624 | tf_op jit(solution)/shard_map/all_gather | solution.py:994
  393.7 23.4 %fusion.10 = (bf16[1024,2048]{0,1:T(8,128)(2,1)}, bf16[1024,2048]{0,1:T(8,128)(2,1)}, bf16[1024,2048]{0,1:T(8,128)(2,1)}) fusion(f32[1024,4096]{0,1:T(8,128)} %fusion.164, bf16[2048,2048]{1,0:T(8,128)(2,1)} %all-gather.4.cloned.1.call-done, bf16[1024,2048]{1,0:T(8,128)(2,1)} %all-gather.6.cloned.1.call-done), kind=kOutput, calls=%fused_computation.21 | convolution fusion | flops 8621391872 | bytes 41943040 | tf_op jit(solution)/shard_map/dot_general | solution.py:928
  417.1 14.1 %convert_bitcast_fusion = bf16[2048,2048]{0,1:T(8,128)(2,1)} fusion(bf16[1024,2048]{0,1:T(8,128)(2,1)} %get-tuple-element.64, bf16[1024,2048]{1,0:T(8,128)(2,1)} %all-gather.6.cloned.1.call-done), kind=kOutput, calls=%fused_computation.23 | convolution fusion | flops 8594128896 | bytes 16777216 | tf_op jit(solution)/shard_map/dot_general | solution.py:924
  431.3 23.9 %fusion.18.terms = bf16[1024,2048]{1,0:T(8,128)(2,1)} fusion(bf16[2048,4096]{1,0:T(8,128)(2,1)} %all-gather.8.cloned.1.call-done, bf16[1024,2048]{0,1:T(8,128)(2,1)} %get-tuple-element.63, bf16[1024,2048]{0,1:T(8,128)(2,1)} %get-tuple-element.62), kind=kOutput, calls=%fused_computation.38 | convolution fusion | flops 17198743552 | bytes 29360128 | tf_op jit(solution)/shard_map/dot_general | solution.py:920
  455.2 77.0 %sum_line.1 = f32[256,2048]{1,0:T(8,128)S(1)} custom-call(bf16[1024,2048]{1,0:T(8,128)(2,1)} %fusion.18.terms), custom_call_target="tpu_custom_call" | custom-call | flops 2097152 | bytes 4194304 | tf_op jit(solution)/shard_map/sum_line/pallas_call | solution.py:494
  532.2 23.8 %convolution_convert_fusion = bf16[2048,4096]{1,0:T(8,128)(2,1)} fusion(bf16[1024,2048]{1,0:T(8,128)(2,1)S(1)} %copy-done.11, bf16[1024,2048]{0,1:T(8,128)(2,1)} %get-tuple-element.63, bf16[1024,2048]{0,1:T(8,128)(2,1)} %get-tuple-element.62), kind=kOutput, calls=%fused_computation.9 | convolution fusion | flops 17205035008 | bytes 29360128 | tf_op jit(solution)/shard_map/dot_general | solution.py:924
  561.3 3.1 fusion.116
  567.3 3.5 fusion.107
  572.2 3.5 fusion.110
  576.9 18.1 %fusion.1 = (f32[4,2,4,256]{3,2,1,0:T(4,128)S(1)}, f32[4,2,768,256,4]{3,2,4,1,0:T(8,128)}) fusion(f32[4,2,4,256,768]{3,4,2,1,0:T(8,128)} %get-tuple-element.87, f32[4,2,4,256]{3,2,1,0:T(4,128)S(1)} %copy-done.46, bf16[1,256,2,4,64]{1,4,3,2,0:T(8,128)(2,1)S(1)} %bitcast.290, bf16[1,256,2,4,64]{1,4,3,2,0:T(8,128)(2,1)S(1)} %bitcast.292, ...), kind=kOutput, calls=%fused_computation.3 | convolution fusion | flops 828366848 | bytes 52232192 | tf_op jit(solution)/shard_map/ztkgd,zskd->zkgts/dot_general | solution.py:1061
  595.1 18.5 %fusion.3 = bf16[4,2,4,256,768]{3,4,2,1,0:T(8,128)(2,1)S(1)} fusion(f32[4,2,768,256,4]{3,2,4,1,0:T(8,128)} %get-tuple-element.91, f32[4,2,4,256]{3,2,1,0:T(4,128)S(1)} %get-tuple-element.90, f32[4,2,4,256,768]{3,4,2,1,0:T(8,128)} %get-tuple-element.87, f32[4,2,4,256]{3,2,1,0:T(4,128)S(1)} %copy-done.46), kind=kLoop, calls=%fused_computation.5 | loop fusion | flops 25165824 | bytes 62980096 | tf_op jit(solution)/shard_map/convert_element_type | solution.py:1063
  613.5 4.6 copy-done
  618.1 6.2 fusion.85
  624.4 11.2 %fusion.86 = f32[4,768,2,1,64]{1,4,2,0,3:T(8,128)S(1)} fusion(bf16[1,256,2,4,64]{1,4,3,2,0:T(8,128)(2,1)S(1)} %bitcast.291, bf16[1,256,2,4,64]{1,4,3,2,0:T(8,128)(2,1)} %bitcast.293, bf16[1,256,2,4,64]{1,4,3,2,0:T(8,128)(2,1)} %bitcast.297, bf16[1,256,2,4,64]{1,4,3,2,0:T(8,128)(2,1)} %bitcast.295, f32[4,2,4,256,768]{3,4,2,1,0:T(8,128)} %get-tuple-element.87, ...), kind=kOutput, calls=%fused_computation.133 | convolution fusion | flops 819462144 | bytes 27820032 | tf_op jit(solution)/shard_map/zkgts,ztkgd->zskd/dot_general | solution.py:1070
  641.0 14.9 %convolution_convert_fusion.1.refs_2_ = bf16[1024,2048]{1,0:T(8,128)(2,1)} fusion(bf16[1024,2048]{0,1:T(8,128)(2,1)} %get-tuple-element.64, bf16[2048,2048]{1,0:T(8,128)(2,1)} %all-gather.4.cloned.1.call-done), kind=kOutput, calls=%fused_computation.39 | convolution fusion | flops 8592031744 | bytes 16777216 | tf_op jit(solution)/shard_map/dot_general | solution.py:920
  655.9 3.9 pad_maximum_fusion.2.refs_1_
  665.6 11.5 %collective-permute-done.3 = bf16[4,256,2,2,64]{1,4,2,0,3:T(8,128)(2,1)S(1)} collective-permute-done((bf16[4,256,2,2,64]{1,4,2,0,3:T(8,128)(2,1)S(1)}, bf16[4,256,2,2,64]{1,4,2,0,3:T(8,128)(2,1)S(1)}, u32[]{:S(2)}, u32[]{:S(2)}) %collective-permute-start.3) | collective-permute-done | bytes 524320 | tf_op jit(solution)/shard_map/ppermute | solution.py:936
  689.0 6.0 pad_maximum_fusion.refs_0_
  694.9 133.4 %sum_weights.1 = (f32[256,768]{1,0:T(8,128)}, f32[256,512]{1,0:T(8,128)}, f32[256,2048]{1,0:T(8,128)}, f32[32,128]{1,0:T(8,128)}) custom-call(bf16[4,4,2,256,768]{4,3,2,1,0:T(8,128)(2,1)} %pad_maximum_fusion.refs_0_, bf16[4,4,2,256,512]{4,3,2,1,0:T(8,128)(2,1)} %pad_maximum_fusion.2.refs_1_, bf16[1024,2048]{1,0:T(8,128)(2,1)} %convolution_convert_fusion.1.refs_2_, ...), custom_call_target="tpu_custom_call" | custom-call | bytes 41943040 | tf_op jit(solution)/shard_map/sum_weights/pallas_call | solution.py:857
  840.7 6.6 reshape.279
  (220 shorter events, 74.0 us)
Async XLA Ops:
  7.2 353.5 %all-gather.8.cloned.1.call-start = ((), (), s32[]{:S(2)}) async-start(), calls=%async_computation.4 | async-start | bytes 18874368 | tf_op jit(solution)/shard_map/all_gather | solution.py:993
  12.0 129.9 %copy-start.4 = (bf16[256,2048]{1,0:T(8,128)(2,1)S(1)}, bf16[256,2048]{1,0:T(8,128)(2,1)}, u32[]{:S(2)}) copy-start(bf16[256,2048]{1,0:T(8,128)(2,1)} %param.10) | copy-start | bytes 3145732
  12.8 130.0 %copy-start.51 = (bf16[2048]{0:T(1024)(128)(2,1)S(1)}, bf16[2048]{0:T(1024)(128)(2,1)}, u32[]{:S(2)}) copy-start(bf16[2048]{0:T(1024)(128)(2,1)} %param.12) | copy-start | bytes 12292
  140.4 244.1 %all-gather.6.cloned.1.call-start = ((), (), s32[]{:S(2)}) async-start(), calls=%async_computation.3 | async-start | bytes 5242880 | tf_op jit(solution)/shard_map/all_gather | solution.py:983
  141.1 252.6 %all-gather.4.cloned.1.call-start = ((), (), s32[]{:S(2)}) async-start(), calls=%async_computation.2 | async-start | bytes 9437184 | tf_op jit(solution)/shard_map/all_gather | solution.py:994
  141.9 696.2 %reduce-scatter.5.cloned.1.call-start = ((), (), s32[]{:S(2)}) async-start(), calls=%async_computation.6 | async-start | bytes 9437184 | tf_op jit(solution)/shard_map/reduce_scatter | solution.py:1049
  142.8 9.9 %copy-start.43 = (f32[256]{0:T(256)}, f32[256]{0:T(256)S(1)}, u32[]{:S(2)}) copy-start(f32[256]{0:T(256)S(1)} %get-tuple-element.83) | copy-start | bytes 3076
  142.8 9.9 %copy-start.34 = (f32[2048]{0:T(1024)}, f32[2048]{0:T(1024)S(1)}, u32[]{:S(2)}) copy-start(f32[2048]{0:T(1024)S(1)} %convert_element_type.119) | copy-start | bytes 24580
  156.2 23.0 %copy-start.31 = (f32[256,32]{0,1:T(8,128)}, f32[256,32]{0,1:T(8,128)S(1)}, u32[]{:S(2)}) copy-start(f32[256,32]{0,1:T(8,128)S(1)} %get-tuple-element.81) | copy-start | bytes 98308
  156.3 20.1 %copy-start.52 = (bf16[2048]{0:T(1024)(128)(2,1)S(1)}, bf16[2048]{0:T(1024)(128)(2,1)}, u32[]{:S(2)}) copy-start(bf16[2048]{0:T(1024)(128)(2,1)} %param.16) | copy-start | bytes 12292
  157.2 13.6 %collective-permute-start = (bf16[4,256,2,2,64]{1,4,2,0,3:T(8,128)(2,1)}, bf16[4,256,2,2,64]{1,4,2,0,3:T(8,128)(2,1)}, u32[]{:S(2)}, u32[]{:S(2)}) collective-permute-start(bf16[4,256,2,2,64]{1,4,2,0,3:T(8,128)(2,1)} %pad_maximum_fusion.15), channel_id=1, source_target_pairs={{0,1},{1,2},{2,3},{4,5},{5,6},{6,7},{8,9},{9,10},{10,11},{12,13},{... | collective-permute-start | bytes 1572872 | tf_op jit(solution)/shard_map/ppermute | solution.py:936
  170.8 15.8 %collective-permute-start.1 = (bf16[4,256,2,2,64]{1,4,2,0,3:T(8,128)(2,1)}, bf16[4,256,2,2,64]{1,4,2,0,3:T(8,128)(2,1)}, u32[]{:S(2)}, u32[]{:S(2)}) collective-permute-start(bf16[4,256,2,2,64]{1,4,2,0,3:T(8,128)(2,1)} %collective-permute-done), channel_id=1, source_target_pairs={{0,1},{1,2},{2,3},{4,5},{5,6},{6,7},{8,9},{9,10},{10,11},{12,13},{... | collective-permute-start | bytes 1572872 | tf_op jit(solution)/shard_map/ppermute | solution.py:936
  176.4 44.3 %copy-start.41 = (f32[2048]{0:T(1024)}, f32[2048]{0:T(1024)S(1)}, u32[]{:S(2)}) copy-start(f32[2048]{0:T(1024)S(1)} %convert_element_type.127) | copy-start | bytes 24580
  182.5 19.9 %copy-start.30 = (bf16[4,256,8,32]{1,3,2,0:T(8,128)(2,1)}, bf16[4,256,8,32]{1,3,2,0:T(8,128)(2,1)S(1)}, u32[]{:S(2)}) copy-start(bf16[4,256,8,32]{1,3,2,0:T(8,128)(2,1)S(1)} %get-tuple-element.67) | copy-start | bytes 1572868
  188.1 14.3 %copy-start.14 = (bf16[4,768,2,2,64]{1,4,2,0,3:T(8,128)(2,1)}, bf16[4,768,2,2,64]{1,4,2,0,3:T(8,128)(2,1)S(1)}, u32[]{:S(2)}) copy-start(bf16[4,768,2,2,64]{1,4,2,0,3:T(8,128)(2,1)S(1)} %maximum_maximum_fusion) | copy-start | bytes 4718596
  202.4 11.1 %copy-start.45 = (f32[4,2,4,256]{3,2,1,0:T(4,128)}, f32[4,2,4,256]{3,2,1,0:T(4,128)S(1)}, u32[]{:S(2)}) copy-start(f32[4,2,4,256]{3,2,1,0:T(4,128)S(1)} %get-tuple-element.86) | copy-start | bytes 98308
  202.4 15.2 %slice-start.3 = ((s8[8388608]{0:T(1024)(128)(4,1)}), s8[4194304]{0:T(1024)(128)(4,1)S(1)}, s32[]{:S(2)}) async-start(s8[8388608]{0:T(1024)(128)(4,1)} %bitcast.262), calls=%async_computation.10 | async-start | bytes 8388608
  202.4 15.1 %slice-start.4 = ((s8[8388608]{0:T(1024)(128)(4,1)}), s8[4194304]{0:T(1024)(128)(4,1)S(1)}, s32[]{:S(2)}) async-start(s8[8388608]{0:T(1024)(128)(4,1)} %bitcast.262), calls=%async_computation.11 | async-start | bytes 8388608
  431.2 409.4 %reduce-scatter.3.cloned.1.call-start = ((), (), s32[]{:S(2)}) async-start(), calls=%async_computation.5 | async-start | bytes 18874368 | tf_op jit(solution)/shard_map/reduce_scatter | solution.py:1048
  455.2 77.0 %copy-start.11 = (bf16[1024,2048]{1,0:T(8,128)(2,1)S(1)}, bf16[1024,2048]{1,0:T(8,128)(2,1)}, u32[]{:S(2)}) copy-start(bf16[1024,2048]{1,0:T(8,128)(2,1)} %gather_line.1) | copy-start | bytes 12582916
  561.3 10.9 %copy-start.6 = (bf16[256,2048]{1,0:T(8,128)(2,1)}, bf16[256,2048]{1,0:T(8,128)(2,1)S(1)}, u32[]{:S(2)}) copy-start(bf16[256,2048]{1,0:T(8,128)(2,1)S(1)} %get-tuple-element.60) | copy-start | bytes 3145732
  572.2 22.9 %copy-start.39 = (bf16[256,512]{0,1:T(8,128)(2,1)}, bf16[256,512]{0,1:T(8,128)(2,1)S(1)}, u32[]{:S(2)}) copy-start(bf16[256,512]{0,1:T(8,128)(2,1)S(1)} %copy.62) | copy-start | bytes 786436
  576.9 18.2 %copy-start.40 = (bf16[256,512]{0,1:T(8,128)(2,1)}, bf16[256,512]{0,1:T(8,128)(2,1)S(1)}, u32[]{:S(2)}) copy-start(bf16[256,512]{0,1:T(8,128)(2,1)S(1)} %copy.63) | copy-start | bytes 786436
  624.4 11.2 %copy-start.8 = (f32[4,768,2,1,64]{1,4,2,0,3:T(8,128)S(1)}, f32[4,768,2,1,64]{1,4,2,0,3:T(8,128)}, u32[]{:S(2)}) copy-start(f32[4,768,2,1,64]{1,4,2,0,3:T(8,128)} %fusion.85) | copy-start | bytes 4718596
  636.4 23.4 %collective-permute-start.2 = (bf16[4,256,2,2,64]{1,4,2,0,3:T(8,128)(2,1)}, bf16[4,256,2,2,64]{1,4,2,0,3:T(8,128)(2,1)}, u32[]{:S(2)}, u32[]{:S(2)}) collective-permute-start(bf16[4,256,2,2,64]{1,4,2,0,3:T(8,128)(2,1)} %fusion.124), channel_id=1, source_target_pairs={{1,0},{2,1},{3,2},{5,4},{6,5},{7,6},{9,8},{10,9},{11,10},{13,12},{... | collective-permute-start | bytes 1572872 | tf_op jit(solution)/shard_map/ppermute | solution.py:936
  640.2 22.5 %slice-start = ((s8[12582912]{0:T(1024)(128)(4,1)}), s8[4194304]{0:T(1024)(128)(4,1)S(1)}, s32[]{:S(2)}) async-start(s8[12582912]{0:T(1024)(128)(4,1)} %bitcast.242), calls=%async_computation.7 | async-start | bytes 8388608
  641.0 21.7 %slice-start.1 = ((s8[12582912]{0:T(1024)(128)(4,1)}), s8[4194304]{0:T(1024)(128)(4,1)S(1)}, s32[]{:S(2)}) async-start(s8[12582912]{0:T(1024)(128)(4,1)} %bitcast.242), calls=%async_computation.8 | async-start | bytes 8388608
  641.0 21.7 %slice-start.2 = ((s8[12582912]{0:T(1024)(128)(4,1)}), s8[4194304]{0:T(1024)(128)(4,1)S(1)}, s32[]{:S(2)}) async-start(s8[12582912]{0:T(1024)(128)(4,1)} %bitcast.242), calls=%async_computation.9 | async-start | bytes 8388608
  661.1 16.0 %collective-permute-start.3 = (bf16[4,256,2,2,64]{1,4,2,0,3:T(8,128)(2,1)S(1)}, bf16[4,256,2,2,64]{1,4,2,0,3:T(8,128)(2,1)S(1)}, u32[]{:S(2)}, u32[]{:S(2)}) collective-permute-start(bf16[4,256,2,2,64]{1,4,2,0,3:T(8,128)(2,1)S(1)} %fusion.121), channel_id=1, source_target_pairs={{1,0},{2,1},{3,2},{5,4},{6,5},{7,6},{9,8},{10,9},{11,10},{13,12},{... | collective-permute-start | bytes 1572872 | tf_op jit(solution)/shard_map/ppermute | solution.py:936
  662.8 14.8 %slice-start.5 = ((s8[12582912]{0:T(1024)(128)(4,1)}), s8[4194304]{0:T(1024)(128)(4,1)S(1)}, s32[]{:S(2)}) async-start(s8[12582912]{0:T(1024)(128)(4,1)} %bitcast.271), calls=%async_computation.12 | async-start | bytes 8388608
  662.8 14.8 %slice-start.6 = ((s8[12582912]{0:T(1024)(128)(4,1)}), s8[4194304]{0:T(1024)(128)(4,1)S(1)}, s32[]{:S(2)}) async-start(s8[12582912]{0:T(1024)(128)(4,1)} %bitcast.271), calls=%async_computation.13 | async-start | bytes 8388608
  665.6 12.0 %slice-start.7 = ((s8[12582912]{0:T(1024)(128)(4,1)}), s8[4194304]{0:T(1024)(128)(4,1)S(1)}, s32[]{:S(2)}) async-start(s8[12582912]{0:T(1024)(128)(4,1)} %bitcast.271), calls=%async_computation.14 | async-start | bytes 8388608
  (39 other events, 134.9 us)
Sparse Core Ops, SparseCore 0:
  140.5 87.1 all-gather.7
  229.2 109.7 all-gather.5
  340.9 52.7 all-gather.3
  431.4 71.2 reduce-scatter.4
  556.2 114.0 reduce-scatter.2

commit v3 on v2

--- a/solution.py
+++ b/solution.py
@@ -149,8 +149,8 @@
 
 
 class PlaneGather:
-    def __init__(self, place, block, send_sems, recv_sems):
-        self.place, self.block = place, block
+    def __init__(self, place, block, own, send_sems, recv_sems):
+        self.place, self.block, self.own = place, block, own
         self.sends, self.recvs = send_sems, recv_sems
 
     @staticmethod
@@ -189,7 +189,8 @@
         number, device = self.copy(half, kind, i, j)
         oi, oj = (i - 1, j) if kind == 0 else ((i, j - 1) if kind == 1 else (i, j))
         ref = self.block(self.origin(half, oi, oj), half)
-        return remote(ref, ref, self.sends.at[half, number], self.recvs.at[half, number], device)
+        source = self.own(half) if (oi, oj) == (0, 0) else ref
+        return remote(source, ref, self.sends.at[half, number], self.recvs.at[half, number], device)
 
     def receiver(self, half, kind, i, j):
         number, device = self.copy(half, kind, i, j)
@@ -250,106 +251,137 @@
                 self.receiver(*copy).wait_recv()
 
 
-def gather_kernel(sizes, count, *refs):
+def nearby(place, number):
+    low, high = place.col, place.cols - 1 - place.col
+    both = jnp.minimum(low, high)
+    way = jnp.minimum(jnp.maximum(high - low, -1), 1)
+    step = (number + 1) // 2 * (-1 if number % 2 else 1)
+    paired = jnp.minimum(jnp.maximum(2 * both - number + 1, 0), 1)
+    return place.col + paired * step + (1 - paired) * way * (number - both)
+
+
+def gather_kernel(sizes, count, inner, *refs):
     row_count, col_count = sizes
-    own = refs[:count]
-    full = refs[count : 2 * count]
-    local_sems, zs, zr, ps, pr = refs[2 * count :]
+    every = count + inner
+    own, own_act = refs[:every], refs[every]
+    full, full_act = refs[every + 1 : 2 * every + 1], refs[2 * every + 1]
+    local_sems, zs, zr, ps, pr = refs[2 * every + 2 :]
     place = Place(row_count, col_count)
     place.greet(True, True)
-    deep = own[0].shape[0]
-    half_deep = deep // 2
+    token_rows = own_act.shape[0]
+
+    def at(n, col, row):
+        deep = own[n].shape[0]
+        if n < count:
+            return full[n].at[col, pl.ds(row * deep, deep)]
+        return full[n].at[pl.ds(row * deep, deep)]
 
     lines = [
-        LineGather(
-            place,
-            own[n],
-            lambda j, n=n: full[n].at[j, pl.ds(place.row * deep, deep)],
-            zs.at[n],
-            zr.at[n],
-        )
+        LineGather(place, own[n], lambda j, n=n: at(n, j, place.row), zs.at[n], zr.at[n])
         for n in range(count)
     ]
+    acts = LineGather(
+        place,
+        own_act,
+        lambda j: full_act.at[pl.ds(j * token_rows, token_rows)],
+        zs.at[count],
+        zr.at[count],
+    )
+
     def keep(n):
-        return pltpu.make_async_copy(
-            own[n], full[n].at[place.col, pl.ds(place.row * deep, deep)], local_sems.at[n]
-        )
-
-    for n in range(count):
+        if n == every:
+            return pltpu.make_async_copy(own_act, acts.block(place.col), local_sems.at[n])
+        return pltpu.make_async_copy(own[n], at(n, place.col, place.row), local_sems.at[n])
+
+    for n in range(every + 1):
         keep(n).start()
     for line in lines:
         for way in (0, 1):
             line.send(way, 1)
-    for n in range(count):
+
+    def inside(n, col, near):
+        deep = own[n].shape[0]
+        half = deep // 2
+
+        def block(row, number):
+            rows = pl.ds(row * deep + number * half, half)
+            return full[n].at[col, rows] if n < count else full[n].at[rows]
+
+        def mine(number):
+            return own[n].at[pl.ds(number * half, half)] if near else block(place.row, number)
+
+        return PlaneGather(place, block, mine, ps.at[n, col], pr.at[n, col])
+
+    entries = [(n, k) for k in range(col_count) for n in range(count)]
+    entries += [(n, 0) for n in range(count, every)]
+    parts = [inside(n, nearby(place, k), k == 0) for n, k in entries]
+    act_steps = list(range(1, col_count))
+
+    def act_step():
+        if act_steps:
+            for way in (0, 1):
+                acts.receive(way, act_steps[0])
+            act_steps.pop(0)
+
+    for number in range(len(parts) + 2):
+        if number < len(parts):
+            n, k = entries[number]
+            if n == 0 and k > 0:
+                for line in lines:
+                    for way in (0, 1):
+                        line.receive(way, k)
+                if k == 1:
+                    for way in (0, 1):
+                        acts.send(way, 1)
+                if k >= 3:
+                    act_step()
+            parts[number].first()
+        if 1 <= number <= len(parts):
+            parts[number - 1].second()
+        if 2 <= number:
+            parts[number - 2].third()
+        if number >= len(parts):
+            act_step()
+    while act_steps:
+        act_step()
+    for n in range(every + 1):
         keep(n).wait()
-
-    def inside(n, col):
-        return PlaneGather(
-            place,
-            lambda row, half: full[n].at[
-                col, pl.ds(row * deep + half * half_deep, half_deep)
-            ],
-            ps.at[n, col],
-            pr.at[n, col],
-        )
-
-    slots = [(0, 0)] + [(way, step) for step in range(1, col_count) for way in (0, 1)]
-    entries = [(way, step, n) for way, step in slots for n in range(count)]
-
-    def at_entry(entry):
-        way, step, n = entry
-        if step == 0:
-            return None, place.col
-        return lines[n].gets_at(way, step)
-
-    for number in range(len(entries) + 2):
-        if number < len(entries):
-            way, step, n = entries[number]
-            condition, col = at_entry(entries[number])
-            if step > 0:
-                lines[n].receive(way, step)
-            when(condition, lambda: inside(n, col).first())
-        if 1 <= number <= len(entries):
-            condition, col = at_entry(entries[number - 1])
-            m = entries[number - 1][2]
-            when(condition, lambda: inside(m, col).second())
-        if 2 <= number:
-            condition, col = at_entry(entries[number - 2])
-            m = entries[number - 2][2]
-            when(condition, lambda: inside(m, col).third())
-    for entry in entries:
-        condition, col = at_entry(entry)
-        m = entry[2]
-        when(condition, lambda: inside(m, col).finish())
-    for line in lines:
+    for part in parts:
+        part.finish()
+    for line in lines + [acts]:
         line.finish()
 
 
-def gather_all(weights, row_count, col_count):
-    count = len(weights)
+def gather_all(weights, inner_weights, act, row_count, col_count):
+    count, inner = len(weights), len(inner_weights)
     sizes = plane_sizes(row_count)
-    deep = weights[0].shape[0]
     steps = max(col_count - 1, 1)
-    plane_sems = (count, col_count, 2, PlaneGather.sem_count(sizes))
+    every = list(weights) + list(inner_weights)
+    plane_sems = (count + inner, col_count, 2, PlaneGather.sem_count(sizes))
     moved = sum(w.size for w in weights) * row_count * col_count * 2
     return pl.pallas_call(
-        functools.partial(gather_kernel, (row_count, col_count), count),
+        functools.partial(gather_kernel, (row_count, col_count), count, inner),
         out_shape=[
-            jax.ShapeDtypeStruct((col_count, row_count * deep, w.shape[1]), bf16) for w in weights
-        ],
-        in_specs=[ANY] * count,
-        out_specs=[ANY] * count,
+            jax.ShapeDtypeStruct((col_count, row_count * w.shape[0], w.shape[1]), bf16)
+            for w in weights
+        ]
+        + [
+            jax.ShapeDtypeStruct((row_count * w.shape[0], w.shape[1]), bf16) for w in inner_weights
+        ]
+        + [jax.ShapeDtypeStruct((col_count * act.shape[0], act.shape[1]), bf16)],
+        in_specs=[pl.BlockSpec(memory_space=pltpu.VMEM)] * (len(every) + 1),
+        out_specs=[ANY] * (len(every) + 1),
         scratch_shapes=[
-            pltpu.SemaphoreType.DMA((count,)),
-            pltpu.SemaphoreType.DMA((count, 2, steps)),
-            pltpu.SemaphoreType.DMA((count, 2, steps)),
+            pltpu.SemaphoreType.DMA((len(every) + 1,)),
+            pltpu.SemaphoreType.DMA((count + 1, 2, steps)),
+            pltpu.SemaphoreType.DMA((count + 1, 2, steps)),
             pltpu.SemaphoreType.DMA(plane_sems),
             pltpu.SemaphoreType.DMA(plane_sems),
         ],
         compiler_params=pltpu.CompilerParams(collective_id=0, has_side_effects=True),
         cost_estimate=pl.CostEstimate(flops=0, bytes_accessed=moved, transcendentals=0),
         name="gather_weights",
-    )(*weights)
+    )(*every, act)
 
 
 def line_gather_kernel(sizes, own, full, local_sem, sends, recvs):
@@ -373,7 +405,7 @@
     return pl.pallas_call(
         functools.partial(line_gather_kernel, (row_count, col_count)),
         out_shape=jax.ShapeDtypeStruct((col_count * own.shape[0], own.shape[1]), own.dtype),
-        in_specs=[ANY],
+        in_specs=[pl.BlockSpec(memory_space=pltpu.VMEM)],
         out_specs=ANY,
         scratch_shapes=[
             pltpu.SemaphoreType.DMA,
@@ -405,16 +437,11 @@
         self.place, self.own, self.held = place, own, held
         self.sends, self.recvs = send_sems, recv_sems
 
-    def target(self, way, distance):
-        col, last = self.place.col, self.place.cols - 1
-        if way == 0:
-            return col + distance <= last, col + distance
-        return col >= distance, col - distance
-
-    def gets(self, way, distance):
-        col, last = self.place.col, self.place.cols - 1
-        there, _ = self.target(way, distance)
-        return there & ((col > 0) if way == 0 else (col < last))
+    def distance(self, way, col):
+        return col - self.place.col if way == 0 else self.place.col - col
+
+    def feeds(self, way):
+        return self.place.col > 0 if way == 0 else self.place.col < self.place.cols - 1
 
     def copy(self, way, distance, source):
         return remote(
@@ -435,25 +462,32 @@
             (self.place.row, self.place.col + (1, -1)[way]),
         )
 
-    def step(self, way, distance):
-        condition, col = self.target(way, distance)
-        if distance < self.place.cols - 1:
-
-            def add():
-                self.arrived(way, distance).wait_recv()
-                add_rows(self.own(col), self.held.at[way, distance])
-
-            when(self.gets(way, distance), add)
-        when(condition, lambda: self.copy(way, distance, self.own(col)).start())
+    def early(self, col, allowed):
+        for way in (0, 1):
+            far = self.distance(way, col)
+
+            @pl.when(allowed & (far > 0) & jnp.logical_not(self.feeds(way)))
+            def _():
+                self.copy(way, far, self.own(col)).start()
+
+    def late(self, col, allowed):
+        for way in (0, 1):
+            far = self.distance(way, col)
+
+            @pl.when(allowed & (far > 0) & self.feeds(way))
+            def _():
+                self.arrived(way, far).wait_recv()
+                add_rows(self.own(col), self.held.at[way, far])
+                self.copy(way, far, self.own(col)).start()
 
     def last(self, out):
         if self.place.cols > 1:
             for way in (0, 1):
-                when(self.gets(way, 0), lambda: self.arrived(way, 0).wait_recv())
+                when(self.feeds(way), lambda: self.arrived(way, 0).wait_recv())
         own = self.own(self.place.col)
         rows = own.shape[0]
         piece = 32 if rows % 32 == 0 else 16
-        has = [self.gets(way, 0) for way in (0, 1)]
+        has = [self.feeds(way) for way in (0, 1)]
 
         def body(n, carry):
             at = pl.ds(pl.multiple_of(n * piece, piece), piece)
@@ -470,45 +504,195 @@
     def finish(self):
         for distance in range(1, self.place.cols):
             for way in (0, 1):
-                condition, col = self.target(way, distance)
-                when(condition, lambda: self.copy(way, distance, self.own(col)).wait_send())
-
-
-def line_sum_kernel(sizes, terms, out, held, sends, recvs):
+                col = self.place.col + (distance if way == 0 else -distance)
+                there = col < self.place.cols if way == 0 else col >= 0
+                when(there, lambda: self.copy(way, distance, self.own(col)).wait_send())
+
+
+def dot_tokens(left, right):
+    return lax.dot_general(left, right, (((0,), (0,)), ((), ())), preferred_element_type=f32)
+
+
+def mlp_kernel(sizes, tile, wide, *refs):
+    hn_in, dy_in, wh_in, wd_in, grad_out, y_out, dwh_out, dwd_out = refs[:8]
+    hn, dy, wh, wd, act, dgu, terms, staged, held = refs[8:17]
+    token_sems, weight_sems, y_sems, dw_sems, sends, recvs = refs[17:]
     place = Place(*sizes)
+    cols = place.cols
+    hidden = wd.shape[1]
+    width = wd.shape[0]
+    tiles = hidden // tile
+    wides = width // wide
+    tokens = hn.shape[1]
+    line = LineSum(place, lambda j: terms.at[j], held, sends, recvs)
+
+    def token_copies(j):
+        return (
+            pltpu.make_async_copy(hn_in.at[j], hn.at[j], token_sems.at[0, j]),
+            pltpu.make_async_copy(dy_in.at[j], dy.at[j], token_sems.at[1, j]),
+        )
+
+    def part(number, base=0):
+        return pl.ds(pl.multiple_of(base + number * tile, tile), tile)
+
+    def weight_copies(f):
+        gate, up = part(f), part(f, hidden)
+        return (
+            pltpu.make_async_copy(wh_in.at[:, gate], wh.at[:, gate], weight_sems.at[0, f]),
+            pltpu.make_async_copy(wh_in.at[:, up], wh.at[:, up], weight_sems.at[1, f]),
+            pltpu.make_async_copy(wd_in.at[:, gate], wd.at[:, gate], weight_sems.at[2, f]),
+        )
+
+    def order(number):
+        return nearby(place, cols - 1 - number)
+
+    for copy in token_copies(order(0)):
+        copy.start()
+    for f in range(tiles):
+        for copy in weight_copies(f):
+            copy.start()
+    for number in range(1, cols):
+        for copy in token_copies(order(number)):
+            copy.start()
     place.greet(False, True)
-    rows = out.shape[0]
-    line = LineSum(
-        place, lambda j: terms.at[pl.ds(pl.multiple_of(j * rows, rows), rows)], held, sends, recvs
-    )
-    for distance in range(place.cols - 1, 0, -1):
-        for way in (0, 1):
-            line.step(way, distance)
-    line.last(out)
+
+    def out_copy(slot, j):
+        return pltpu.make_async_copy(staged.at[slot], y_out.at[j], y_sems.at[slot])
+
+    for number in range(cols):
+        j = order(number)
+        for copy in token_copies(j):
+            copy.wait()
+
+        def hidden_tile(f, carry):
+            if number == 0:
+                for copy in weight_copies(f):
+                    copy.wait()
+            gate_at, up_at = part(f), part(f, hidden)
+            gate = matmul(hn[j], wh[:, gate_at])
+            up = matmul(hn[j], wh[:, up_at])
+            back = matmul(dy[j], wd[:, gate_at])
+            sigmoid = jax.nn.sigmoid(gate)
+            silu = gate * sigmoid
+            act[j, :, gate_at] = (silu * up).astype(bf16)
+            dgu[j, :, gate_at] = (back * up * sigmoid * (1.0 + gate * (1.0 - sigmoid))).astype(bf16)
+            dgu[j, :, up_at] = (back * silu).astype(bf16)
+            return carry
+
+        lax.fori_loop(0, tiles, hidden_tile, 0)
+
+        def grad_tile(n, carry):
+            at = pl.ds(pl.multiple_of(n * wide, wide), wide)
+            terms[j, :, at] = against(dgu[j], wh[at]).astype(bf16)
+            return carry
+
+        lax.fori_loop(0, wides, grad_tile, 0)
+        line.early(j, True)
+        slot = number % 2
+        if number >= 2:
+            out_copy(slot, order(number - 2)).wait()
+
+        def y_tile(n, carry):
+            at = pl.ds(pl.multiple_of(n * wide, wide), wide)
+            staged[slot, :, at] = against(act[j], wd[at]).astype(bf16)
+            return carry
+
+        lax.fori_loop(0, wides, y_tile, 0)
+        out_copy(slot, j).start()
+        if number >= 2:
+            line.late(order(number - 2), True)
+
+    rest = [number for number in range(max(cols - 2, 0), cols - 1)]
+    strips = width // 256
+    calls = [functools.partial(line.late, order(number), True) for number in rest]
+
+    def flat(ref):
+        return ref[...].reshape(cols * tokens, ref.shape[2])
+
+    def weight_strip(left, right, store, target, sem, at):
+        columns = jnp.concatenate([left[j, :, at] for j in range(cols)], axis=0)
+        store[at] = dot_tokens(columns, flat(right)).astype(bf16)
+        pltpu.make_async_copy(store.at[at], target.at[at], sem).start()
+
+    def down_strip(n, carry):
+        at = pl.ds(pl.multiple_of(n * 256, 256), 256)
+        weight_strip(dy, act, wd, dwd_out, dw_sems.at[0, n], at)
+        return carry
+
+    def hidden_strip(n, carry):
+        at = pl.ds(pl.multiple_of(n * 256, 256), 256)
+        weight_strip(hn, dgu, wh, dwh_out, dw_sems.at[1, n], at)
+        return carry
+
+    pieces = [(down_strip, 0, strips // 2), (down_strip, strips // 2, strips)]
+    pieces += [(hidden_strip, n, n + 2) for n in range(0, strips, 2)]
+    for body, begin, end in pieces:
+        lax.fori_loop(begin, end, body, 0)
+        if calls:
+            calls.pop(0)()
+    for call in calls:
+        call()
+    line.last(grad_out)
+    for number in range(max(cols - 2, 0), cols):
+        out_copy(number % 2, order(number)).wait()
+
+    def finish(n, carry):
+        at = pl.ds(pl.multiple_of(n * 256, 256), 256)
+        pltpu.make_async_copy(wd.at[at], dwd_out.at[at], dw_sems.at[0, n]).wait()
+        pltpu.make_async_copy(wh.at[at], dwh_out.at[at], dw_sems.at[1, n]).wait()
+        return carry
+
+    lax.fori_loop(0, strips, finish, 0)
     line.finish()
 
 
-def line_sum(terms, row_count, col_count, collective_id):
+def mlp(hn, dy, wh, wd, row_count, col_count, collective_id):
     steps = max(col_count - 1, 1)
-    rows, width = terms.shape[0] // col_count, terms.shape[1]
-    return pl.pallas_call(
-        functools.partial(line_sum_kernel, (row_count, col_count)),
-        out_shape=jax.ShapeDtypeStruct((rows, width), f32),
-        in_specs=[pl.BlockSpec(memory_space=pltpu.VMEM)],
-        out_specs=pl.BlockSpec(memory_space=pltpu.VMEM),
+    rows, width = hn.shape[0] // col_count, hn.shape[1]
+    hidden = wd.shape[1]
+    tile = min(512, hidden)
+    wide = min(512, width)
+    shape = (col_count, rows, width)
+    vmem = pl.BlockSpec(memory_space=pltpu.VMEM)
+    total = col_count * rows
+    grad, y, dwh, dwd = pl.pallas_call(
+        functools.partial(mlp_kernel, (row_count, col_count), tile, wide),
+        out_shape=[
+            jax.ShapeDtypeStruct((rows, width), f32),
+            jax.ShapeDtypeStruct(shape, bf16),
+            jax.ShapeDtypeStruct(wh.shape, bf16),
+            jax.ShapeDtypeStruct(wd.shape, bf16),
+        ],
+        in_specs=[ANY] * 4,
+        out_specs=[vmem, ANY, ANY, ANY],
         scratch_shapes=[
+            pltpu.VMEM(shape, bf16),
+            pltpu.VMEM(shape, bf16),
+            pltpu.VMEM(wh.shape, bf16),
+            pltpu.VMEM(wd.shape, bf16),
+            pltpu.VMEM((col_count, rows, hidden), bf16),
+            pltpu.VMEM((col_count, rows, 2 * hidden), bf16),
+            pltpu.VMEM(shape, bf16),
+            pltpu.VMEM((2, rows, width), bf16),
             pltpu.VMEM((2, steps, rows, width), bf16),
+            pltpu.SemaphoreType.DMA((2, col_count)),
+            pltpu.SemaphoreType.DMA((3, hidden // tile)),
+            pltpu.SemaphoreType.DMA((2,)),
+            pltpu.SemaphoreType.DMA((2, width // 256)),
             pltpu.SemaphoreType.DMA((2, steps)),
             pltpu.SemaphoreType.DMA((2, steps)),
         ],
         compiler_params=pltpu.CompilerParams(
-            collective_id=collective_id, has_side_effects=True, vmem_limit_bytes=48 << 20
+            collective_id=collective_id, has_side_effects=True, vmem_limit_bytes=63 << 20
         ),
         cost_estimate=pl.CostEstimate(
-            flops=terms.size, bytes_accessed=terms.size * 2, transcendentals=0
+            flops=2 * 9 * total * width * hidden,
+            bytes_accessed=(wh.size + wd.size) * 4,
+            transcendentals=total * hidden,
         ),
-        name="sum_line",
-    )(terms)
+        name="feed_forward",
+    )(hn.reshape(shape), dy.reshape(shape), wh, wd)
+    return grad, y.reshape(total, width), dwh, dwd
 
 
 class PlaneSum:
@@ -697,8 +881,7 @@
     core = place.at[2]
     token_rows = act_out.shape[0]
 
-    slots = [(way, step) for step in range(col_count - 1, 0, -1) for way in (0, 1)] + [(0, 0)]
-    entries = [(way, step, n) for way, step in slots for n in range(count)]
+    entries = [(n, nearby(place, k)) for k in range(col_count - 1, -1, -1) for n in range(count)]
 
     acts = LineSum(
         place,
@@ -719,12 +902,6 @@
         for n in range(count)
     ]
 
-    def at_entry(entry):
-        way, step, n = entry
-        if step == 0:
-            return None, place.col
-        return lines[n].target(way, step)
-
     def load(n, col):
         return pltpu.make_async_copy(
             terms[n].at[col, :, core], acc[n].at[col], load_sems.at[n, col]
@@ -749,19 +926,15 @@
             (ps.at[n, col], pr.at[n, col]),
         )
 
-    for entry in entries:
-        condition, col = at_entry(entry)
-        n = entry[2]
-        when(condition, lambda: load(n, col).start())
+    for n, col in entries:
+        load(n, col).start()
     place.greet(True, True)
     if cores > 1:
-        for entry in entries:
-            condition, col = at_entry(entry)
-            n = entry[2]
-            when(condition, lambda: share(n, col).start())
-    for way in (0, 1):
-        if col_count > 1:
-            acts.step(way, col_count - 1)
+        for n, col in entries:
+            share(n, col).start()
+    act_order = [nearby(place, k) for k in range(col_count - 1, 0, -1)]
+    for col in act_order:
+        acts.early(col, True)
     smalls = SmallSum(place, small, small_out, ring_held, line_held, ring_sems, line_sems)
     smalls.begin()
     stages = list(smalls.stages)
@@ -774,46 +947,41 @@
                 add_rows(acc[n].at[col, chip], per[n][1].at[col, chip])
         inside(n, col).first()
 
+    parts = [inside(n, col) for n, col in entries]
+    final = len(entries) - count
     for number in range(len(entries) + 2):
         if number < len(entries):
-            condition, col = at_entry(entries[number])
-            n = entries[number][2]
-            when(condition, lambda: start(n, col))
+            start(*entries[number])
         if 1 <= number <= len(entries):
-            condition, col = at_entry(entries[number - 1])
-            n = entries[number - 1][2]
-            when(condition, lambda: inside(n, col).second())
+            parts[number - 1].second()
         if 2 <= number:
-            way, step, n = entries[number - 2]
-            condition, col = at_entry(entries[number - 2])
-            when(condition, lambda: inside(n, col).third())
-            if step > 0:
-                lines[n].step(way, step)
-            else:
-                lines[n].last(per[n][5])
-                pltpu.make_async_copy(per[n][5], outs[n], load_sems.at[n, place.col]).start()
-        if number < len(entries):
-            way, step, n = entries[number]
-            if 1 < step and way == 1 and n == count - 1:
-                for other in (0, 1):
-                    acts.step(other, step - 1)
+            parts[number - 2].third()
+            n, col = entries[number - 2]
+            if number - 2 < final:
+                lines[n].early(col, True)
+                if number - 2 >= count:
+                    lines[n].late(entries[number - 2 - count][1], True)
+        if act_order and number % 2 == 1:
+            acts.late(act_order.pop(0), True)
         if stages:
             stages.pop(0)()
     for stage in stages:
         stage()
+    for col in act_order:
+        acts.late(col, True)
+    if col_count > 1:
+        for n in range(count):
+            lines[n].late(entries[final - count][1], True)
+    for n in range(count):
+        lines[n].last(per[n][5])
+        pltpu.make_async_copy(per[n][5], outs[n], load_sems.at[n, place.col]).start()
     acts.last(act_out)
     for n in range(count):
         pltpu.make_async_copy(per[n][5], outs[n], load_sems.at[n, place.col]).wait()
-    for entry in entries:
-        condition, col = at_entry(entry)
-        n = entry[2]
-
-        def done():
-            if cores > 1:
-                share(n, col).wait_send()
-            inside(n, col).finish()
-
-        when(condition, done)
+    for number, (n, col) in enumerate(entries):
+        if cores > 1:
+            share(n, col).wait_send()
+        parts[number].finish()
     for line in lines + [acts]:
         line.finish()
 
@@ -980,18 +1148,17 @@
     gain_first = attn_gain.astype(f32)
     gain_second = mlp_gain.astype(f32)
 
-    rows_grad = lax.all_gather(out_grad, "col", axis=0, tiled=True)
-
     first_weight = jnp.concatenate(
         [query_weight, keyvalue_weight.reshape(deep, pairs * 2 * HD)], axis=1
     )
-    full_first, full_output = gather_all([first_weight, output_weight], row_count, col_count)
-
-    hidden_flat, down_flat, full_first = lax.optimization_barrier(
-        (hidden_weight.reshape(deep, 2 * hidden), down_weight, full_first)
+    full_first, full_output, full_down, rows_grad = gather_all(
+        [first_weight, output_weight], [down_weight], out_grad, row_count, col_count
+    )
+
+    hidden_flat, full_first = lax.optimization_barrier(
+        (hidden_weight.reshape(deep, 2 * hidden), full_first)
     )
     full_hidden = lax.all_gather(hidden_flat, "row", axis=0, tiled=True)
-    full_down = lax.all_gather(down_flat, "row", axis=0, tiled=True)
 
     inputs = tokens.astype(f32)
     normal_in, scale_in = normalize(inputs, gain_first)
@@ -1029,22 +1196,9 @@
     normal_mid, scale_mid = normalize(hidden_in, gain_second)
 
     rows_mid = line_gather(normal_mid, row_count, col_count, 2)
-    gate_up = matmul(rows_mid, full_hidden)
-    gate_part = gate_up[:, :hidden]
-    up_part = gate_up[:, hidden:]
-    sigmoid_gate = jax.nn.sigmoid(gate_part)
-    silu_gate = gate_part * sigmoid_gate
-    gated_act = (silu_gate * up_part).astype(bf16)
-    grad_gated = matmul(rows_grad, full_down)
-    grad_gate = grad_gated * up_part * sigmoid_gate * (1.0 + gate_part * (1.0 - sigmoid_gate))
-    grad_up = grad_gated * silu_gate
-    grad_gate_up = jnp.concatenate([grad_gate, grad_up], axis=1).astype(bf16)
-    grad_mid = line_sum(
-        against(grad_gate_up, full_hidden).astype(bf16), row_count, col_count, 3
-    )
-    out_terms = against(gated_act, full_down).astype(bf16)
-    grad_down_part = over_rows(rows_grad, gated_act).astype(bf16)
-    grad_hidden_part = over_rows(rows_mid, grad_gate_up).astype(bf16)
+    grad_mid, out_terms, grad_hidden_part, grad_down_part = mlp(
+        rows_mid, rows_grad, full_hidden, full_down, row_count, col_count, 3
+    )
     sum_hidden = lax.psum_scatter(grad_hidden_part, "row", scatter_dimension=0, tiled=True)
     sum_down = lax.psum_scatter(grad_down_part, "row", scatter_dimension=0, tiled=True)
 

time: 870 us -> 743 us (0.85)
  matrix products: 229 us -> 106 us
  Pallas kernels: 476 us -> 486 us
    pallas_call x1, Pallas kernels: 138 us -> 72.9 us  [line_gather(): pl.pallas_call(functools.partial(line_gather_kernel, (row_count, col_coun...]
    dot_general x10 -> x8, matrix products: 70.3 us -> 21.2 us  [matmul(): return jnp.dot(left, right, preferred_element_type=f32)]
    dot_general x10 -> x8, matrix products: 45.6 us -> 7.65 us  [over_rows(): lax.dot_general(left, right, (((0,), (0,)), ((), ())), preferred_element_...]
    pallas_call x1, Pallas kernels: 133 us -> 171 us  [sum_all(): pl.pallas_call(functools.partial(sum_kernel, (row_count, col_count), coun...]
    dot_general x10 -> x8, matrix products: 49.9 us -> 16 us  [against(): lax.dot_general(left, right, (((1,), (1,)), ((), ())), preferred_element_...]
    pallas_call x1, Pallas kernels: 77 us -> 102 us  [mlp(): pl.pallas_call(functools.partial(mlp_kernel, (row_count, col_count), tile...]
    pallas_call x1, Pallas kernels: 128 us -> 140 us  [gather_all(): pl.pallas_call(functools.partial(gather_kernel, (row_count, col_count), c...]
    all_gather x2 -> x0, waiting for transfers between devices: 9.23 us -> none  [the longest x1 9.23 us: shards(): full_down = lax.all_gather(down_flat, 'row', axis=0, tiled=True)]
  transfers between devices with their start and end apart: 9 -> 7, of which waited for: 4 -> 4; matrix products, arithmetic and copies ran while one was open for 30% -> 23% of each run, Pallas kernels for 41% -> 33%
where the time goes in v3:
time: 743 us; the launch traced here: 736 us
  Pallas kernels  486 us (65%)
  matrix products  106 us (14%)
  other arithmetic  53.3 us (7%)
  waiting for transfers between devices  33.8 us (5%)
  local copies, waits for them, and re-layouts  30.2 us (4%)
  between operations  15 us (2%)
  starting transfers between devices  11.1 us (1%)
    pallas_call x1, Pallas kernels, sum_all(): pl.pallas_call(functools.partial(sum_kernel, (row_count, col_count), coun...  171 us
    pallas_call x1, Pallas kernels, gather_all(): pl.pallas_call(functools.partial(gather_kernel, (row_count, col_count), c...  140 us
    pallas_call x1, Pallas kernels, mlp(): pl.pallas_call(functools.partial(mlp_kernel, (row_count, col_count), tile...  102 us
    pallas_call x1, Pallas kernels, line_gather(): pl.pallas_call(functools.partial(line_gather_kernel, (row_count, col_coun...  72.9 us
    ppermute x4, waiting for transfers between devices, shift(): return lax.ppermute(values, 'col', pairs)  33.3 us
    dot_general x8, matrix products, matmul(): return jnp.dot(left, right, preferred_element_type=f32)  21.2 us
    convert_element_type x1, other arithmetic, shards(): grad_score = (chances * (grad_chance - centre)).astype(bf16)  17.7 us
    dot_general x1, matrix products, shards(): jnp.einsum('ztkgd,zskd->zkgts', grad_mixed, values, preferred_element_typ...  17.6 us
  transfers between devices with their start and end apart: 7, of which 4 were waited for; matrix products, arithmetic and copies ran while one was open for 23% of the time, Pallas kernels for 33%

profile of v3, /device:TPU:0, one launch (start us, length us, event | category | flops | bytes accessed | tf_op | source)
XLA Modules:
  0.0 735.6 jit_solution(3318524675073878742)
XLA Ops:
  8.2 3.8 copy.72
  12.8 140.3 %gather_weights.1 = (bf16[4,2048,768]{2,1,0:T(8,128)(2,1)}, bf16[4,2048,512]{2,1,0:T(8,128)(2,1)}, bf16[2048,2048]{1,0:T(8,128)(2,1)}, bf16[1024,2048]{1,0:T(8,128)(2,1)}) custom-call(bf16[256,768]{1,0:T(8,128)(2,1)} %pad_maximum_fusion.13.refs_0_, bf16[256,512]{1,0:T(8,128)(2,1)} %refs_1_.1, bf16[256,2048]{1,0:T(8,128)(2,1)} %refs_2_.1, ...), custom_call_target="tpu_custom_call" | custom-call | bytes 20971520 | tf_op jit(solution)/shard_map/gather_weights/pallas_call | solution.py:362
  154.3 3.1 fusion.97
  157.4 4.7 fusion.94
  171.6 9.8 %collective-permute-done = bf16[4,256,2,2,64]{1,4,2,0,3:T(8,128)(2,1)} collective-permute-done((bf16[4,256,2,2,64]{1,4,2,0,3:T(8,128)(2,1)}, bf16[4,256,2,2,64]{1,4,2,0,3:T(8,128)(2,1)}, u32[]{:S(2)}, u32[]{:S(2)}) %collective-permute-start) | collective-permute-done | bytes 524320 | tf_op jit(solution)/shard_map/ppermute | solution.py:1104
  181.4 5.5 collective-permute-start.1
  189.8 2.7 subtract_convert_fusion.1
  192.5 4.8 collective-permute-done.1
  198.7 14.2 %fusion.154 = (f32[4,2,4,256]{3,2,1,0:T(4,128)S(1)}, f32[4,2,4,256,768]{3,4,2,1,0:T(8,128)}) fusion(pred[256,768]{0,1:T(8,128)(4,1)} %fusion.118, bf16[4,768,2,2,64]{1,4,2,0,3:T(8,128)(2,1)S(1)} %maximum_maximum_fusion, bf16[4,256,2,4,32]{1,4,3,2,0:T(8,128)(2,1)} %bitcast.267, bf16[4,256,2,4,32]{1,4,3,2,0:T(8,128)(2,1)S(1)} %bitcast.265), kind=kOutput, calls=%fused_computation.202 | convolution fusion | flops 832570112 | bytes 27230208 | tf_op jit(solution)/shard_map/sub | solution.py:1185
  212.9 9.9 %fusion.85 = bf16[4,256,2,4,64]{1,4,3,2,0:T(8,128)(2,1)S(1)} fusion(bf16[4,768,2,2,64]{1,4,2,0,3:T(8,128)(2,1)S(1)} %maximum_maximum_fusion, f32[4,2,4,256,768]{3,4,2,1,0:T(8,128)} %get-tuple-element.67, f32[4,2,4,256]{3,2,1,0:T(4,128)S(1)} %get-tuple-element.66), kind=kOutput, calls=%fused_computation.120 | convolution fusion | flops 818413568 | bytes 27033600 | tf_op jit(solution)/shard_map/zkgts,zskd->ztkgd/dot_general | solution.py:1190
  222.9 2.8 fusion.68
  228.1 2.4 convolution_add_fusion.1
  230.5 2.5 multiply_reduce_fusion.2
  235.6 72.9 %gather_line.1 = bf16[1024,2048]{1,0:T(8,128)(2,1)} custom-call(bf16[256,2048]{1,0:T(8,128)(2,1)} %multiply_convert_fusion.own), custom_call_target="tpu_custom_call" | custom-call | bytes 4194304 | tf_op jit(solution)/shard_map/gather_line/pallas_call | solution.py:405
  308.5 101.9 %feed_forward.1 = (f32[256,2048]{1,0:T(8,128)}, bf16[4,256,2048]{2,1,0:T(8,128)(2,1)}, bf16[2048,4096]{1,0:T(8,128)(2,1)}, bf16[2048,2048]{1,0:T(8,128)(2,1)}) custom-call(bf16[4,256,2048]{2,1,0:T(8,128)(2,1)} %bitcast.251, bf16[4,256,2048]{2,1,0:T(8,128)(2,1)} %bitcast.284, bf16[2048,4096]{1,0:T(8,128)(2,1)} %all-gather.2.cloned.1.call-done.refs_2_, ...), custom_call_target="tpu_custom_call" | custom-call | flops 77309411328 | bytes 50331648 | tf_op jit(solution)/shard_map/feed_forward/pallas_call | solution.py:658
  416.8 2.7 fusion.109
  422.0 2.8 fusion.100
  425.0 3.6 fusion.103
  429.8 17.6 %fusion.1 = (f32[4,2,4,256]{3,2,1,0:T(4,128)S(1)}, f32[4,2,768,256,4]{3,2,4,1,0:T(8,128)}) fusion(f32[4,2,4,256,768]{3,4,2,1,0:T(8,128)} %get-tuple-element.67, f32[4,2,4,256]{3,2,1,0:T(4,128)S(1)} %get-tuple-element.66, bf16[1,256,2,4,64]{1,4,3,2,0:T(8,128)(2,1)S(1)} %bitcast.270, bf16[1,256,2,4,64]{1,4,3,2,0:T(8,128)(2,1)S(1)} %bitcast.272, ...), kind=kOutput, calls=%fused_computation.3 | convolution fusion | flops 828366848 | bytes 52232192 | tf_op jit(solution)/shard_map/ztkgd,zskd->zkgts/dot_general | solution.py:1215
  447.5 17.7 %fusion.3 = bf16[4,2,4,256,768]{3,4,2,1,0:T(8,128)(2,1)S(1)} fusion(f32[4,2,768,256,4]{3,2,4,1,0:T(8,128)} %get-tuple-element.71, f32[4,2,4,256]{3,2,1,0:T(4,128)S(1)} %get-tuple-element.70, f32[4,2,4,256,768]{3,4,2,1,0:T(8,128)} %get-tuple-element.67, f32[4,2,4,256]{3,2,1,0:T(4,128)S(1)} %get-tuple-element.66), kind=kLoop, calls=%fused_computation.5 | loop fusion | flops 25165824 | bytes 62980096 | tf_op jit(solution)/shard_map/convert_element_type | solution.py:1217
  465.2 4.6 copy-done
  469.8 6.3 fusion.78
  476.1 10.8 %fusion.79 = f32[4,768,2,1,64]{1,4,2,0,3:T(8,128)S(1)} fusion(bf16[1,256,2,4,64]{1,4,3,2,0:T(8,128)(2,1)S(1)} %bitcast.271, bf16[1,256,2,4,64]{1,4,3,2,0:T(8,128)(2,1)} %bitcast.273, bf16[1,256,2,4,64]{1,4,3,2,0:T(8,128)(2,1)} %bitcast.277, bf16[1,256,2,4,64]{1,4,3,2,0:T(8,128)(2,1)} %bitcast.275, f32[4,2,4,256,768]{3,4,2,1,0:T(8,128)} %get-tuple-element.67, ...), kind=kOutput, calls=%fused_computation.118 | convolution fusion | flops 819462144 | bytes 27820032 | tf_op jit(solution)/shard_map/zkgts,ztkgd->zskd/dot_general | solution.py:1224
  491.9 4.4 pad_maximum_fusion.1.refs_1_
  496.3 5.8 collective-permute-done.2
  507.0 12.9 %collective-permute-done.3 = bf16[4,256,2,2,64]{1,4,2,0,3:T(8,128)(2,1)S(1)} collective-permute-done((bf16[4,256,2,2,64]{1,4,2,0,3:T(8,128)(2,1)S(1)}, bf16[4,256,2,2,64]{1,4,2,0,3:T(8,128)(2,1)S(1)}, u32[]{:S(2)}, u32[]{:S(2)}) %collective-permute-start.3) | collective-permute-done | bytes 524320 | tf_op jit(solution)/shard_map/ppermute | solution.py:1104
  523.8 2.8 fusion.56
  531.8 5.9 pad_maximum_fusion.refs_0_
  537.7 171.2 %sum_weights.1 = (f32[256,768]{1,0:T(8,128)}, f32[256,512]{1,0:T(8,128)}, f32[256,2048]{1,0:T(8,128)}, f32[32,128]{1,0:T(8,128)}) custom-call(bf16[4,4,2,256,768]{4,3,2,1,0:T(8,128)(2,1)} %pad_maximum_fusion.refs_0_, bf16[4,4,2,256,512]{4,3,2,1,0:T(8,128)(2,1)} %pad_maximum_fusion.1.refs_1_, bf16[1024,2048]{1,0:T(8,128)(2,1)} %bitcast.255, ...), custom_call_target="tpu_custom_call" | custom-call | bytes 41943040 | tf_op jit(solution)/shard_map/sum_weights/pallas_call | solution.py:1025
  714.1 3.0 add_convert_fusion
  718.7 2.8 convert_element_type.129
  721.5 6.6 reshape.291
  (189 shorter events, 58.0 us)
Async XLA Ops:
  7.2 301.3 %all-gather.2.cloned.1.call-start = ((), (), s32[]{:S(2)}) async-start(), calls=%async_computation.2 | async-start | bytes 18874368 | tf_op jit(solution)/shard_map/all_gather | solution.py:1161
  12.8 140.4 %copy-start.46 = (s32[1,3]{1,0:T(1,128)S(1)}, s32[1,3]{1,0:T(1,128)}, u32[]{:S(2)}) copy-start(s32[1,3]{1,0:T(1,128)} %param.11) | copy-start | bytes 40
  12.8 140.6 %copy-start.44 = (bf16[2048]{0:T(1024)(128)(2,1)S(1)}, bf16[2048]{0:T(1024)(128)(2,1)}, u32[]{:S(2)}) copy-start(bf16[2048]{0:T(1024)(128)(2,1)} %param.12) | copy-start | bytes 12292
  12.8 140.6 %copy-start.4 = (bf16[256,2048]{1,0:T(8,128)(2,1)S(1)}, bf16[256,2048]{1,0:T(8,128)(2,1)}, u32[]{:S(2)}) copy-start(bf16[256,2048]{1,0:T(8,128)(2,1)} %param.10) | copy-start | bytes 3145732
  153.1 565.5 %reduce-scatter.5.cloned.1.call-start = ((), (), s32[]{:S(2)}) async-start(), calls=%async_computation.4 | async-start | bytes 9437184 | tf_op jit(solution)/shard_map/reduce_scatter | solution.py:1203
  153.4 9.9 %copy-start.34 = (f32[2048]{0:T(1024)}, f32[2048]{0:T(1024)S(1)}, u32[]{:S(2)}) copy-start(f32[2048]{0:T(1024)S(1)} %convert_element_type.100) | copy-start | bytes 24580
  154.3 9.0 %copy-start.41 = (f32[256]{0:T(256)}, f32[256]{0:T(256)S(1)}, u32[]{:S(2)}) copy-start(f32[256]{0:T(256)S(1)} %get-tuple-element.63) | copy-start | bytes 3076
  154.3 8.0 %copy-start.11 = (bf16[4,2048,768]{2,1,0:T(8,128)(2,1)S(1)}, bf16[4,2048,768]{2,1,0:T(8,128)(2,1)}, u32[]{:S(2)}) copy-start(bf16[4,2048,768]{2,1,0:T(8,128)(2,1)} %get-tuple-element.24) | copy-start | bytes 37748740
  157.4 7.1 copy-start.17
  166.8 23.0 %copy-start.31 = (f32[256,32]{0,1:T(8,128)}, f32[256,32]{0,1:T(8,128)S(1)}, u32[]{:S(2)}) copy-start(f32[256,32]{0,1:T(8,128)S(1)} %get-tuple-element.61) | copy-start | bytes 98308
  167.8 13.6 %collective-permute-start = (bf16[4,256,2,2,64]{1,4,2,0,3:T(8,128)(2,1)}, bf16[4,256,2,2,64]{1,4,2,0,3:T(8,128)(2,1)}, u32[]{:S(2)}, u32[]{:S(2)}) collective-permute-start(bf16[4,256,2,2,64]{1,4,2,0,3:T(8,128)(2,1)} %pad_maximum_fusion.10), channel_id=1, source_target_pairs={{0,1},{1,2},{2,3},{4,5},{5,6},{6,7},{8,9},{9,10},{10,11},{12,13},{... | collective-permute-start | bytes 1572872 | tf_op jit(solution)/shard_map/ppermute | solution.py:1104
  169.9 17.1 %copy-start.45 = (bf16[2048]{0:T(1024)(128)(2,1)S(1)}, bf16[2048]{0:T(1024)(128)(2,1)}, u32[]{:S(2)}) copy-start(bf16[2048]{0:T(1024)(128)(2,1)} %param.16) | copy-start | bytes 12292
  181.4 15.8 %collective-permute-start.1 = (bf16[4,256,2,2,64]{1,4,2,0,3:T(8,128)(2,1)}, bf16[4,256,2,2,64]{1,4,2,0,3:T(8,128)(2,1)}, u32[]{:S(2)}, u32[]{:S(2)}) collective-permute-start(bf16[4,256,2,2,64]{1,4,2,0,3:T(8,128)(2,1)} %collective-permute-done), channel_id=1, source_target_pairs={{0,1},{1,2},{2,3},{4,5},{5,6},{6,7},{8,9},{9,10},{10,11},{12,13},{... | collective-permute-start | bytes 1572872 | tf_op jit(solution)/shard_map/ppermute | solution.py:1104
  192.5 20.5 %copy-start.30 = (bf16[4,256,8,32]{1,3,2,0:T(8,128)(2,1)}, bf16[4,256,8,32]{1,3,2,0:T(8,128)(2,1)S(1)}, u32[]{:S(2)}) copy-start(bf16[4,256,8,32]{1,3,2,0:T(8,128)(2,1)S(1)} %get-tuple-element.47) | copy-start | bytes 1572868
  198.7 14.2 %copy-start.14 = (bf16[4,768,2,2,64]{1,4,2,0,3:T(8,128)(2,1)}, bf16[4,768,2,2,64]{1,4,2,0,3:T(8,128)(2,1)S(1)}, u32[]{:S(2)}) copy-start(bf16[4,768,2,2,64]{1,4,2,0,3:T(8,128)(2,1)S(1)} %maximum_maximum_fusion) | copy-start | bytes 4718596
  222.9 5.2 copy-start.25
  222.9 7.6 %copy-start.27 = (bf16[1,256,2,4,64]{1,4,3,2,0:T(8,128)(2,1)}, bf16[1,256,2,4,64]{1,4,3,2,0:T(8,128)(2,1)S(1)}, u32[]{:S(2)}) copy-start(bf16[1,256,2,4,64]{1,4,3,2,0:T(8,128)(2,1)S(1)} %get-tuple-element.49) | copy-start | bytes 786436
  410.4 311.0 %reduce-scatter.3.cloned.1.call-start = ((), (), s32[]{:S(2)}) async-start(), calls=%async_computation.3 | async-start | bytes 18874368 | tf_op jit(solution)/shard_map/reduce_scatter | solution.py:1202
  416.8 8.2 %copy-start.6 = (bf16[256,2048]{1,0:T(8,128)(2,1)}, bf16[256,2048]{1,0:T(8,128)(2,1)S(1)}, u32[]{:S(2)}) copy-start(bf16[256,2048]{1,0:T(8,128)(2,1)S(1)} %get-tuple-element.43) | copy-start | bytes 3145732
  422.0 7.8 %copy-start.38 = (bf16[256,512]{0,1:T(8,128)(2,1)}, bf16[256,512]{0,1:T(8,128)(2,1)S(1)}, u32[]{:S(2)}) copy-start(bf16[256,512]{0,1:T(8,128)(2,1)S(1)} %copy.56) | copy-start | bytes 786436
  429.8 17.7 %copy-start.40 = (bf16[256,512]{0,1:T(8,128)(2,1)}, bf16[256,512]{0,1:T(8,128)(2,1)S(1)}, u32[]{:S(2)}) copy-start(bf16[256,512]{0,1:T(8,128)(2,1)S(1)} %copy.55) | copy-start | bytes 786436
  476.1 10.8 %copy-start.8 = (f32[4,768,2,1,64]{1,4,2,0,3:T(8,128)S(1)}, f32[4,768,2,1,64]{1,4,2,0,3:T(8,128)}, u32[]{:S(2)}) copy-start(f32[4,768,2,1,64]{1,4,2,0,3:T(8,128)} %fusion.78) | copy-start | bytes 4718596
  487.0 15.2 %collective-permute-start.2 = (bf16[4,256,2,2,64]{1,4,2,0,3:T(8,128)(2,1)S(1)}, bf16[4,256,2,2,64]{1,4,2,0,3:T(8,128)(2,1)S(1)}, u32[]{:S(2)}, u32[]{:S(2)}) collective-permute-start(bf16[4,256,2,2,64]{1,4,2,0,3:T(8,128)(2,1)S(1)} %fusion.117), channel_id=1, source_target_pairs={{1,0},{2,1},{3,2},{5,4},{6,5},{7,6},{9,8},{10,9},{11,10},{13,12},{... | collective-permute-start | bytes 1572872 | tf_op jit(solution)/shard_map/ppermute | solution.py:1104
  491.1 13.1 %slice-start = ((s8[12582912]{0:T(1024)(128)(4,1)}), s8[4194304]{0:T(1024)(128)(4,1)S(1)}, s32[]{:S(2)}) async-start(s8[12582912]{0:T(1024)(128)(4,1)} %bitcast.222), calls=%async_computation.5 | async-start | bytes 8388608
  491.9 12.3 %slice-start.1 = ((s8[12582912]{0:T(1024)(128)(4,1)}), s8[4194304]{0:T(1024)(128)(4,1)S(1)}, s32[]{:S(2)}) async-start(s8[12582912]{0:T(1024)(128)(4,1)} %bitcast.222), calls=%async_computation.6 | async-start | bytes 8388608
  491.9 12.3 %slice-start.2 = ((s8[12582912]{0:T(1024)(128)(4,1)}), s8[4194304]{0:T(1024)(128)(4,1)S(1)}, s32[]{:S(2)}) async-start(s8[12582912]{0:T(1024)(128)(4,1)} %bitcast.222), calls=%async_computation.7 | async-start | bytes 8388608
  496.3 7.9 %copy-start.16 = (bf16[4,768,2,2,64]{1,4,2,0,3:T(8,128)(2,1)S(1)}, bf16[4,768,2,2,64]{1,4,2,0,3:T(8,128)(2,1)}, u32[]{:S(2)}) copy-start(bf16[4,768,2,2,64]{1,4,2,0,3:T(8,128)(2,1)} %copy-done.14) | copy-start | bytes 4718596
  502.4 17.6 %collective-permute-start.3 = (bf16[4,256,2,2,64]{1,4,2,0,3:T(8,128)(2,1)S(1)}, bf16[4,256,2,2,64]{1,4,2,0,3:T(8,128)(2,1)S(1)}, u32[]{:S(2)}, u32[]{:S(2)}) collective-permute-start(bf16[4,256,2,2,64]{1,4,2,0,3:T(8,128)(2,1)S(1)} %fusion.114), channel_id=1, source_target_pairs={{1,0},{2,1},{3,2},{5,4},{6,5},{7,6},{9,8},{10,9},{11,10},{13,12},{... | collective-permute-start | bytes 1572872 | tf_op jit(solution)/shard_map/ppermute | solution.py:1104
  504.3 16.2 %slice-start.3 = ((s8[12582912]{0:T(1024)(128)(4,1)}), s8[4194304]{0:T(1024)(128)(4,1)S(1)}, s32[]{:S(2)}) async-start(s8[12582912]{0:T(1024)(128)(4,1)} %bitcast.249), calls=%async_computation.8 | async-start | bytes 8388608
  504.3 16.2 %slice-start.4 = ((s8[12582912]{0:T(1024)(128)(4,1)}), s8[4194304]{0:T(1024)(128)(4,1)S(1)}, s32[]{:S(2)}) async-start(s8[12582912]{0:T(1024)(128)(4,1)} %bitcast.249), calls=%async_computation.9 | async-start | bytes 8388608
  507.0 13.4 %slice-start.5 = ((s8[12582912]{0:T(1024)(128)(4,1)}), s8[4194304]{0:T(1024)(128)(4,1)S(1)}, s32[]{:S(2)}) async-start(s8[12582912]{0:T(1024)(128)(4,1)} %bitcast.249), calls=%async_computation.10 | async-start | bytes 8388608
  721.5 6.6 copy-start.33
  (28 other events, 73.1 us)
Sparse Core Ops, SparseCore 0:
  153.3 89.0 all-gather.1
  410.5 78.0 reduce-scatter.4
  492.6 168.8 reduce-scatter.2

commit v4 on v3

--- a/solution.py
+++ b/solution.py
@@ -82,8 +82,10 @@
 
 
 def when(condition, action):
-    if condition is None:
+    if condition is None or condition is True:
         action()
+    elif condition is False:
+        pass
     else:
         pl.when(condition)(action)
 
@@ -788,6 +790,118 @@
                 self.copy(half, 0, step, 0).wait_send()
 
 
+def core_rows(place, chip, step, deep):
+    cores = place.sizes[2]
+    row = chip * cores + lax.rem(place.at[2] + step, cores)
+    return pl.ds(pl.multiple_of(row * deep, deep), deep)
+
+
+class InnerSum:
+    def __init__(self, place, terms, out, chunk, refs):
+        self.place, self.terms, self.out, self.chunk = place, terms, out, chunk
+        self.acc, self.core_held, self.second, self.first, self.staged = refs[:5]
+        self.load_sems, self.core_sems, self.plane_sems, self.out_sems = refs[5:]
+        self.count = out.shape[1] // chunk
+        self.ahead = min(3, self.count)
+
+    @staticmethod
+    def scratch(sizes, deep, width, chunk):
+        na, nb, _ = sizes
+        count = width // chunk
+        firsts, seconds = PlaneSum.counts_of(sizes)
+        sems = (2, count, 2, max(PlaneSum.sem_count(sizes), 1))
+        return [
+            pltpu.VMEM((count, na * nb, deep, chunk), bf16),
+            pltpu.VMEM((count, na * nb, deep, chunk), bf16),
+            pltpu.VMEM((count, 2, max(seconds, 1), deep // 2, chunk), bf16),
+            pltpu.VMEM((count, 2, max(firsts, 1), deep // 2, chunk), bf16),
+            pltpu.VMEM((2, deep, chunk), f32),
+            pltpu.SemaphoreType.DMA((count,)),
+            pltpu.SemaphoreType.DMA((2, count)),
+            pltpu.SemaphoreType.DMA(sems),
+            pltpu.SemaphoreType.DMA((2,)),
+        ]
+
+    def columns(self, e):
+        return pl.ds(pl.multiple_of(e * self.chunk, self.chunk), self.chunk)
+
+    def load(self, e):
+        source = self.terms.at[:, self.place.at[2], :, self.columns(e)]
+        return pltpu.make_async_copy(source, self.acc.at[e], self.load_sems.at[e])
+
+    def share(self, e):
+        other = lax.rem(self.place.at[2] + 1, self.place.sizes[2])
+        return remote(
+            self.terms.at[:, other, :, self.columns(e)],
+            self.core_held.at[e],
+            self.core_sems.at[0, e],
+            self.core_sems.at[1, e],
+            self.place.device(2, 1),
+        )
+
+    def inside(self, e):
+        return PlaneSum(
+            self.place,
+            self.acc.at[e],
+            self.core_held.at[e],
+            self.second.at[e],
+            self.first.at[e],
+            (self.plane_sems.at[0, e], self.plane_sems.at[1, e]),
+        )
+
+    def out_copy(self, e):
+        slot = lax.rem(e, 2)
+        return pltpu.make_async_copy(
+            self.staged.at[slot], self.out.at[:, self.columns(e)], self.out_sems.at[slot]
+        )
+
+    def prepare(self, e):
+        self.load(e).start()
+        if self.place.sizes[2] > 1:
+            self.share(e).start()
+
+    def begin(self):
+        for e in range(self.ahead):
+            self.prepare(e)
+
+    def start(self, e):
+        when(e + self.ahead < self.count, lambda: self.prepare(e + self.ahead))
+        self.load(e).wait()
+        if self.place.sizes[2] > 1:
+            self.share(e).wait_recv()
+            for chip in range(self.acc.shape[1]):
+                add_rows(self.acc.at[e, chip], self.core_held.at[e, chip])
+        self.inside(e).first()
+
+    def middle(self, e):
+        self.inside(e).second()
+
+    def close(self, e):
+        self.inside(e).third()
+        when(e >= 2, lambda: self.out_copy(e - 2).wait())
+        slot = lax.rem(e, 2)
+        own = self.acc.at[e, self.place.chip_of(self.place.at)]
+        self.staged[slot] = own[...].astype(f32)
+        self.out_copy(e).start()
+
+    def tick(self, t):
+        when(t < self.count, lambda: self.start(t))
+        when((t >= 1) & (t - 1 < self.count), lambda: self.middle(t - 1))
+        when((t >= 2) & (t - 2 < self.count), lambda: self.close(t - 2))
+
+    def finish(self):
+        for e in range(max(self.count - 2, 0), self.count):
+            self.out_copy(e).wait()
+
+        def done(e, carry):
+            if self.place.sizes[2] > 1:
+                self.share(e).wait_send()
+            self.inside(e).finish()
+            return carry
+
+        lax.fori_loop(0, self.count, done, 0)
+
+
 class SmallSum:
     def __init__(self, place, own, total, ring_held, line_held, ring_sems, line_sems):
         self.place, self.own, self.total = place, own, total
@@ -866,19 +980,20 @@
         self.total[...] = total
 
 
-def sum_kernel(sizes, count, *refs):
+def sum_kernel(sizes, count, chunk, *refs):
     row_count, col_count = sizes
-    terms = refs[:count]
-    act_terms, small = refs[count : count + 2]
-    outs = refs[count + 2 : 2 * count + 2]
-    act_out, small_out = refs[2 * count + 2 : 2 * count + 4]
-    refs = refs[2 * count + 4 :]
-    per = [refs[6 * n : 6 * n + 6] for n in range(count)]
-    act_held, load_sems, cs, cr, ps, pr, zs, zr = refs[6 * count : 6 * count + 8]
-    ring_held, line_held, ring_sems, line_sems = refs[6 * count + 8 :]
     place = Place(row_count, col_count)
     cores = place.sizes[2]
-    core = place.at[2]
+    lefts, rights = refs[: cores * count], refs[cores * count : 2 * cores * count]
+    refs = refs[2 * cores * count :]
+    inner_terms, act_terms, small = refs[:3]
+    outs = refs[3 : 3 + count]
+    inner_out, act_out, small_out = refs[3 + count : 6 + count]
+    refs = refs[6 + count :]
+    per = [refs[7 * n : 7 * n + 7] for n in range(count)]
+    inner = InnerSum(place, inner_terms, inner_out, chunk, refs[7 * count : 7 * count + 9])
+    act_held, load_sems, out_sems, ps, pr, zs, zr = refs[7 * count + 9 : 7 * count + 16]
+    ring_held, line_held, ring_sems, line_sems, chip_sems = refs[7 * count + 16 :]
     token_rows = act_out.shape[0]
 
     entries = [(n, nearby(place, k)) for k in range(col_count - 1, -1, -1) for n in range(count)]
@@ -895,123 +1010,168 @@
         LineSum(
             place,
             lambda j, n=n: acc[n].at[j, place.chip_of(place.at)],
-            per[n][4],
+            per[n][3],
             zs.at[n],
             zr.at[n],
         )
         for n in range(count)
     ]
-
-    def load(n, col):
-        return pltpu.make_async_copy(
-            terms[n].at[col, :, core], acc[n].at[col], load_sems.at[n, col]
-        )
-
-    def share(n, col):
-        return remote(
-            terms[n].at[col, :, lax.rem(core + 1, cores)],
-            per[n][1].at[col],
-            cs.at[n, col],
-            cr.at[n, col],
-            place.device(2, 1),
-        )
+    tokens = lefts[0].shape[0]
+    chips, deep = acc[0].shape[1:3]
+
+    def loads():
+        for n in range(count):
+            left, right = per[n][5], per[n][6]
+            for k in range(cores):
+                at = pl.ds(k * tokens, tokens)
+                if k == 0:
+                    for chip in range(chips):
+                        yield pltpu.make_async_copy(
+                            lefts[n * cores].at[:, core_rows(place, chip, 0, deep)],
+                            left.at[at, pl.ds(chip * deep, deep)],
+                            chip_sems.at[n, chip],
+                        )
+                else:
+                    yield pltpu.make_async_copy(
+                        lefts[n * cores + k], left.at[at], load_sems.at[0, n * cores + k]
+                    )
+                yield pltpu.make_async_copy(
+                    rights[n * cores + k], right.at[:, at], load_sems.at[1, n * cores + k]
+                )
+
+    for copy in loads():
+        copy.start()
+    place.greet(True, True)
+    inner.begin()
+    act_order = [nearby(place, k) for k in range(col_count - 1, 0, -1)]
+    act_early, act_late = list(act_order), list(act_order)
+    acts.early(act_early.pop(0), True) if act_early else None
+    smalls = SmallSum(place, small, small_out, ring_held, line_held, ring_sems, line_sems)
+    smalls.begin()
+    stages = list(smalls.stages)
+    for copy in loads():
+        copy.wait()
 
     def inside(n, col):
         return PlaneSum(
             place,
             acc[n].at[col],
+            None,
             per[n][1].at[col],
             per[n][2].at[col],
-            per[n][3].at[col],
             (ps.at[n, col], pr.at[n, col]),
         )
 
-    for n, col in entries:
-        load(n, col).start()
-    place.greet(True, True)
-    if cores > 1:
-        for n, col in entries:
-            share(n, col).start()
-    act_order = [nearby(place, k) for k in range(col_count - 1, 0, -1)]
-    for col in act_order:
-        acts.early(col, True)
-    smalls = SmallSum(place, small, small_out, ring_held, line_held, ring_sems, line_sems)
-    smalls.begin()
-    stages = list(smalls.stages)
-
-    def start(n, col):
-        load(n, col).wait()
-        if cores > 1:
-            share(n, col).wait_recv()
-            for chip in range(acc[n].shape[1]):
-                add_rows(acc[n].at[col, chip], per[n][1].at[col, chip])
-        inside(n, col).first()
-
     parts = [inside(n, col) for n, col in entries]
     final = len(entries) - count
-    for number in range(len(entries) + 2):
-        if number < len(entries):
-            start(*entries[number])
-        if 1 <= number <= len(entries):
-            parts[number - 1].second()
+    total = len(entries) + inner.count
+
+    def start(number):
+        if number >= len(entries):
+            inner.start(number - len(entries))
+            return
+        n, col = entries[number]
+        left, right = per[n][5], per[n][6]
+        deep = acc[n].shape[2]
+
+        def chip_rows(chip, carry):
+            at = pl.ds(pl.multiple_of(chip * deep, deep), deep)
+            acc[n][col, chip] = dot_tokens(left[:, at], right[col]).astype(bf16)
+            return carry
+
+        lax.fori_loop(0, acc[n].shape[1], chip_rows, 0)
+        parts[number].first()
+
+    def middle(number):
+        if number >= len(entries):
+            inner.middle(number - len(entries))
+        else:
+            parts[number].second()
+
+    def out_copy(n):
+        return pltpu.make_async_copy(per[n][4], outs[n], out_sems.at[n])
+
+    def close(number):
+        if number >= len(entries):
+            inner.close(number - len(entries))
+            if number == len(entries) + 1 or total == len(entries) + 1:
+                finish_lines()
+            return
+        parts[number].third()
+        n, col = entries[number]
+        if number < final:
+            lines[n].early(col, True)
+        if number >= 2 * count:
+            waiting.pop(0)()
+
+    waiting = [functools.partial(lines[n].late, col, True) for n, col in entries[:final]]
+
+    def finish_lines():
+        while waiting:
+            waiting.pop(0)()
+        for n in range(count):
+            lines[n].last(per[n][4])
+            out_copy(n).start()
+
+    for number in range(total + 2):
+        if number < total:
+            start(number)
+        if 1 <= number <= total:
+            middle(number - 1)
         if 2 <= number:
-            parts[number - 2].third()
-            n, col = entries[number - 2]
-            if number - 2 < final:
-                lines[n].early(col, True)
-                if number - 2 >= count:
-                    lines[n].late(entries[number - 2 - count][1], True)
-        if act_order and number % 2 == 1:
-            acts.late(act_order.pop(0), True)
+            close(number - 2)
+        if act_early and number % 2 == 1:
+            acts.early(act_early.pop(0), True)
+        if act_late and number >= 3 and number % 2 == 1:
+            acts.late(act_late.pop(0), True)
         if stages:
             stages.pop(0)()
     for stage in stages:
         stage()
-    for col in act_order:
+    for col in act_early:
+        acts.early(col, True)
+    for col in act_late:
         acts.late(col, True)
-    if col_count > 1:
-        for n in range(count):
-            lines[n].late(entries[final - count][1], True)
-    for n in range(count):
-        lines[n].last(per[n][5])
-        pltpu.make_async_copy(per[n][5], outs[n], load_sems.at[n, place.col]).start()
     acts.last(act_out)
     for n in range(count):
-        pltpu.make_async_copy(per[n][5], outs[n], load_sems.at[n, place.col]).wait()
-    for number, (n, col) in enumerate(entries):
-        if cores > 1:
-            share(n, col).wait_send()
-        parts[number].finish()
+        out_copy(n).wait()
+    for part in parts:
+        part.finish()
+    inner.finish()
     for line in lines + [acts]:
         line.finish()
 
 
-def sum_all(terms, act_terms, small, row_count, col_count, act_type):
-    count = len(terms)
+def sum_all(lefts, rights, inner_terms, act_terms, small, row_count, col_count, act_type):
+    count = len(rights)
     sizes = plane_sizes(row_count)
     na, nb, nk = sizes
     chips = na * nb
-    deep = terms[0].shape[1] // row_count
+    tokens = lefts[0][0].shape[0]
+    deep = lefts[0][0].shape[1] // row_count
     steps = max(col_count - 1, 1)
     firsts, seconds = PlaneSum.counts_of(sizes)
-    widths = [t.shape[2] for t in terms]
+    widths = [right[0].shape[2] for right in rights]
     token_rows = act_terms.shape[0] // col_count
+    inner_width = inner_terms.shape[1]
+    chunk = min(512, inner_width)
     scratch = []
     for width in widths:
         scratch += [
-            pltpu.VMEM((col_count, chips, deep, width), bf16),
             pltpu.VMEM((col_count, chips, deep, width), bf16),
             pltpu.VMEM((col_count, 2, max(seconds, 1), deep // 2, width), bf16),
             pltpu.VMEM((col_count, 2, max(firsts, 1), deep // 2, width), bf16),
             pltpu.VMEM((2, steps, deep, width), bf16),
             pltpu.VMEM((deep, width), f32),
+            pltpu.VMEM((nk * tokens, chips * deep), bf16),
+            pltpu.VMEM((col_count, nk * tokens, width), bf16),
         ]
+    scratch += InnerSum.scratch(sizes, deep, inner_width, chunk)
     plane_sems = (count, col_count, 2, max(PlaneSum.sem_count(sizes), 1))
     scratch += [
         pltpu.VMEM((2, steps, token_rows, act_terms.shape[1]), bf16),
-        pltpu.SemaphoreType.DMA((count, col_count)),
-        pltpu.SemaphoreType.DMA((count, col_count)),
-        pltpu.SemaphoreType.DMA((count, col_count)),
+        pltpu.SemaphoreType.DMA((2, count * nk)),
+        pltpu.SemaphoreType.DMA((count,)),
         pltpu.SemaphoreType.DMA(plane_sems),
         pltpu.SemaphoreType.DMA(plane_sems),
         pltpu.SemaphoreType.DMA((count + 1, 2, steps)),
@@ -1020,29 +1180,485 @@
         pltpu.VMEM((col_count,) + small.shape, f32),
         pltpu.SemaphoreType.DMA((2, 3, max(max(sizes) - 1, 1))),
         pltpu.SemaphoreType.DMA((2, 2, steps)),
+        pltpu.SemaphoreType.DMA((count, chips)),
     ]
     vmem = pl.BlockSpec(memory_space=pltpu.VMEM)
+    flops = sum(2 * nk * tokens * chips * deep * width * col_count for width in widths)
     return pl.pallas_call(
-        functools.partial(sum_kernel, (row_count, col_count), count),
+        functools.partial(sum_kernel, (row_count, col_count), count, chunk),
         out_shape=[jax.ShapeDtypeStruct((deep, width), f32) for width in widths]
         + [
+            jax.ShapeDtypeStruct((deep, inner_width), f32),
             jax.ShapeDtypeStruct((token_rows, act_terms.shape[1]), act_type),
             jax.ShapeDtypeStruct(small.shape, f32),
         ],
-        in_specs=[ANY] * count + [vmem, vmem],
-        out_specs=[ANY] * count + [vmem, vmem],
+        in_specs=[ANY] * (2 * count * nk) + [ANY, vmem, vmem],
+        out_specs=[ANY] * (count + 1) + [vmem, vmem],
         scratch_shapes=scratch,
         compiler_params=pltpu.CompilerParams(
-            collective_id=1, has_side_effects=True, vmem_limit_bytes=60 << 20
+            collective_id=1, has_side_effects=True, vmem_limit_bytes=63 << 20
         ),
         cost_estimate=pl.CostEstimate(
-            flops=0, bytes_accessed=sum(t.size for t in terms) * 4, transcendentals=0
+            flops=flops, bytes_accessed=inner_terms.size * 2, transcendentals=0
         ),
         name="sum_weights",
     )(
-        *[t.reshape(col_count, chips, nk, deep, t.shape[2]) for t in terms],
+        *[left for pair in lefts for left in pair],
+        *[right for pair in rights for right in pair],
+        inner_terms.reshape(chips, nk, deep, inner_width),
         act_terms,
         small,
+    )
+
+
+LANES = 2 * HD
+
+
+def lower_lanes():
+    return lax.broadcasted_iota(jnp.int32, (1, LANES), 1) < HD
+
+
+def rope_lanes(values, cosine, sinusoid):
+    lane = lax.broadcasted_iota(jnp.int32, (1, LANES), 1)
+    other = jnp.where(
+        lane % HD < HD // 2,
+        pltpu.roll(values, LANES - HD // 2, 1),
+        pltpu.roll(values, HD // 2, 1),
+    )
+    return values * cosine + other * sinusoid
+
+
+def head_at(tile, head, upper):
+    if (head % 2 == 1) != upper:
+        tile = pltpu.roll(tile, HD, 1)
+    keep = lower_lanes()
+    if upper:
+        keep = jnp.logical_not(keep)
+    return jnp.where(keep, tile, 0.0)
+
+
+def tile_of(head):
+    return slice(head // 2 * LANES, head // 2 * LANES + LANES)
+
+
+def pair_tile(even, odd, upper):
+    if upper:
+        even = pltpu.roll(even, HD, 1)
+    else:
+        odd = pltpu.roll(odd, HD, 1)
+    return jnp.where(lower_lanes(), even, odd)
+
+
+def attend_kernel(sizes, heads, group, back, *refs):
+    xn, x, wf_in, wo_in, bias, cosq, sinq, coskv, sinkv, gain = refs[:10]
+    q_out, kv_out, mixed_out, lse_out, hidden, hn = refs[10:16]
+    q, kv, mixed, lse, wf, wo, w_sems, o_sems, sends, recvs = refs[16:]
+    place = Place(*sizes)
+    cols, col = place.cols, place.col
+    tokens = xn.shape[0]
+    query_width = heads * HD
+    own_rows = pl.ds(back * tokens, tokens)
+    pairs = heads // group
+
+    def weight_copies(z):
+        return (
+            pltpu.make_async_copy(wf_in.at[z], wf.at[z], w_sems.at[0, z]),
+            pltpu.make_async_copy(wo_in.at[z], wo.at[z], w_sems.at[1, z]),
+        )
+
+    for number in (0, 1):
+        for z in range(cols):
+            weight_copies(z)[number].start()
+    for step in range(1, back + 1):
+
+        @pl.when(col < step)
+        def _():
+            kv[:, (back - step) * tokens : (back - step + 1) * tokens] = jnp.zeros(
+                (cols, tokens, kv.shape[2]), bf16
+            )
+
+    place.greet(False, True)
+
+    def hop(z, step):
+        source = kv.at[z, pl.ds((back - step + 1) * tokens, tokens)]
+        target = kv.at[z, pl.ds((back - step) * tokens, tokens)]
+        return remote(
+            source, target, sends.at[step - 1, z], recvs.at[step - 1, z], (place.row, col + 1)
+        )
+
+    def goes(step):
+        return (col < cols - 1) & (col >= step - 1)
+
+    def send(z, step):
+        pl.when(goes(step))(lambda: hop(z, step).start())
+
+    def receive(z, step):
+        ref = kv.at[z, pl.ds((back - step) * tokens, tokens)]
+
+        @pl.when(col >= step)
+        def _():
+            remote(
+                ref, ref, sends.at[step - 1, z], recvs.at[step - 1, z], (place.row, col + 1)
+            ).wait_recv()
+
+    def project(z, carry):
+        weight_copies(z)[0].wait()
+        pre = matmul(xn[...], wf[z])
+        for n in range(query_width // LANES):
+            at = slice(n * LANES, (n + 1) * LANES)
+            q[z, :, at] = rope_lanes(pre[:, at], cosq[...], sinq[...]).astype(bf16)
+        for n in range(pairs):
+            at = slice(n * LANES, (n + 1) * LANES)
+            tile = pre[:, query_width + n * LANES : query_width + (n + 1) * LANES]
+            kv[z, own_rows, at] = rope_lanes(tile, coskv[...], sinkv[...]).astype(bf16)
+        if back > 0:
+            send(z, 1)
+        return carry
+
+    lax.fori_loop(0, cols, project, 0)
+    for step in range(1, back):
+        for z in range(cols):
+            receive(z, step)
+            send(z, step + 1)
+
+    def attend(z, carry):
+        if back > 0:
+            receive(z, back)
+        lane = lax.broadcasted_iota(jnp.int32, (1, LANES), 1)
+        logs = jnp.zeros((tokens, LANES), f32)
+        outs = []
+        for head in range(heads):
+            pair = head // group
+            keyval = kv[z, :, pair * LANES : (pair + 1) * LANES]
+            query = head_at(q[z, :, tile_of(head)].astype(f32), head, False) * HD**-0.5
+            scores = against(query.astype(bf16), keyval) + bias[...]
+            summit = jnp.max(scores, axis=1, keepdims=True)
+            weights = jnp.exp(scores - summit)
+            total = jnp.sum(weights, axis=1, keepdims=True)
+            chances = (weights * (1.0 / total)).astype(bf16)
+            outs.append(matmul(chances, keyval))
+            logs = jnp.where(lane == head, summit + jnp.log(total), logs)
+            if head % 2 == 1:
+                mixed[z, :, tile_of(head)] = pair_tile(outs[-2], outs[-1], True).astype(bf16)
+        lse[z] = jnp.transpose(logs)[:heads]
+        return carry
+
+    lax.fori_loop(0, cols, attend, 0)
+    outputs = [
+        pltpu.make_async_copy(source, target, o_sems.at[n])
+        for n, (source, target) in enumerate(
+            ((q, q_out), (kv, kv_out), (mixed, mixed_out), (lse, lse_out))
+        )
+    ]
+    for copy in outputs:
+        copy.start()
+    hidden[...] = x[...].astype(f32)
+
+    def project_out(z, carry):
+        weight_copies(z)[1].wait()
+        hidden[...] += against(mixed[z], wo[z])
+        return carry
+
+    lax.fori_loop(0, cols, project_out, 0)
+    total = hidden[...]
+    scale = lax.rsqrt(jnp.mean(total * total, axis=1, keepdims=True) + epsilon)
+    hn[...] = (total * scale * gain[...]).astype(bf16)
+    for copy in outputs:
+        copy.wait()
+    for step in range(1, back + 1):
+        for z in range(cols):
+            pl.when(goes(step))(lambda: hop(z, step).wait_send())
+
+
+def attend(xn, x, wf, wo, bias, tables, gain, heads, group, back, row_count, col_count, cid):
+    tokens, width = xn.shape
+    query_width = heads * HD
+    kv_shape = (col_count, (back + 1) * tokens, heads // group * LANES)
+    q_shape = (col_count, tokens, query_width)
+    lse_shape = (col_count, heads, tokens)
+    vmem = pl.BlockSpec(memory_space=pltpu.VMEM)
+    keys = (back + 1) * tokens
+    return pl.pallas_call(
+        functools.partial(attend_kernel, (row_count, col_count), heads, group, back),
+        out_shape=[
+            jax.ShapeDtypeStruct(q_shape, bf16),
+            jax.ShapeDtypeStruct(kv_shape, bf16),
+            jax.ShapeDtypeStruct(q_shape, bf16),
+            jax.ShapeDtypeStruct(lse_shape, f32),
+            jax.ShapeDtypeStruct((tokens, width), f32),
+            jax.ShapeDtypeStruct((tokens, width), bf16),
+        ],
+        in_specs=[vmem, vmem, ANY, ANY] + [vmem] * 6,
+        out_specs=[ANY] * 4 + [vmem] * 2,
+        scratch_shapes=[
+            pltpu.VMEM(q_shape, bf16),
+            pltpu.VMEM(kv_shape, bf16),
+            pltpu.VMEM(q_shape, bf16),
+            pltpu.VMEM(lse_shape, f32),
+            pltpu.VMEM(wf.shape, bf16),
+            pltpu.VMEM(wo.shape, bf16),
+            pltpu.SemaphoreType.DMA((2, col_count)),
+            pltpu.SemaphoreType.DMA((4,)),
+            pltpu.SemaphoreType.DMA((max(back, 1), col_count)),
+            pltpu.SemaphoreType.DMA((max(back, 1), col_count)),
+        ],
+        compiler_params=pltpu.CompilerParams(
+            collective_id=cid, has_side_effects=True, vmem_limit_bytes=56 << 20
+        ),
+        cost_estimate=pl.CostEstimate(
+            flops=2 * tokens * (wf.size + wo.size) + 4 * col_count * heads * tokens * keys * HD,
+            bytes_accessed=(wf.size + wo.size) * 2,
+            transcendentals=col_count * heads * tokens * keys,
+        ),
+        name="attend",
+    )(xn, x, wf, wo, bias, *tables, gain)
+
+
+def attend_back_kernel(sizes, heads, group, back, chunk, *refs):
+    dhb, xn, lse, bias, cosq, sinq, coskv, sinkv = refs[:8]
+    mixed_in, q_in, kv_in, wo_in, wf_in, terms = refs[8:14]
+    dxn, dqkv_out, sum_out, xn_sib, dhb_sib, mixed_sib, dqkv_sib = refs[14:21]
+    q, kv, wo, wf, dmix, dkv, dqkv, going, coming, dst, pst, rhs_q, rhs_o = refs[21:34]
+    in_sems, wo_sems, wf_sems, out_sems, pair_sems, row_sems, sends, recvs = refs[34:42]
+    place = Place(*sizes)
+    cols, col = place.cols, place.col
+    cores = place.sizes[2]
+    tokens = dhb.shape[0]
+    query_width = heads * HD
+    pairs = heads // group
+    inner = InnerSum(place, terms, sum_out, chunk, refs[42:])
+
+    in_copies = [
+        pltpu.make_async_copy(q_in, q, in_sems.at[0]),
+        pltpu.make_async_copy(kv_in, kv, in_sems.at[1]),
+    ]
+
+    def wo_copy(z):
+        slot = lax.rem(z, 2)
+        return pltpu.make_async_copy(wo_in.at[z], wo.at[slot], wo_sems.at[slot])
+
+    def wf_copy(z):
+        slot = lax.rem(z, 2)
+        return pltpu.make_async_copy(wf_in.at[z], wf.at[slot], wf_sems.at[slot])
+
+    wo_copy(0).start()
+    for copy in in_copies:
+        copy.start()
+    for z in range(min(2, cols)):
+        wf_copy(z).start()
+    place.greet(True, True)
+
+    other = place.device(2, 1)
+    exchanges = []
+    if cores > 1:
+        chips, deep = terms.shape[0], terms.shape[2]
+        moves = [(mixed_in, mixed_sib)]
+        for chip in range(chips):
+            to, rows = pl.ds(chip * deep, deep), core_rows(place, chip, 1, deep)
+            moves += [(xn.at[:, rows], xn_sib.at[:, to]), (dhb.at[:, rows], dhb_sib.at[:, to])]
+        exchanges = [
+            remote(source, target, pair_sems.at[0, n], pair_sems.at[1, n], other)
+            for n, (source, target) in enumerate(moves)
+        ]
+
+    def row_exchange(z):
+        return remote(dqkv.at[z], dqkv_sib.at[z], row_sems.at[0, z], row_sems.at[1, z], other)
+
+    def out_copy(z):
+        return pltpu.make_async_copy(dqkv.at[z], dqkv_out.at[z], out_sems.at[z])
+
+    inner.begin()
+    for exchange in exchanges:
+        exchange.start()
+    dxn[...] = jnp.zeros_like(dxn)
+    for copy in in_copies:
+        copy.wait()
+
+    def hop(z, step):
+        return remote(
+            going.at[step - 1, z],
+            coming.at[step - 1, z],
+            sends.at[step - 1, z],
+            recvs.at[step - 1, z],
+            (place.row, col - 1),
+        )
+
+    def goes(step):
+        return col - back + step - 1 >= 0
+
+    def comes(step):
+        return (col < cols - 1) & (col + step - back >= 0)
+
+    def send(z, step):
+        pl.when(goes(step))(lambda: hop(z, step).start())
+
+    def chunk_rows(step):
+        return slice(step * tokens, (step + 1) * tokens)
+
+    def halo(step, z):
+        if step > 0:
+            pl.when(comes(step))(lambda: hop(z, step).wait_recv())
+            term = jnp.where(comes(step), coming[step - 1, z].astype(f32), 0.0)
+            total = dkv[z, chunk_rows(step)] + term
+        else:
+            total = dkv[z, chunk_rows(step)]
+        if step < back:
+            going[step, z] = total.astype(bf16)
+            send(z, step + 1)
+            return
+        for n in range(pairs):
+            at = slice(n * LANES, (n + 1) * LANES)
+            dqkv[z, :, query_width + n * LANES : query_width + (n + 1) * LANES] = rope_lanes(
+                total[:, at], coskv[...], sinkv[...]
+            ).astype(bf16)
+        out_copy(z).start()
+        if cores > 1:
+            row_exchange(z).start()
+        wf_copy(z).wait()
+        dxn[...] += against(dqkv[z], wf[lax.rem(z, 2)])
+        when(z + 2 < cols, lambda: wf_copy(z + 2).start())
+
+    def halos(z):
+        for step in range(1, back + 1):
+            at = z - step
+            when((at >= 0) & (at < cols), lambda: halo(step, at))
+
+    def one_col(z, carry):
+        wo_copy(z).wait()
+        when(z + 1 < cols, lambda: wo_copy(z + 1).start())
+        dmix[...] = matmul(dhb[...], wo[lax.rem(z, 2)]).astype(bf16)
+        for n in range(pairs):
+            keyval = kv[z, :, n * LANES : (n + 1) * LANES]
+            for i in range(group):
+                head = n * group + i
+                at = slice(i * tokens, (i + 1) * tokens)
+                query = head_at(q[z, :, tile_of(head)].astype(f32), head, False) * HD**-0.5
+                query = query.astype(bf16)
+                grad = head_at(dmix[:, tile_of(head)].astype(f32), head, True).astype(bf16)
+                rhs_q[at] = query
+                rhs_o[at] = grad
+                chances = jnp.exp(against(keyval, query) + bias[...] - lse[z, head : head + 1])
+                grad_chance = against(keyval, grad)
+                centre = jnp.sum(chances * grad_chance, axis=0, keepdims=True)
+                dst[:, at] = (chances * (grad_chance - centre)).astype(bf16)
+                pst[:, at] = chances.astype(bf16)
+            dkv[z, :, n * LANES : (n + 1) * LANES] = matmul(dst[...], rhs_q[...]) + matmul(
+                pst[...], rhs_o[...]
+            )
+            grad_rows = dot_tokens(keyval, dst[...])
+            for i in range(0, group, 2):
+                tile = jnp.concatenate(
+                    [
+                        grad_rows[:HD, i * tokens : (i + 1) * tokens],
+                        grad_rows[:HD, (i + 1) * tokens : (i + 2) * tokens],
+                    ],
+                    axis=0,
+                )
+                turned = rope_lanes(jnp.transpose(tile), cosq[...], sinq[...]) * HD**-0.5
+                dqkv[z, :, tile_of(n * group + i)] = turned.astype(bf16)
+            inner.tick(z * pairs + n)
+        halo(0, z)
+        halos(z)
+        return carry
+
+    lax.fori_loop(0, cols, one_col, 0)
+    ticks = list(range(cols * pairs, inner.count + 2))
+    for z in range(cols, cols + back):
+        if ticks:
+            inner.tick(ticks.pop(0))
+        halos(z)
+    for t in ticks:
+        inner.tick(t)
+    for z in range(cols):
+        out_copy(z).wait()
+        if cores > 1:
+            row_exchange(z).wait_send()
+            row_exchange(z).wait_recv()
+    for exchange in exchanges:
+        exchange.wait_send()
+        exchange.wait_recv()
+    for step in range(1, back + 1):
+        for z in range(cols):
+            pl.when(goes(step))(lambda: hop(z, step).wait_send())
+    inner.finish()
+
+
+def attend_back(
+    dhb, xn, lse, bias, tables, mixed, q, kv, wo, wf, terms, group, sizes, cid
+):
+    row_count, col_count = sizes
+    plane = plane_sizes(row_count)
+    chips = plane[0] * plane[1]
+    tokens, width = dhb.shape
+    heads = lse.shape[1]
+    back = kv.shape[1] // tokens - 1
+    pairs = heads // group
+    keys = kv.shape[1]
+    all_width = wf.shape[2]
+    inner_width = terms.shape[1]
+    chunk = min(512, inner_width)
+    deep = terms.shape[0] // row_count
+    row_shape = (col_count, tokens, all_width)
+    halo_shape = (max(back, 1), col_count, tokens, kv.shape[2])
+    vmem = pl.BlockSpec(memory_space=pltpu.VMEM)
+    return pl.pallas_call(
+        functools.partial(attend_back_kernel, sizes, heads, group, back, chunk),
+        out_shape=[
+            jax.ShapeDtypeStruct((tokens, width), f32),
+            jax.ShapeDtypeStruct(row_shape, bf16),
+            jax.ShapeDtypeStruct((deep, inner_width), f32),
+            jax.ShapeDtypeStruct((tokens, chips * deep), bf16),
+            jax.ShapeDtypeStruct((tokens, chips * deep), bf16),
+            jax.ShapeDtypeStruct(mixed.shape, bf16),
+            jax.ShapeDtypeStruct(row_shape, bf16),
+        ],
+        in_specs=[vmem] * 8 + [ANY] * 6,
+        out_specs=[vmem] + [ANY] * 6,
+        scratch_shapes=[
+            pltpu.VMEM(q.shape, bf16),
+            pltpu.VMEM(kv.shape, bf16),
+            pltpu.VMEM((2,) + wo.shape[1:], bf16),
+            pltpu.VMEM((2,) + wf.shape[1:], bf16),
+            pltpu.VMEM((tokens, heads * HD), bf16),
+            pltpu.VMEM(kv.shape, f32),
+            pltpu.VMEM(row_shape, bf16),
+            pltpu.VMEM(halo_shape, bf16),
+            pltpu.VMEM(halo_shape, bf16),
+            pltpu.VMEM((keys, group * tokens), bf16),
+            pltpu.VMEM((keys, group * tokens), bf16),
+            pltpu.VMEM((group * tokens, LANES), bf16),
+            pltpu.VMEM((group * tokens, LANES), bf16),
+            pltpu.SemaphoreType.DMA((2,)),
+            pltpu.SemaphoreType.DMA((2,)),
+            pltpu.SemaphoreType.DMA((2,)),
+            pltpu.SemaphoreType.DMA((col_count,)),
+            pltpu.SemaphoreType.DMA((2, 1 + 2 * chips)),
+            pltpu.SemaphoreType.DMA((2, col_count)),
+            pltpu.SemaphoreType.DMA((max(back, 1), col_count)),
+            pltpu.SemaphoreType.DMA((max(back, 1), col_count)),
+        ]
+        + InnerSum.scratch(plane, deep, inner_width, chunk),
+        compiler_params=pltpu.CompilerParams(
+            collective_id=cid, has_side_effects=True, vmem_limit_bytes=62 << 20
+        ),
+        cost_estimate=pl.CostEstimate(
+            flops=2 * tokens * (wf.size + wo.size) + 10 * col_count * heads * tokens * keys * HD,
+            bytes_accessed=(wf.size + wo.size + terms.size) * 2,
+            transcendentals=col_count * heads * tokens * keys,
+        ),
+        name="attend_back",
+    )(
+        dhb,
+        xn,
+        lse,
+        bias,
+        *tables,
+        mixed,
+        q,
+        kv,
+        wo,
+        wf,
+        terms.reshape(chips, plane[2], deep, inner_width),
     )
 
 
@@ -1162,90 +1778,69 @@
 
     inputs = tokens.astype(f32)
     normal_in, scale_in = normalize(inputs, gain_first)
-    projected = jnp.stack([matmul(normal_in, full_first[z]) for z in range(col_count)])
-    queries = (
-        rotate(projected[:, :, :query_width].reshape(col_count, local, heads, HD), cosine, sinusoid)
-        .astype(bf16)
-        .reshape(col_count, local, pairs, group, HD)
-    )
-    keyvals = projected[:, :, query_width:].reshape(col_count, local, pairs, 2, HD)
-    keyvals = jnp.stack(
-        [rotate(keyvals[:, :, :, 0], cosine, sinusoid), keyvals[:, :, :, 1]], axis=3
-    ).astype(bf16)
-    chunks = [keyvals]
-    for _ in range(back):
-        chunks.insert(0, shift(chunks[0], 1, col_count))
-    all_keyvals = jnp.concatenate(chunks, axis=1)
-    key_rows, values = all_keyvals[:, :, :, 0], all_keyvals[:, :, :, 1]
-
-    factor = HD ** (-0.5)
-    scores = jnp.einsum("ztkgd,zskd->zkgts", queries, key_rows, preferred_element_type=f32) * factor
-    scores = jnp.where(allowed, scores, blocked)
-    summit = jnp.max(scores, axis=-1, keepdims=True)
-    weights = jnp.exp(scores - summit)
-    totals = jnp.sum(weights, axis=-1, keepdims=True)
-    chances = weights / totals
-    rounded = chances.astype(bf16)
-    mixed = (
-        jnp.einsum("zkgts,zskd->ztkgd", rounded, values, preferred_element_type=f32)
-        .astype(bf16)
-        .reshape(col_count, local, query_width)
-    )
-    attended = sum(against(mixed[z], full_output[z]) for z in range(col_count))
-    hidden_in = inputs + attended
-    normal_mid, scale_mid = normalize(hidden_in, gain_second)
+    halves = jnp.concatenate([cosine, cosine], axis=1)
+    signed = jnp.concatenate([-sinusoid, sinusoid], axis=1)
+    tables = (
+        jnp.concatenate([halves, halves], axis=1),
+        jnp.concatenate([signed, signed], axis=1),
+        jnp.concatenate([halves, jnp.ones_like(halves)], axis=1),
+        jnp.concatenate([signed, jnp.zeros_like(signed)], axis=1),
+    )
+    bias = jnp.where(allowed, 0.0, blocked).astype(f32)
+    queries, all_keyvals, mixed, lse, hidden_in, normal_mid = attend(
+        normal_in,
+        tokens,
+        full_first,
+        full_output,
+        bias,
+        tables,
+        gain_second[None],
+        heads,
+        group,
+        back,
+        row_count,
+        col_count,
+        4,
+    )
+    scale_mid = lax.rsqrt(jnp.mean(hidden_in * hidden_in, axis=1, keepdims=True) + epsilon)
 
     rows_mid = line_gather(normal_mid, row_count, col_count, 2)
     grad_mid, out_terms, grad_hidden_part, grad_down_part = mlp(
         rows_mid, rows_grad, full_hidden, full_down, row_count, col_count, 3
     )
-    sum_hidden = lax.psum_scatter(grad_hidden_part, "row", scatter_dimension=0, tiled=True)
-    sum_down = lax.psum_scatter(grad_down_part, "row", scatter_dimension=0, tiled=True)
-
     back_mid, gain_mid_part = norm_back(grad_mid, hidden_in, scale_mid, gain_second)
     grad_hidden_in = out_grad.astype(f32) + back_mid
     grad_low = grad_hidden_in.astype(bf16)
-    grad_mixed = jnp.stack(
-        [matmul(grad_low, full_output[z]).astype(bf16) for z in range(col_count)]
-    ).reshape(col_count, local, pairs, group, HD)
-    grad_output_part = jnp.stack(
-        [over_rows(grad_low, mixed[z]).astype(bf16) for z in range(col_count)]
-    )
-
-    grad_chance = jnp.einsum("ztkgd,zskd->zkgts", grad_mixed, values, preferred_element_type=f32)
-    centre = jnp.sum(chances * grad_chance, axis=-1, keepdims=True)
-    grad_score = (chances * (grad_chance - centre)).astype(bf16)
-    grad_query = (
-        jnp.einsum("zkgts,zskd->ztkgd", grad_score, key_rows, preferred_element_type=f32) * factor
-    )
-    grad_key = (
-        jnp.einsum("zkgts,ztkgd->zskd", grad_score, queries, preferred_element_type=f32) * factor
-    )
-    grad_value = jnp.einsum("zkgts,ztkgd->zskd", rounded, grad_mixed, preferred_element_type=f32)
-    grad_keyval = jnp.stack([grad_key, grad_value], axis=3)
-    carried = None
-    for number in range(back + 1):
-        part = grad_keyval[:, number * local : (number + 1) * local]
-        if carried is not None:
-            part = part + carried.astype(f32)
-        if number < back:
-            carried = shift(part.astype(bf16), -1, col_count)
-    grad_query = rotate(
-        grad_query.reshape(col_count, local, heads, HD), cosine, -sinusoid
-    ).reshape(col_count, local, query_width)
-    grad_keyval = jnp.stack(
-        [rotate(part[:, :, :, 0], cosine, -sinusoid), part[:, :, :, 1]], axis=3
-    ).reshape(col_count, local, pairs * 2 * HD)
-    grad_first = jnp.concatenate([grad_query, grad_keyval], axis=2).astype(bf16)
-    grad_first_part = jnp.stack(
-        [over_rows(normal_in, grad_first[z]).astype(bf16) for z in range(col_count)]
-    )
-    grad_in = sum(against(grad_first[z], full_first[z]) for z in range(col_count))
+    cores = plane_sizes(row_count)[2]
+    tables_back = (tables[0], -tables[1], tables[2], -tables[3])
+    grad_in, grad_first, sum_hidden, normal_sib, grad_low_sib, mixed_sib, grad_first_sib = (
+        attend_back(
+            grad_low,
+            normal_in,
+            lse,
+            bias.T,
+            tables_back,
+            mixed,
+            queries,
+            all_keyvals,
+            full_output,
+            full_first,
+            grad_hidden_part,
+            group,
+            (row_count, col_count),
+            5,
+        )
+    )
     back_in, gain_in_part = norm_back(grad_in, inputs, scale_in, gain_first)
     grad_tokens = (grad_hidden_in + back_in).astype(bf16)
     gain_parts = jnp.concatenate([gain_in_part, gain_mid_part]).reshape(-1, 128)
-    sum_first, sum_output, out_sum, gain_sums = sum_all(
-        [grad_first_part, grad_output_part], out_terms, gain_parts, row_count, col_count, f32
+    lefts = [
+        (normal_in, normal_sib)[:cores],
+        (grad_low, grad_low_sib)[:cores],
+    ]
+    rights = [(grad_first, grad_first_sib)[:cores], (mixed, mixed_sib)[:cores]]
+    sum_first, sum_output, sum_down, out_sum, gain_sums = sum_all(
+        lefts, rights, grad_down_part, out_terms, gain_parts, row_count, col_count, f32
     )
     block_out = hidden_in + out_sum
     gain_in_sum, gain_mid_sum = gain_sums.reshape(2, width)
@@ -1257,8 +1852,8 @@
         sum_first[:, query_width:].reshape(deep, pairs, 2 * HD),
         sum_output,
         gain_mid_sum,
-        sum_hidden.astype(f32).reshape(deep, 2, hidden),
-        sum_down.astype(f32),
+        sum_hidden.reshape(deep, 2, hidden),
+        sum_down,
     )
 
 

time: 743 us -> 659 us (0.89)
  Pallas kernels: 486 us -> 593 us
  matrix products: 106 us -> 0 us
  waiting for transfers between devices: 33.8 us -> 0.02 us
  other arithmetic: 53.3 us -> 23.5 us
  local copies, waits for them, and re-layouts: 30.2 us -> 18.7 us
  starting transfers between devices: 11.1 us -> 0.04 us
    pallas_call x0 -> x2, Pallas kernels: none -> 126 us  [the longest x1 92.5 us: attend_back(): pl.pallas_call(functools.partial(attend_back_kernel, sizes, heads, group,...]
    dot_general x29 -> x0, matrix products: 91.7 us -> none  [the longest x8 21.2 us: matmul(): return jnp.dot(left, right, preferred_element_type=f32)]
    ppermute x4 -> x0, waiting for transfers between devices: 33.3 us -> none  [shift(): return lax.ppermute(values, 'col', pairs)]
    pallas_call x1, Pallas kernels: 171 us -> 142 us  [sum_all(): pl.pallas_call(functools.partial(sum_kernel, (row_count, col_count), coun...]
    convert_element_type x3 -> x0, other arithmetic: 20.7 us -> none  [the longest x1 17.7 us: shards(): grad_score = (chances * (grad_chance - centre)).astype(bf16)]
    another operation x13 -> x1, other arithmetic: 16.3 us -> 0.18 us  [the longest x1 5.87 us: shards(): jnp.stack([over_rows(normal_in, grad_first[z]).astype(bf16) for z in rang...]
    sub x1 -> x0, matrix products: 14.2 us -> none  [shards(): weights = jnp.exp(scores - summit)]
    ppermute x4 -> x0, starting transfers between devices: 10.8 us -> none  [shift(): return lax.ppermute(values, 'col', pairs)]
  transfers between devices with their start and end apart: 7 -> 1, of which waited for: 4 -> 0; matrix products, arithmetic and copies ran while one was open for 23% -> 1% of each run, Pallas kernels for 33% -> 18%
where the time goes in v4:
time: 659 us; the launch traced here: 650 us
  Pallas kernels  593 us (90%)
  other arithmetic  23.5 us (4%)
  local copies, waits for them, and re-layouts  18.7 us (3%)
  between operations  14.7 us (2%)
    pallas_call x1, Pallas kernels, sum_all(): pl.pallas_call(functools.partial(sum_kernel, (row_count, col_count), coun...  142 us
    pallas_call x1, Pallas kernels, gather_all(): pl.pallas_call(functools.partial(gather_kernel, (row_count, col_count), c...  140 us
    pallas_call x1, Pallas kernels, mlp(): pl.pallas_call(functools.partial(mlp_kernel, (row_count, col_count), tile...  102 us
    pallas_call x1, Pallas kernels, attend_back(): pl.pallas_call(functools.partial(attend_back_kernel, sizes, heads, group,...  92.5 us
    pallas_call x1, Pallas kernels, line_gather(): pl.pallas_call(functools.partial(line_gather_kernel, (row_count, col_coun...  83.1 us
    pallas_call x1, Pallas kernels, attend(): pl.pallas_call(functools.partial(attend_kernel, (row_count, col_count), h...  33.2 us
  transfers between devices with their start and end apart: 1, of which 0 were waited for; matrix products, arithmetic and copies ran while one was open for 1% of the time, Pallas kernels for 18%

profile of v4, /device:TPU:0, one launch (start us, length us, event | category | flops | bytes accessed | tf_op | source)
XLA Modules:
  0.0 650.2 jit_solution(17638285071883147483)
XLA Ops:
  7.2 0.9 copy.22
  8.2 3.8 copy.19
  12.0 0.8 pad_maximum_fusion.refs_0_
  12.8 140.4 %gather_weights.1 = (bf16[4,2048,768]{2,1,0:T(8,128)(2,1)}, bf16[4,2048,512]{2,1,0:T(8,128)(2,1)}, bf16[2048,2048]{1,0:T(8,128)(2,1)}, bf16[1024,2048]{1,0:T(8,128)(2,1)}) custom-call(bf16[256,768]{1,0:T(8,128)(2,1)} %pad_maximum_fusion.refs_0_, bf16[256,512]{1,0:T(8,128)(2,1)} %refs_1_.2, bf16[256,2048]{1,0:T(8,128)(2,1)} %refs_2_.1, bf16[256,2048]{1,0:T(8,128)(2,1)} %refs_3_.1), custom_call_target="tpu_custom_call" | custom-call | bytes 20971520 | tf_op jit(solution)/shard_map/gather_weights/pallas_call | solution.py:364
  153.2 0.2 reduce-window.8
  153.5 0.6 convert_element_type.35
  154.5 0.3 fusion
  154.8 0.5 fusion.16
  155.4 1.1 fusion.14
  156.5 1.0 fusion.11.refs_4_
  157.5 1.3 fusion.2.refs_0_.refs_1_
  158.8 33.2 %attend.1 = (bf16[4,256,512]{2,1,0:T(8,128)(2,1)}, bf16[4,768,256]{2,1,0:T(8,128)(2,1)}, bf16[4,256,512]{2,1,0:T(8,128)(2,1)}, f32[4,8,256]{2,1,0:T(8,128)}, f32...) custom-call(bf16[256,2048]{1,0:T(8,128)(2,1)} %fusion.2.refs_0_.refs_1_, bf16[256,2048]{1,0:T(8,128)(2,1)} %refs_1_.3, ...), custom_call_target="tpu_custom_call" | custom-call | flops 6979321856 | bytes 20971520 | tf_op jit(solution)/shard_map/attend/pallas_call | solution.py:1381
  192.0 83.1 %gather_line.1 = bf16[1024,2048]{1,0:T(8,128)(2,1)} custom-call(bf16[256,2048]{1,0:T(8,128)(2,1)} %get-tuple-element.41.own), custom_call_target="tpu_custom_call" | custom-call | bytes 4194304 | tf_op jit(solution)/shard_map/gather_line/pallas_call | solution.py:407
  275.1 0.2 multiply_reduce_fusion.2
  275.4 1.2 fusion.13.refs_3_
  276.5 101.9 %feed_forward.1 = (f32[256,2048]{1,0:T(8,128)}, bf16[4,256,2048]{2,1,0:T(8,128)(2,1)}, bf16[2048,4096]{1,0:T(8,128)(2,1)}, bf16[2048,2048]{1,0:T(8,128)(2,1)}) custom-call(bf16[4,256,2048]{2,1,0:T(8,128)(2,1)} %bitcast.24, bf16[4,256,2048]{2,1,0:T(8,128)(2,1)} %bitcast.35, bf16[2048,4096]{1,0:T(8,128)(2,1)} %all-gather.2.cloned.1.call-done.refs_2_, ...), custom_call_target="tpu_custom_call" | custom-call | flops 77309411328 | bytes 50331648 | tf_op jit(solution)/shard_map/feed_forward/pallas_call | solution.py:660
  378.5 2.9 multiply_reduce_fusion
  381.4 0.5 copy-done.6
  381.9 3.5 fusion.20
  385.5 92.5 %attend_back.1 = (f32[256,2048]{1,0:T(8,128)}, bf16[4,256,768]{2,1,0:T(8,128)(2,1)}, f32[256,4096]{1,0:T(8,128)}, bf16[256,1024]{1,0:T(8,128)(2,1)}, bf16[256,10...) custom-call(bf16[256,2048]{1,0:T(8,128)(2,1)} %get-tuple-element.75.refs_0_.refs_2_, ...), custom_call_target="tpu_custom_call" | custom-call | flops 9395240960 | bytes 37748736 | tf_op jit(solution)/shard_map/attend_back/pallas_call | solution.py:1604
  477.9 2.1 fusion.9
  480.1 0.6 pad_maximum_fusion.5.refs_10_
  480.7 142.3 %sum_weights.1 = (f32[256,768]{1,0:T(8,128)}, f32[256,512]{1,0:T(8,128)}, f32[256,2048]{1,0:T(8,128)}, f32[256,2048]{1,0:T(8,128)}, f32[32,128]{1,0:T(8,128)}) custom-call(bf16[256,2048]{1,0:T(8,128)(2,1)} %fusion.2.refs_0_.refs_1_, bf16[256,1024]{1,0:T(8,128)(2,1)} %get-tuple-element.51.refs_1_, bf16[256,2048]{1,0:T(8,128)(2,1)} %get-tuple-element.75.refs_0_.refs_2_, ...), custom_call_target="tpu_custom_call" | custom-call | flops 5368709120 | bytes 8388608 | tf_op jit(solution)/shard_map/sum_weights/pallas_call | solution.py:1187
  622.9 1.0 slice.9
  623.9 1.9 slice.8
  625.8 3.5 add_convert_fusion
  629.3 0.8 reshape.152
  630.1 0.6 slice_bitcast_fusion
  630.7 6.7 %reshape.153 = f32[256,2,2048]{2,1,0:T(2,128)} reshape(f32[256,4096]{1,0:T(8,128)} %get-tuple-element.63) | data formatting | bytes 8388608 | tf_op jit(solution)/shard_map/reshape | solution.py:1855
  637.4 3.3 fusion.8
  640.8 0.8 copy.25
  641.6 1.3 copy.26
  (47 shorter events, 0.7 us)
Async XLA Ops:
  7.2 269.3 %all-gather.2.cloned.1.call-start = ((), (), s32[]{:S(2)}) async-start(), calls=%async_computation | async-start | bytes 18874368 | tf_op jit(solution)/shard_map/all_gather | solution.py:1777
  8.1 3.9 copy-start.9
  12.8 140.4 %copy-start.14 = (s32[1,3]{1,0:T(1,128)S(1)}, s32[1,3]{1,0:T(1,128)}, u32[]{:S(2)}) copy-start(s32[1,3]{1,0:T(1,128)} %param.11) | copy-start | bytes 40
  12.8 140.7 %copy-start.12 = (bf16[2048]{0:T(1024)(128)(2,1)S(1)}, bf16[2048]{0:T(1024)(128)(2,1)}, u32[]{:S(2)}) copy-start(bf16[2048]{0:T(1024)(128)(2,1)} %param.12) | copy-start | bytes 12292
  12.8 140.8 %copy-start.13 = (bf16[2048]{0:T(1024)(128)(2,1)S(1)}, bf16[2048]{0:T(1024)(128)(2,1)}, u32[]{:S(2)}) copy-start(bf16[2048]{0:T(1024)(128)(2,1)} %param.16) | copy-start | bytes 12292
  12.8 141.7 %copy-start.2 = (bf16[256,2048]{1,0:T(8,128)(2,1)S(1)}, bf16[256,2048]{1,0:T(8,128)(2,1)}, u32[]{:S(2)}) copy-start(bf16[256,2048]{1,0:T(8,128)(2,1)} %refs_1_.3) | copy-start | bytes 3145732
  192.0 83.2 %copy-start = (f32[256,2048]{1,0:T(8,128)S(1)}, f32[256,2048]{1,0:T(8,128)}, u32[]{:S(2)}) copy-start(f32[256,2048]{1,0:T(8,128)} %get-tuple-element.40) | copy-start | bytes 6291460
  276.5 101.9 %copy-start.10 = (f32[2048]{0:T(1024)S(1)}, f32[2048]{0:T(1024)}, u32[]{:S(2)}) copy-start(f32[2048]{0:T(1024)} %convert_element_type.35) | copy-start | bytes 24580
  378.4 3.0 copy-start.1
  378.4 3.5 copy-start.6
  385.5 92.5 %copy-start.3 = (bf16[256,2048]{1,0:T(8,128)(2,1)S(1)}, bf16[256,2048]{1,0:T(8,128)(2,1)}, u32[]{:S(2)}) copy-start(bf16[256,2048]{1,0:T(8,128)(2,1)} %refs_1_.3) | copy-start | bytes 3145732
  625.8 4.3 copy-start.11
  630.7 6.7 %copy-start.4 = (bf16[256,2048]{1,0:T(8,128)(2,1)S(1)}, bf16[256,2048]{1,0:T(8,128)(2,1)}, u32[]{:S(2)}) copy-start(bf16[256,2048]{1,0:T(8,128)(2,1)} %refs_1_.3) | copy-start | bytes 3145732
  630.7 6.7 %copy-start.5 = (f32[256,2048]{1,0:T(8,128)S(1)}, f32[256,2048]{1,0:T(8,128)}, u32[]{:S(2)}) copy-start(f32[256,2048]{1,0:T(8,128)} %get-tuple-element.58) | copy-start | bytes 6291460
  637.4 3.3 copy-start.8
  637.4 4.1 copy-start.7
Sparse Core Ops, SparseCore 0:
  153.3 89.0 all-gather.1

commit v5 on v4

--- a/solution.py
+++ b/solution.py
@@ -246,11 +246,33 @@
                         self.sender(half, 1, i, j + 1).start()
                     self.share(half, i, j)
 
-    def finish(self):
+    def shared(self):
+        for copy in self.all_copies():
+            if copy[1] == 2:
+                self.receiver(*copy).wait_recv()
+
+    def sent(self):
         for copy in self.all_copies():
             self.sender(*copy).wait_send()
-            if copy[1] == 2:
-                self.receiver(*copy).wait_recv()
+
+    def finish(self):
+        self.shared()
+        self.sent()
+
+
+def tile_gather(place, full, own, send_sems, recv_sems):
+    deep = full.shape[0] // place.rows
+    half = deep // 2
+
+    def block(row, number):
+        return full.at[pl.ds(row * deep + number * half, half)]
+
+    def mine(number):
+        if own is None:
+            return block(place.row, number)
+        return own.at[pl.ds(number * half, half)]
+
+    return PlaneGather(place, block, mine, send_sems, recv_sems)
 
 
 def nearby(place, number):
@@ -515,185 +537,301 @@
     return lax.dot_general(left, right, (((0,), (0,)), ((), ())), preferred_element_type=f32)
 
 
-def mlp_kernel(sizes, tile, wide, *refs):
-    hn_in, dy_in, wh_in, wd_in, grad_out, y_out, dwh_out, dwd_out = refs[:8]
-    hn, dy, wh, wd, act, dgu, terms, staged, held = refs[8:17]
-    token_sems, weight_sems, y_sems, dw_sems, sends, recvs = refs[17:]
+def plan_units(cols, tiles, early, hop_us, tile_us, unit_us):
+    begin = 4.0
+    chunk_at = [0.0] + [begin + hop_us * k for k in range(1, cols)]
+    tile_at = [0.0] * early + [begin + 2.0 + tile_us * (n + 1) for n in range(tiles - early)]
+    events = [(chunk_at[k], ("chunk", k)) for k in range(1, cols)]
+    for f in range(early, tiles):
+        second_at = begin + 1.0 + 0.35 * tile_us * (f - early + 1)
+        events.append((second_at, ("second", f)))
+        events.append((tile_at[f], ("third", f)))
+    events.sort(key=lambda event: event[0])
+    units = [(max(chunk_at[k], tile_at[f]), k, f) for k in range(cols) for f in range(tiles)]
+    units.sort()
+    plan, now, after = [], 0.0, []
+    while units or events or after:
+        while events and events[0][0] <= now:
+            plan.append(events.pop(0)[1])
+        if after and (not units or units[0][0] > now):
+            step, cost = after.pop(0)
+            plan.append(step)
+            now += cost
+            continue
+        if units and units[0][0] <= now:
+            _, k, f = units.pop(0)
+            plan.append(("unit", k, f))
+            now += unit_us
+            if not any(unit[1] == k for unit in units):
+                if k > 0:
+                    after.append((("grad", k), 2.6 * unit_us))
+                after.append((("y", k), 1.3 * unit_us))
+                after.sort(key=lambda item: -item[0][1] if item[0][0] == "grad" else 1)
+            continue
+        now = min([events[0][0]] * bool(events) + [units[0][0]] * bool(units))
+    return plan + [("grad", 0)]
+
+
+def mlp_kernel(sizes, early, wide, *refs):
+    hn_own, dy_in, wh_in, wh_own, wd_in, grad_out, y_out, dwh_out, dwd_out = refs[:9]
+    hn, dy, wh, wd, act, dgu, terms, staged, held = refs[9:18]
+    token_sems, tile_sems, wd_sems, y_sems, dw_sems, sends, recvs = refs[18:25]
+    hs, hr, ps, pr, own_sem = refs[25:]
     place = Place(*sizes)
     cols = place.cols
-    hidden = wd.shape[1]
-    width = wd.shape[0]
-    tiles = hidden // tile
+    width, hidden = wd.shape
+    tiles = wh.shape[0]
+    tile = hidden // tiles
     wides = width // wide
     tokens = hn.shape[1]
-    line = LineSum(place, lambda j: terms.at[j], held, sends, recvs)
-
-    def token_copies(j):
-        return (
-            pltpu.make_async_copy(hn_in.at[j], hn.at[j], token_sems.at[0, j]),
-            pltpu.make_async_copy(dy_in.at[j], dy.at[j], token_sems.at[1, j]),
+    deep = wh_own.shape[1]
+
+    def wide_at(n):
+        return pl.ds(pl.multiple_of(n * wide, wide), wide)
+
+    def piece(n):
+        return LineSum(
+            place, lambda j: terms.at[j, :, wide_at(n)], held.at[n], sends.at[n], recvs.at[n]
         )
 
-    def part(number, base=0):
-        return pl.ds(pl.multiple_of(base + number * tile, tile), tile)
-
-    def weight_copies(f):
-        gate, up = part(f), part(f, hidden)
-        return (
-            pltpu.make_async_copy(wh_in.at[:, gate], wh.at[:, gate], weight_sems.at[0, f]),
-            pltpu.make_async_copy(wh_in.at[:, up], wh.at[:, up], weight_sems.at[1, f]),
-            pltpu.make_async_copy(wd_in.at[:, gate], wd.at[:, gate], weight_sems.at[2, f]),
-        )
-
-    def order(number):
-        return nearby(place, cols - 1 - number)
-
-    for copy in token_copies(order(0)):
-        copy.start()
+    near = [nearby(place, k) for k in range(cols)]
+
+    def dy_copy(j):
+        return pltpu.make_async_copy(dy_in.at[j], dy.at[j], token_sems.at[j])
+
+    def wd_copy(f):
+        at = slice(f * tile, (f + 1) * tile)
+        return pltpu.make_async_copy(wd_in.at[:, at], wd.at[:, at], wd_sems.at[f])
+
+    def tile_copy(f):
+        if f < early:
+            return pltpu.make_async_copy(wh_in.at[f], wh.at[f], tile_sems.at[f])
+        rows = pl.ds(place.row * deep, deep)
+        return pltpu.make_async_copy(wh_own.at[f - early], wh.at[f, rows], tile_sems.at[f])
+
+    own_copy = pltpu.make_async_copy(hn_own, hn.at[place.col], own_sem)
+    own_copy.start()
+    for f in range(early, tiles):
+        tile_copy(f).start()
+    dy_copy(near[0]).start()
     for f in range(tiles):
-        for copy in weight_copies(f):
-            copy.start()
-    for number in range(1, cols):
-        for copy in token_copies(order(number)):
-            copy.start()
-    place.greet(False, True)
+        if f < early:
+            tile_copy(f).start()
+        wd_copy(f).start()
+    for k in range(1, cols):
+        dy_copy(near[k]).start()
+    place.greet(True, True)
+    own_copy.wait()
+    line = LineGather(place, hn.at[place.col], lambda j: hn.at[j], hs, hr)
+    for way in (0, 1):
+        line.send(way, 1)
+    parts = {
+        f: tile_gather(place, wh.at[f], None, ps.at[f - early], pr.at[f - early])
+        for f in range(early, tiles)
+    }
+    for f in range(early, tiles):
+        tile_copy(f).wait()
+        parts[f].first()
 
     def out_copy(slot, j):
         return pltpu.make_async_copy(staged.at[slot], y_out.at[j], y_sems.at[slot])
 
-    for number in range(cols):
-        j = order(number)
-        for copy in token_copies(j):
-            copy.wait()
-
-        def hidden_tile(f, carry):
-            if number == 0:
-                for copy in weight_copies(f):
-                    copy.wait()
-            gate_at, up_at = part(f), part(f, hidden)
-            gate = matmul(hn[j], wh[:, gate_at])
-            up = matmul(hn[j], wh[:, up_at])
-            back = matmul(dy[j], wd[:, gate_at])
-            sigmoid = jax.nn.sigmoid(gate)
-            silu = gate * sigmoid
-            act[j, :, gate_at] = (silu * up).astype(bf16)
-            dgu[j, :, gate_at] = (back * up * sigmoid * (1.0 + gate * (1.0 - sigmoid))).astype(bf16)
-            dgu[j, :, up_at] = (back * silu).astype(bf16)
+    def unit(k, f):
+        j = near[k]
+        at = slice(f * tile, (f + 1) * tile)
+        gate_up = matmul(hn[j], wh[f])
+        gate, up = gate_up[:, :tile], gate_up[:, tile:]
+        back = matmul(dy[j], wd[:, at])
+        sigmoid = jax.nn.sigmoid(gate)
+        silu = gate * sigmoid
+        act[j, :, at] = (silu * up).astype(bf16)
+        dgate = back * up * sigmoid * (1.0 + gate * (1.0 - sigmoid))
+        dgu[j, :, 2 * f * tile : (2 * f + 1) * tile] = dgate.astype(bf16)
+        dgu[j, :, (2 * f + 1) * tile : (2 * f + 2) * tile] = (back * silu).astype(bf16)
+
+    def grad(k):
+        j = near[k]
+
+        def body(n, carry):
+            at = wide_at(n)
+            total = 0.0
+            for f in range(tiles):
+                total += against(dgu[j, :, 2 * f * tile : 2 * (f + 1) * tile], wh[f, at])
+            terms[j, :, at] = total.astype(bf16)
+            piece(n).early(j, True)
             return carry
 
-        lax.fori_loop(0, tiles, hidden_tile, 0)
-
-        def grad_tile(n, carry):
-            at = pl.ds(pl.multiple_of(n * wide, wide), wide)
-            terms[j, :, at] = against(dgu[j], wh[at]).astype(bf16)
-            return carry
-
-        lax.fori_loop(0, wides, grad_tile, 0)
-        line.early(j, True)
-        slot = number % 2
-        if number >= 2:
-            out_copy(slot, order(number - 2)).wait()
-
-        def y_tile(n, carry):
-            at = pl.ds(pl.multiple_of(n * wide, wide), wide)
+        lax.fori_loop(0, wides, body, 0)
+
+    stored = []
+
+    def y_part(k):
+        j = near[k]
+        slot = len(stored) % 2
+        if len(stored) >= 2:
+            out_copy(slot, near[stored[-2]]).wait()
+
+        def body(n, carry):
+            at = wide_at(n)
             staged[slot, :, at] = against(act[j], wd[at]).astype(bf16)
             return carry
 
-        lax.fori_loop(0, wides, y_tile, 0)
+        lax.fori_loop(0, wides, body, 0)
         out_copy(slot, j).start()
-        if number >= 2:
-            line.late(order(number - 2), True)
-
-    rest = [number for number in range(max(cols - 2, 0), cols - 1)]
+        stored.append(k)
+
+    def late(number):
+        low, high = place.col, cols - 1 - place.col
+        up_first = jnp.minimum(jnp.maximum(high - low, 0), 1)
+        side = up_first * high + (1 - up_first) * low
+        way = 2 * up_first - 1
+        first = jnp.minimum(jnp.maximum(side - number, 0), 1)
+        col = place.col + first * way * (number + 1) - (1 - first) * way * (number + 1 - side)
+        return col
+
+    calls = [(number, n) for number in range(cols - 1) for n in range(wides)]
+
+    def next_late():
+        if calls:
+            number, n = calls.pop(0)
+            piece(n).late(late(number), True)
+
+    seen_tiles, seen_chunks = set(), set()
+    for step in plan_units(cols, tiles, early, 24.0, 18.0, 2.1):
+        if step[0] == "chunk":
+            for way in (0, 1):
+                line.receive(way, step[1])
+        elif step[0] == "second":
+            parts[step[1]].second()
+        elif step[0] == "third":
+            parts[step[1]].third()
+            parts[step[1]].shared()
+        elif step[0] == "unit":
+            _, k, f = step
+            if f not in seen_tiles:
+                seen_tiles.add(f)
+                if f < early:
+                    tile_copy(f).wait()
+                wd_copy(f).wait()
+            if k not in seen_chunks:
+                seen_chunks.add(k)
+                dy_copy(near[k]).wait()
+            unit(k, f)
+        elif step[0] == "grad":
+            grad(step[1])
+            if step[1] in (0, cols - 1):
+                next_late()
+        else:
+            y_part(step[1])
+            if step[1] == cols - 1:
+                next_late()
+
+    for f in parts:
+        parts[f].sent()
     strips = width // 256
-    calls = [functools.partial(line.late, order(number), True) for number in rest]
 
     def flat(ref):
         return ref[...].reshape(cols * tokens, ref.shape[2])
 
-    def weight_strip(left, right, store, target, sem, at):
-        columns = jnp.concatenate([left[j, :, at] for j in range(cols)], axis=0)
-        store[at] = dot_tokens(columns, flat(right)).astype(bf16)
-        pltpu.make_async_copy(store.at[at], target.at[at], sem).start()
+    def columns(ref, at):
+        return jnp.concatenate([ref[j, :, at] for j in range(cols)], axis=0)
 
     def down_strip(n, carry):
         at = pl.ds(pl.multiple_of(n * 256, 256), 256)
-        weight_strip(dy, act, wd, dwd_out, dw_sems.at[0, n], at)
+        wd[at] = dot_tokens(columns(dy, at), flat(act)).astype(bf16)
+        pltpu.make_async_copy(wd.at[at], dwd_out.at[at], dw_sems.at[0, n]).start()
         return carry
 
     def hidden_strip(n, carry):
         at = pl.ds(pl.multiple_of(n * 256, 256), 256)
-        weight_strip(hn, dgu, wh, dwh_out, dw_sems.at[1, n], at)
+        result = dot_tokens(columns(hn, at), flat(dgu)).astype(bf16)
+        for f in range(tiles):
+            wh[f, at] = result[:, 2 * f * tile : 2 * (f + 1) * tile]
+        pltpu.make_async_copy(wh.at[:, at], dwh_out.at[:, at], dw_sems.at[1, n]).start()
         return carry
 
-    pieces = [(down_strip, 0, strips // 2), (down_strip, strips // 2, strips)]
-    pieces += [(hidden_strip, n, n + 2) for n in range(0, strips, 2)]
-    for body, begin, end in pieces:
-        lax.fori_loop(begin, end, body, 0)
-        if calls:
-            calls.pop(0)()
-    for call in calls:
-        call()
-    line.last(grad_out)
+    for begin, end in ((0, strips // 2), (strips // 2, strips)):
+        lax.fori_loop(begin, end, down_strip, 0)
+        if begin == 0:
+            next_late()
+    for begin, end in ((0, 1), (1, 3), (3, 5), (5, 7), (7, strips)):
+        lax.fori_loop(begin, end, hidden_strip, 0)
+        next_late()
+    while calls:
+        next_late()
+    for n in range(wides):
+        piece(n).last(grad_out.at[:, wide_at(n)])
     for number in range(max(cols - 2, 0), cols):
-        out_copy(number % 2, order(number)).wait()
+        out_copy(number % 2, near[stored[number]]).wait()
 
     def finish(n, carry):
         at = pl.ds(pl.multiple_of(n * 256, 256), 256)
         pltpu.make_async_copy(wd.at[at], dwd_out.at[at], dw_sems.at[0, n]).wait()
-        pltpu.make_async_copy(wh.at[at], dwh_out.at[at], dw_sems.at[1, n]).wait()
+        pltpu.make_async_copy(wh.at[:, at], dwh_out.at[:, at], dw_sems.at[1, n]).wait()
         return carry
 
     lax.fori_loop(0, strips, finish, 0)
     line.finish()
-
-
-def mlp(hn, dy, wh, wd, row_count, col_count, collective_id):
+    for n in range(wides):
+        piece(n).finish()
+
+
+def mlp(hn, dy, wh, wh_own, wd, row_count, col_count, collective_id):
     steps = max(col_count - 1, 1)
-    rows, width = hn.shape[0] // col_count, hn.shape[1]
+    rows, width = hn.shape
     hidden = wd.shape[1]
-    tile = min(512, hidden)
+    early, left = wh.shape[0], wh_own.shape[0]
+    tiles = early + left
+    tile = hidden // tiles
     wide = min(512, width)
     shape = (col_count, rows, width)
     vmem = pl.BlockSpec(memory_space=pltpu.VMEM)
     total = col_count * rows
+    wh_shape = (tiles, width, 2 * tile)
+    plane_sems = (left, 2, PlaneGather.sem_count(plane_sizes(row_count)))
     grad, y, dwh, dwd = pl.pallas_call(
-        functools.partial(mlp_kernel, (row_count, col_count), tile, wide),
+        functools.partial(mlp_kernel, (row_count, col_count), early, wide),
         out_shape=[
             jax.ShapeDtypeStruct((rows, width), f32),
             jax.ShapeDtypeStruct(shape, bf16),
-            jax.ShapeDtypeStruct(wh.shape, bf16),
+            jax.ShapeDtypeStruct(wh_shape, bf16),
             jax.ShapeDtypeStruct(wd.shape, bf16),
         ],
-        in_specs=[ANY] * 4,
+        in_specs=[ANY] * 5,
         out_specs=[vmem, ANY, ANY, ANY],
         scratch_shapes=[
             pltpu.VMEM(shape, bf16),
             pltpu.VMEM(shape, bf16),
-            pltpu.VMEM(wh.shape, bf16),
+            pltpu.VMEM(wh_shape, bf16),
             pltpu.VMEM(wd.shape, bf16),
             pltpu.VMEM((col_count, rows, hidden), bf16),
             pltpu.VMEM((col_count, rows, 2 * hidden), bf16),
             pltpu.VMEM(shape, bf16),
             pltpu.VMEM((2, rows, width), bf16),
-            pltpu.VMEM((2, steps, rows, width), bf16),
-            pltpu.SemaphoreType.DMA((2, col_count)),
-            pltpu.SemaphoreType.DMA((3, hidden // tile)),
+            pltpu.VMEM((width // wide, 2, steps, rows, wide), bf16),
+            pltpu.SemaphoreType.DMA((col_count,)),
+            pltpu.SemaphoreType.DMA((tiles,)),
+            pltpu.SemaphoreType.DMA((tiles,)),
             pltpu.SemaphoreType.DMA((2,)),
             pltpu.SemaphoreType.DMA((2, width // 256)),
+            pltpu.SemaphoreType.DMA((width // wide, 2, steps)),
+            pltpu.SemaphoreType.DMA((width // wide, 2, steps)),
             pltpu.SemaphoreType.DMA((2, steps)),
             pltpu.SemaphoreType.DMA((2, steps)),
+            pltpu.SemaphoreType.DMA(plane_sems),
+            pltpu.SemaphoreType.DMA(plane_sems),
+            pltpu.SemaphoreType.DMA,
         ],
         compiler_params=pltpu.CompilerParams(
             collective_id=collective_id, has_side_effects=True, vmem_limit_bytes=63 << 20
         ),
         cost_estimate=pl.CostEstimate(
             flops=2 * 9 * total * width * hidden,
-            bytes_accessed=(wh.size + wd.size) * 4,
+            bytes_accessed=6 * width * hidden * 2,
             transcendentals=total * hidden,
         ),
         name="feed_forward",
-    )(hn.reshape(shape), dy.reshape(shape), wh, wd)
+    )(hn, dy.reshape(shape), wh, wh_own, wd)
     return grad, y.reshape(total, width), dwh, dwd
 
 
@@ -797,11 +935,10 @@
 
 
 class InnerSum:
-    def __init__(self, place, terms, out, chunk, refs):
-        self.place, self.terms, self.out, self.chunk = place, terms, out, chunk
+    def __init__(self, place, count, terms, target, refs):
+        self.place, self.count, self.terms, self.target = place, count, terms, target
         self.acc, self.core_held, self.second, self.first, self.staged = refs[:5]
         self.load_sems, self.core_sems, self.plane_sems, self.out_sems = refs[5:]
-        self.count = out.shape[1] // chunk
         self.ahead = min(3, self.count)
 
     @staticmethod
@@ -822,17 +959,14 @@
             pltpu.SemaphoreType.DMA((2,)),
         ]
 
-    def columns(self, e):
-        return pl.ds(pl.multiple_of(e * self.chunk, self.chunk), self.chunk)
-
     def load(self, e):
-        source = self.terms.at[:, self.place.at[2], :, self.columns(e)]
+        source = self.terms(e, self.place.at[2])
         return pltpu.make_async_copy(source, self.acc.at[e], self.load_sems.at[e])
 
     def share(self, e):
         other = lax.rem(self.place.at[2] + 1, self.place.sizes[2])
         return remote(
-            self.terms.at[:, other, :, self.columns(e)],
+            self.terms(e, other),
             self.core_held.at[e],
             self.core_sems.at[0, e],
             self.core_sems.at[1, e],
@@ -852,7 +986,7 @@
     def out_copy(self, e):
         slot = lax.rem(e, 2)
         return pltpu.make_async_copy(
-            self.staged.at[slot], self.out.at[:, self.columns(e)], self.out_sems.at[slot]
+            self.staged.at[slot], self.target(e), self.out_sems.at[slot]
         )
 
     def prepare(self, e):
@@ -991,7 +1125,17 @@
     inner_out, act_out, small_out = refs[3 + count : 6 + count]
     refs = refs[6 + count :]
     per = [refs[7 * n : 7 * n + 7] for n in range(count)]
-    inner = InnerSum(place, inner_terms, inner_out, chunk, refs[7 * count : 7 * count + 9])
+
+    def inner_columns(e):
+        return pl.ds(pl.multiple_of(e * chunk, chunk), chunk)
+
+    inner = InnerSum(
+        place,
+        inner_out.shape[1] // chunk,
+        lambda e, core: inner_terms.at[:, core, :, inner_columns(e)],
+        lambda e: inner_out.at[:, inner_columns(e)],
+        refs[7 * count : 7 * count + 9],
+    )
     act_held, load_sems, out_sems, ps, pr, zs, zr = refs[7 * count + 9 : 7 * count + 16]
     ring_held, line_held, ring_sems, line_sems, chip_sems = refs[7 * count + 16 :]
     token_rows = act_out.shape[0]
@@ -1250,9 +1394,9 @@
 
 
 def attend_kernel(sizes, heads, group, back, *refs):
-    xn, x, wf_in, wo_in, bias, cosq, sinq, coskv, sinkv, gain = refs[:10]
-    q_out, kv_out, mixed_out, lse_out, hidden, hn = refs[10:16]
-    q, kv, mixed, lse, wf, wo, w_sems, o_sems, sends, recvs = refs[16:]
+    xn, x, wf_in, wo_in, bias, cosq, sinq, coskv, sinkv, gain, tiles = refs[:11]
+    q_out, kv_out, mixed_out, lse_out, full_tiles, hidden, hn = refs[11:18]
+    q, kv, mixed, lse, wf, wo, w_sems, o_sems, sends, recvs, t_sems, ps, pr = refs[18:]
     place = Place(*sizes)
     cols, col = place.cols, place.col
     tokens = xn.shape[0]
@@ -1277,7 +1421,23 @@
                 (cols, tokens, kv.shape[2]), bf16
             )
 
-    place.greet(False, True)
+    keeps = [
+        pltpu.make_async_copy(
+            tiles.at[f],
+            full_tiles.at[f, pl.ds(place.row * tiles.shape[1], tiles.shape[1])],
+            t_sems.at[f],
+        )
+        for f in range(tiles.shape[0])
+    ]
+    for keep in keeps:
+        keep.start()
+    place.greet(True, True)
+    parts = [
+        tile_gather(place, full_tiles.at[f], tiles.at[f], ps.at[f], pr.at[f])
+        for f in range(tiles.shape[0])
+    ]
+    for part in parts:
+        part.first()
 
     def hop(z, step):
         source = kv.at[z, pl.ds((back - step + 1) * tokens, tokens)]
@@ -1316,6 +1476,8 @@
         return carry
 
     lax.fori_loop(0, cols, project, 0)
+    if parts:
+        parts[0].second()
     for step in range(1, back):
         for z in range(cols):
             receive(z, step)
@@ -1341,6 +1503,17 @@
             if head % 2 == 1:
                 mixed[z, :, tile_of(head)] = pair_tile(outs[-2], outs[-1], True).astype(bf16)
         lse[z] = jnp.transpose(logs)[:heads]
+
+        @pl.when(z == 0)
+        def _():
+            for part in parts[1:]:
+                part.second()
+
+        @pl.when(z == max(cols - 2, 1))
+        def _():
+            for part in parts[:-1]:
+                part.third()
+
         return carry
 
     lax.fori_loop(0, cols, attend, 0)
@@ -1363,14 +1536,20 @@
     total = hidden[...]
     scale = lax.rsqrt(jnp.mean(total * total, axis=1, keepdims=True) + epsilon)
     hn[...] = (total * scale * gain[...]).astype(bf16)
-    for copy in outputs:
+    if parts:
+        parts[-1].third()
+    for part in parts:
+        part.finish()
+    for copy in keeps + outputs:
         copy.wait()
     for step in range(1, back + 1):
         for z in range(cols):
             pl.when(goes(step))(lambda: hop(z, step).wait_send())
 
 
-def attend(xn, x, wf, wo, bias, tables, gain, heads, group, back, row_count, col_count, cid):
+def attend(
+    xn, x, wf, wo, bias, tables, gain, tiles, heads, group, back, row_count, col_count, cid
+):
     tokens, width = xn.shape
     query_width = heads * HD
     kv_shape = (col_count, (back + 1) * tokens, heads // group * LANES)
@@ -1378,6 +1557,8 @@
     lse_shape = (col_count, heads, tokens)
     vmem = pl.BlockSpec(memory_space=pltpu.VMEM)
     keys = (back + 1) * tokens
+    count = tiles.shape[0]
+    plane_sems = (count, 2, PlaneGather.sem_count(plane_sizes(row_count)))
     return pl.pallas_call(
         functools.partial(attend_kernel, (row_count, col_count), heads, group, back),
         out_shape=[
@@ -1385,11 +1566,12 @@
             jax.ShapeDtypeStruct(kv_shape, bf16),
             jax.ShapeDtypeStruct(q_shape, bf16),
             jax.ShapeDtypeStruct(lse_shape, f32),
+            jax.ShapeDtypeStruct((count, row_count * tiles.shape[1], tiles.shape[2]), bf16),
             jax.ShapeDtypeStruct((tokens, width), f32),
             jax.ShapeDtypeStruct((tokens, width), bf16),
         ],
-        in_specs=[vmem, vmem, ANY, ANY] + [vmem] * 6,
-        out_specs=[ANY] * 4 + [vmem] * 2,
+        in_specs=[vmem, vmem, ANY, ANY] + [vmem] * 7,
+        out_specs=[ANY] * 5 + [vmem] * 2,
         scratch_shapes=[
             pltpu.VMEM(q_shape, bf16),
             pltpu.VMEM(kv_shape, bf16),
@@ -1401,6 +1583,9 @@
             pltpu.SemaphoreType.DMA((4,)),
             pltpu.SemaphoreType.DMA((max(back, 1), col_count)),
             pltpu.SemaphoreType.DMA((max(back, 1), col_count)),
+            pltpu.SemaphoreType.DMA((count,)),
+            pltpu.SemaphoreType.DMA(plane_sems),
+            pltpu.SemaphoreType.DMA(plane_sems),
         ],
         compiler_params=pltpu.CompilerParams(
             collective_id=cid, has_side_effects=True, vmem_limit_bytes=56 << 20
@@ -1411,7 +1596,7 @@
             transcendentals=col_count * heads * tokens * keys,
         ),
         name="attend",
-    )(xn, x, wf, wo, bias, *tables, gain)
+    )(xn, x, wf, wo, bias, *tables, gain, tiles)
 
 
 def attend_back_kernel(sizes, heads, group, back, chunk, *refs):
@@ -1426,7 +1611,17 @@
     tokens = dhb.shape[0]
     query_width = heads * HD
     pairs = heads // group
-    inner = InnerSum(place, terms, sum_out, chunk, refs[42:])
+    hidden = sum_out.shape[1] // 2
+
+    def inner_target(e):
+        at = lax.rem(e, 2) * hidden + e // 2 * chunk
+        return sum_out.at[:, pl.ds(pl.multiple_of(at, chunk), chunk)]
+
+    def inner_terms(e, core):
+        at = pl.multiple_of(lax.rem(e, 2) * chunk, chunk)
+        return terms.at[e // 2, :, core, :, pl.ds(at, chunk)]
+
+    inner = InnerSum(place, 2 * hidden // chunk, inner_terms, inner_target, refs[42:])
 
     in_copies = [
         pltpu.make_async_copy(q_in, q, in_sems.at[0]),
@@ -1451,7 +1646,7 @@
     other = place.device(2, 1)
     exchanges = []
     if cores > 1:
-        chips, deep = terms.shape[0], terms.shape[2]
+        chips, deep = terms.shape[1], terms.shape[3]
         moves = [(mixed_in, mixed_sib)]
         for chip in range(chips):
             to, rows = pl.ds(chip * deep, deep), core_rows(place, chip, 1, deep)
@@ -1595,9 +1790,10 @@
     pairs = heads // group
     keys = kv.shape[1]
     all_width = wf.shape[2]
-    inner_width = terms.shape[1]
-    chunk = min(512, inner_width)
-    deep = terms.shape[0] // row_count
+    tiles, _, chunk = terms.shape
+    chunk = chunk // 2
+    inner_width = 2 * tiles * chunk
+    deep = terms.shape[1] // row_count
     row_shape = (col_count, tokens, all_width)
     halo_shape = (max(back, 1), col_count, tokens, kv.shape[2])
     vmem = pl.BlockSpec(memory_space=pltpu.VMEM)
@@ -1658,7 +1854,7 @@
         kv,
         wo,
         wf,
-        terms.reshape(chips, plane[2], deep, inner_width),
+        terms.reshape(tiles, chips, plane[2], deep, 2 * chunk),
     )
 
 
@@ -1771,10 +1967,11 @@
         [first_weight, output_weight], [down_weight], out_grad, row_count, col_count
     )
 
-    hidden_flat, full_first = lax.optimization_barrier(
-        (hidden_weight.reshape(deep, 2 * hidden), full_first)
-    )
-    full_hidden = lax.all_gather(hidden_flat, "row", axis=0, tiled=True)
+    tile = min(512, hidden)
+    tiles = hidden // tile
+    early = max(tiles // 2, 1)
+    hidden_tiles = jnp.transpose(hidden_weight.reshape(deep, 2, tiles, tile), (2, 0, 1, 3))
+    hidden_tiles = hidden_tiles.reshape(tiles, deep, 2 * tile)
 
     inputs = tokens.astype(f32)
     normal_in, scale_in = normalize(inputs, gain_first)
@@ -1787,7 +1984,7 @@
         jnp.concatenate([signed, jnp.zeros_like(signed)], axis=1),
     )
     bias = jnp.where(allowed, 0.0, blocked).astype(f32)
-    queries, all_keyvals, mixed, lse, hidden_in, normal_mid = attend(
+    queries, all_keyvals, mixed, lse, early_tiles, hidden_in, normal_mid = attend(
         normal_in,
         tokens,
         full_first,
@@ -1795,6 +1992,7 @@
         bias,
         tables,
         gain_second[None],
+        hidden_tiles[:early],
         heads,
         group,
         back,
@@ -1804,9 +2002,15 @@
     )
     scale_mid = lax.rsqrt(jnp.mean(hidden_in * hidden_in, axis=1, keepdims=True) + epsilon)
 
-    rows_mid = line_gather(normal_mid, row_count, col_count, 2)
     grad_mid, out_terms, grad_hidden_part, grad_down_part = mlp(
-        rows_mid, rows_grad, full_hidden, full_down, row_count, col_count, 3
+        normal_mid,
+        rows_grad,
+        early_tiles,
+        hidden_tiles[early:],
+        full_down,
+        row_count,
+        col_count,
+        3,
     )
     back_mid, gain_mid_part = norm_back(grad_mid, hidden_in, scale_mid, gain_second)
     grad_hidden_in = out_grad.astype(f32) + back_mid

time: 659 us -> 619 us (0.939)
  Pallas kernels: 593 us -> 570 us
  between operations: 14.7 us -> 1.13 us
    pallas_call x2 -> x1, Pallas kernels: 185 us -> 160 us  [mlp(): pl.pallas_call(functools.partial(mlp_kernel, (row_count, col_count), earl...]
    pallas_call x1, Pallas kernels: 33.2 us -> 44 us  [attend(): pl.pallas_call(functools.partial(attend_kernel, (row_count, col_count), h...]
    pallas_call x1, Pallas kernels: 92.5 us -> 85.3 us  [attend_back(): pl.pallas_call(functools.partial(attend_back_kernel, sizes, heads, group,...]
  transfers between devices with their start and end apart: 1 -> 0, of which waited for: 0 -> 0; matrix products, arithmetic and copies ran while one was open for 1% -> 0% of each run, Pallas kernels for 18% -> 0%
where the time goes in v5:
time: 619 us; the launch traced here: 613 us
  Pallas kernels  570 us (92%)
  other arithmetic  24.8 us (4%)
  local copies, waits for them, and re-layouts  17.9 us (3%)
    pallas_call x1, Pallas kernels, mlp(): pl.pallas_call(functools.partial(mlp_kernel, (row_count, col_count), earl...  160 us
    pallas_call x1, Pallas kernels, sum_all(): pl.pallas_call(functools.partial(sum_kernel, (row_count, col_count), coun...  140 us
    pallas_call x1, Pallas kernels, gather_all(): pl.pallas_call(functools.partial(gather_kernel, (row_count, col_count), c...  140 us
    pallas_call x1, Pallas kernels, attend_back(): pl.pallas_call(functools.partial(attend_back_kernel, sizes, heads, group,...  85.3 us
    pallas_call x1, Pallas kernels, attend(): pl.pallas_call(functools.partial(attend_kernel, (row_count, col_count), h...  44 us

profile of v5, /device:TPU:0, one launch (start us, length us, event | category | flops | bytes accessed | tf_op | source)
XLA Modules:
  0.0 613.4 jit_solution(10328188771671444123)
XLA Ops:
  0.7 0.9 reduce-window.8
  1.6 0.7 select_reduce_fusion
  2.4 0.5 fusion.16
  3.2 1.1 fusion.14
  4.4 1.0 fusion.11.refs_4_
  5.5 0.3 fusion
  5.8 1.3 fusion.2.refs_0_.refs_1_
  7.1 0.8 pad_maximum_fusion.refs_0_
  7.9 140.2 %gather_weights.1 = (bf16[4,2048,768]{2,1,0:T(8,128)(2,1)}, bf16[4,2048,512]{2,1,0:T(8,128)(2,1)}, bf16[2048,2048]{1,0:T(8,128)(2,1)}, bf16[1024,2048]{1,0:T(8,128)(2,1)}) custom-call(bf16[256,768]{1,0:T(8,128)(2,1)} %pad_maximum_fusion.refs_0_, bf16[256,512]{1,0:T(8,128)(2,1)} %refs_1_.2, bf16[256,2048]{1,0:T(8,128)(2,1)} %refs_2_.1, bf16[256,2048]{1,0:T(8,128)(2,1)} %refs_3_.1), custom_call_target="tpu_custom_call" | custom-call | bytes 20971520 | tf_op jit(solution)/shard_map/gather_weights/pallas_call | solution.py:386
  148.1 0.6 convert_element_type.35
  148.7 1.4 copy.25
  150.2 1.5 fusion.21
  151.7 1.5 slice.21.refs_10_
  153.2 44.0 %attend.1 = (bf16[4,256,512]{2,1,0:T(8,128)(2,1)}, bf16[4,768,256]{2,1,0:T(8,128)(2,1)}, bf16[4,256,512]{2,1,0:T(8,128)(2,1)}, f32[4,8,256]{2,1,0:T(8,128)}, bf1...) custom-call(bf16[256,2048]{1,0:T(8,128)(2,1)} %fusion.2.refs_0_.refs_1_, ...), custom_call_target="tpu_custom_call" | custom-call | flops 6979321856 | bytes 20971520 | tf_op jit(solution)/shard_map/attend/pallas_call | solution.py:1562
  197.2 1.5 slice.23.refs_3_
  198.7 159.6 %feed_forward.1 = (f32[256,2048]{1,0:T(8,128)}, bf16[4,256,2048]{2,1,0:T(8,128)(2,1)}, bf16[4,2048,1024]{2,1,0:T(8,128)(2,1)}, bf16[2048,2048]{1,0:T(8,128)(2,1)}) custom-call(bf16[256,2048]{1,0:T(8,128)(2,1)} %get-tuple-element.39.refs_0_, bf16[4,256,2048]{2,1,0:T(8,128)(2,1)} %bitcast.38, bf16[2,2048,1024]{2,1,0:T(8,128)(2,1)} %get-tuple-element.41.refs_2_, ...), custom_call_target="tpu_custom_call" | custom-call | flops 77309411328 | bytes 50331648 | tf_op jit(solution)/shard_map/feed_forward/pallas_call | solution.py:792
  358.4 2.0 multiply_reduce_fusion.2
  360.6 2.3 multiply_reduce_fusion
  363.1 2.3 fusion.20
  365.4 1.1 fusion.13.refs_3_
  366.6 85.3 %attend_back.1 = (f32[256,2048]{1,0:T(8,128)}, bf16[4,256,768]{2,1,0:T(8,128)(2,1)}, f32[256,4096]{1,0:T(8,128)}, bf16[256,1024]{1,0:T(8,128)(2,1)}, bf16[256,10...) custom-call(bf16[256,2048]{1,0:T(8,128)(2,1)} %get-tuple-element.73.refs_0_.refs_2_, ...), custom_call_target="tpu_custom_call" | custom-call | flops 9395240960 | bytes 37748736 | tf_op jit(solution)/shard_map/attend_back/pallas_call | solution.py:1800
  451.9 2.3 fusion.9
  454.2 3.2 fusion.8
  457.4 0.6 pad_maximum_fusion.5.refs_10_
  458.0 140.3 %sum_weights.1 = (f32[256,768]{1,0:T(8,128)}, f32[256,512]{1,0:T(8,128)}, f32[256,2048]{1,0:T(8,128)}, f32[256,2048]{1,0:T(8,128)}, f32[32,128]{1,0:T(8,128)}) custom-call(bf16[256,2048]{1,0:T(8,128)(2,1)} %fusion.2.refs_0_.refs_1_, bf16[256,1024]{1,0:T(8,128)(2,1)} %get-tuple-element.49.refs_1_, bf16[256,2048]{1,0:T(8,128)(2,1)} %get-tuple-element.73.refs_0_.refs_2_, ...), custom_call_target="tpu_custom_call" | custom-call | flops 5368709120 | bytes 8388608 | tf_op jit(solution)/shard_map/sum_weights/pallas_call | solution.py:1331
  598.4 3.5 add_convert_fusion
  602.0 0.8 reshape.151
  602.8 0.9 slice.24
  603.7 0.6 slice_bitcast_fusion
  604.3 6.7 %reshape.152 = f32[256,2,2048]{2,1,0:T(2,128)} reshape(f32[256,4096]{1,0:T(8,128)} %get-tuple-element.61) | data formatting | bytes 8388608 | tf_op jit(solution)/shard_map/reshape | solution.py:2059
  611.0 0.8 copy.29
  611.8 1.3 copy.30
  (48 shorter events, 0.9 us)
Async XLA Ops:
  0.6 4.8 copy-start.1
  0.7 5.1 copy-start.14
  4.3 2.8 copy-start.11
  4.4 2.6 copy-start.10
  7.0 141.1 %copy-start.15 = (bf16[2048]{0:T(1024)(128)(2,1)S(1)}, bf16[2048]{0:T(1024)(128)(2,1)}, u32[]{:S(2)}) copy-start(bf16[2048]{0:T(1024)(128)(2,1)} %param.16) | copy-start | bytes 12292
  7.0 141.7 %copy-start.6 = (bf16[256,2,2048]{2,1,0:T(2,128)(2,1)S(1)}, bf16[256,2,2048]{2,1,0:T(2,128)(2,1)}, u32[]{:S(2)}) copy-start(bf16[256,2,2048]{2,1,0:T(2,128)(2,1)} %param.17) | copy-start | bytes 6291460
  358.4 2.2 copy-start
  358.4 2.2 copy-start.12
  360.6 2.3 copy-start.4
  360.6 2.5 copy-start.5
  366.6 85.3 %copy-start.2 = (bf16[256,2048]{1,0:T(8,128)(2,1)S(1)}, bf16[256,2048]{1,0:T(8,128)(2,1)}, u32[]{:S(2)}) copy-start(bf16[256,2048]{1,0:T(8,128)(2,1)} %refs_1_.3) | copy-start | bytes 3145732
  451.9 2.3 copy-start.3
  598.4 3.5 copy-start.8
  601.9 1.7 copy-start.13
  604.3 6.7 %copy-start.9 = (f32[256,512]{1,0:T(8,128)S(1)}, f32[256,512]{1,0:T(8,128)}, u32[]{:S(2)}) copy-start(f32[256,512]{1,0:T(8,128)} %get-tuple-element.110) | copy-start | bytes 1572868
  604.3 7.5 %copy-start.7 = (f32[256,2048]{1,0:T(8,128)S(1)}, f32[256,2048]{1,0:T(8,128)}, u32[]{:S(2)}) copy-start(f32[256,2048]{1,0:T(8,128)} %get-tuple-element.113) | copy-start | bytes 6291460

commit v6 on v5

--- a/solution.py
+++ b/solution.py
@@ -10,6 +10,7 @@
 HD = 64
 SEQ_MAX = 512
 MESH = pl.DeviceIdType.MESH
+LAG = 2
 ANY = pl.BlockSpec(memory_space=pl.ANY)
 
 epsilon = 1e-05
@@ -569,14 +570,16 @@
                 after.sort(key=lambda item: -item[0][1] if item[0][0] == "grad" else 1)
             continue
         now = min([events[0][0]] * bool(events) + [units[0][0]] * bool(units))
-    return plan + [("grad", 0)]
+    return plan
 
 
 def mlp_kernel(sizes, early, wide, *refs):
-    hn_own, dy_in, wh_in, wh_own, wd_in, grad_out, y_out, dwh_out, dwd_out = refs[:9]
-    hn, dy, wh, wd, act, dgu, terms, staged, held = refs[9:18]
-    token_sems, tile_sems, wd_sems, y_sems, dw_sems, sends, recvs = refs[18:25]
-    hs, hr, ps, pr, own_sem = refs[25:]
+    hn_own, dy_in, wh_in, wh_own, wd_in = refs[:5]
+    grad_out, y_out, dwh_out, down_out, core_held, second_held, first_held = refs[5:12]
+    hn, dy, wh, wd, act, dgu, terms, staged, held, grad_staged, down_staged = refs[12:23]
+    token_sems, tile_sems, wd_sems, y_sem, dw_sems, sends, recvs = refs[23:30]
+    hs, hr, ps, pr, own_sem, grad_sems = refs[30:36]
+    inner_sems, inner_stage = refs[36:39], refs[39:]
     place = Place(*sizes)
     cols = place.cols
     width, hidden = wd.shape
@@ -584,7 +587,7 @@
     tile = hidden // tiles
     wides = width // wide
     tokens = hn.shape[1]
-    deep = wh_own.shape[1]
+    deep = wh_own.shape[0]
 
     def wide_at(n):
         return pl.ds(pl.multiple_of(n * wide, wide), wide)
@@ -603,23 +606,24 @@
         at = slice(f * tile, (f + 1) * tile)
         return pltpu.make_async_copy(wd_in.at[:, at], wd.at[:, at], wd_sems.at[f])
 
-    def tile_copy(f):
+    def tile_copies(f):
         if f < early:
-            return pltpu.make_async_copy(wh_in.at[f], wh.at[f], tile_sems.at[f])
+            return [pltpu.make_async_copy(wh_in.at[f], wh.at[f], tile_sems.at[f, 0])]
         rows = pl.ds(place.row * deep, deep)
-        return pltpu.make_async_copy(wh_own.at[f - early], wh.at[f, rows], tile_sems.at[f])
+        return [
+            pltpu.make_async_copy(
+                wh_own.at[:, pl.ds(number * hidden + f * tile, tile)],
+                wh.at[f, rows, pl.ds(number * tile, tile)],
+                tile_sems.at[f, number],
+            )
+            for number in (0, 1)
+        ]
 
     own_copy = pltpu.make_async_copy(hn_own, hn.at[place.col], own_sem)
     own_copy.start()
     for f in range(early, tiles):
-        tile_copy(f).start()
-    dy_copy(near[0]).start()
-    for f in range(tiles):
-        if f < early:
-            tile_copy(f).start()
-        wd_copy(f).start()
-    for k in range(1, cols):
-        dy_copy(near[k]).start()
+        for copy in tile_copies(f):
+            copy.start()
     place.greet(True, True)
     own_copy.wait()
     line = LineGather(place, hn.at[place.col], lambda j: hn.at[j], hs, hr)
@@ -630,11 +634,19 @@
         for f in range(early, tiles)
     }
     for f in range(early, tiles):
-        tile_copy(f).wait()
+        for copy in tile_copies(f):
+            copy.wait()
         parts[f].first()
-
-    def out_copy(slot, j):
-        return pltpu.make_async_copy(staged.at[slot], y_out.at[j], y_sems.at[slot])
+    dy_copy(near[0]).start()
+    for f in range(tiles):
+        if f < early:
+            tile_copies(f)[0].start()
+        wd_copy(f).start()
+    for k in range(1, cols):
+        dy_copy(near[k]).start()
+
+    def out_copy(j):
+        return pltpu.make_async_copy(staged, y_out.at[j], y_sem)
 
     def unit(k, f):
         j = near[k]
@@ -667,17 +679,16 @@
 
     def y_part(k):
         j = near[k]
-        slot = len(stored) % 2
-        if len(stored) >= 2:
-            out_copy(slot, near[stored[-2]]).wait()
+        if stored:
+            out_copy(near[stored[-1]]).wait()
 
         def body(n, carry):
             at = wide_at(n)
-            staged[slot, :, at] = against(act[j], wd[at]).astype(bf16)
+            staged[:, at] = against(act[j], wd[at]).astype(bf16)
             return carry
 
         lax.fori_loop(0, wides, body, 0)
-        out_copy(slot, j).start()
+        out_copy(j).start()
         stored.append(k)
 
     def late(number):
@@ -691,10 +702,13 @@
 
     calls = [(number, n) for number in range(cols - 1) for n in range(wides)]
 
+    def do_late(call):
+        number, n = call
+        piece(n).late(late(number), True)
+
     def next_late():
         if calls:
-            number, n = calls.pop(0)
-            piece(n).late(late(number), True)
+            do_late(calls.pop(0))
 
     seen_tiles, seen_chunks = set(), set()
     for step in plan_units(cols, tiles, early, 24.0, 18.0, 2.1):
@@ -711,7 +725,7 @@
             if f not in seen_tiles:
                 seen_tiles.add(f)
                 if f < early:
-                    tile_copy(f).wait()
+                    tile_copies(f)[0].wait()
                 wd_copy(f).wait()
             if k not in seen_chunks:
                 seen_chunks.add(k)
@@ -719,7 +733,7 @@
             unit(k, f)
         elif step[0] == "grad":
             grad(step[1])
-            if step[1] in (0, cols - 1):
+            if step[1] == cols - 1:
                 next_late()
         else:
             y_part(step[1])
@@ -739,38 +753,68 @@
     def down_strip(n, carry):
         at = pl.ds(pl.multiple_of(n * 256, 256), 256)
         wd[at] = dot_tokens(columns(dy, at), flat(act)).astype(bf16)
-        pltpu.make_async_copy(wd.at[at], dwd_out.at[at], dw_sems.at[0, n]).start()
         return carry
+
+    for begin, end in ((0, strips // 2), (strips // 2, strips)):
+        lax.fori_loop(begin, end, down_strip, 0)
+        next_late()
+    chunk = down_staged.shape[2]
+    inner = InnerSumInPlace(
+        place,
+        wd,
+        lambda e: down_out.at[:, pl.ds(pl.multiple_of(e * chunk, chunk), chunk)],
+        chunk,
+        (core_held, second_held, first_held, down_staged) + tuple(inner_sems),
+        inner_stage,
+    )
+    inner.begin()
+    grad(0)
+    beside = []
+    for number in ((1, 3) + (2,) * strips)[:strips]:
+        beside.append(calls[:number])
+        del calls[:number]
 
     def hidden_strip(n, carry):
         at = pl.ds(pl.multiple_of(n * 256, 256), 256)
-        result = dot_tokens(columns(hn, at), flat(dgu)).astype(bf16)
+        left = columns(hn, at)
         for f in range(tiles):
-            wh[f, at] = result[:, 2 * f * tile : 2 * (f + 1) * tile]
-        pltpu.make_async_copy(wh.at[:, at], dwh_out.at[:, at], dw_sems.at[1, n]).start()
+            span = slice(2 * f * tile, 2 * (f + 1) * tile)
+            right = dgu[:, :, span].reshape(cols * tokens, 2 * tile)
+            wh[f, at] = dot_tokens(left, right).astype(bf16)
+        pltpu.make_async_copy(wh.at[:, at], dwh_out.at[:, at], dw_sems.at[n]).start()
+        inner.tick(n)
+        for number, some in enumerate(beside):
+            for call in some:
+                pl.when(n == number)(functools.partial(do_late, call))
         return carry
 
-    for begin, end in ((0, strips // 2), (strips // 2, strips)):
-        lax.fori_loop(begin, end, down_strip, 0)
-        if begin == 0:
-            next_late()
-    for begin, end in ((0, 1), (1, 3), (3, 5), (5, 7), (7, strips)):
-        lax.fori_loop(begin, end, hidden_strip, 0)
-        next_late()
+    lax.fori_loop(0, strips, hidden_strip, 0)
+    for t in range(strips, inner.count + 2 * LAG):
+        inner.tick(t)
     while calls:
         next_late()
+
+    def grad_copy(n):
+        return pltpu.make_async_copy(
+            grad_staged.at[n % 2], grad_out.at[:, wide_at(n)], grad_sems.at[n % 2]
+        )
+
     for n in range(wides):
-        piece(n).last(grad_out.at[:, wide_at(n)])
-    for number in range(max(cols - 2, 0), cols):
-        out_copy(number % 2, near[stored[number]]).wait()
+        if n >= 2:
+            grad_copy(n - 2).wait()
+        piece(n).last(grad_staged.at[n % 2])
+        grad_copy(n).start()
+    for n in range(max(wides - 2, 0), wides):
+        grad_copy(n).wait()
+    out_copy(near[stored[-1]]).wait()
 
     def finish(n, carry):
         at = pl.ds(pl.multiple_of(n * 256, 256), 256)
-        pltpu.make_async_copy(wd.at[at], dwd_out.at[at], dw_sems.at[0, n]).wait()
-        pltpu.make_async_copy(wh.at[:, at], dwh_out.at[:, at], dw_sems.at[1, n]).wait()
+        pltpu.make_async_copy(wh.at[:, at], dwh_out.at[:, at], dw_sems.at[n]).wait()
         return carry
 
     lax.fori_loop(0, strips, finish, 0)
+    inner.finish()
     line.finish()
     for n in range(wides):
         piece(n).finish()
@@ -780,25 +824,34 @@
     steps = max(col_count - 1, 1)
     rows, width = hn.shape
     hidden = wd.shape[1]
-    early, left = wh.shape[0], wh_own.shape[0]
-    tiles = early + left
-    tile = hidden // tiles
+    early, tile = wh.shape[0], wh.shape[2] // 2
+    tiles = hidden // tile
+    left = tiles - early
     wide = min(512, width)
     shape = (col_count, rows, width)
-    vmem = pl.BlockSpec(memory_space=pltpu.VMEM)
     total = col_count * rows
     wh_shape = (tiles, width, 2 * tile)
-    plane_sems = (left, 2, PlaneGather.sem_count(plane_sizes(row_count)))
-    grad, y, dwh, dwd = pl.pallas_call(
+    plane = plane_sizes(row_count)
+    plane_sems = (left, 2, PlaneGather.sem_count(plane))
+    deep = width // row_count
+    chunk = min(512, hidden)
+    count = hidden // chunk
+    inner_sems = InnerSum.sems(plane, count)
+    inner_sems[0] = pltpu.SemaphoreType.DMA((2, count, plane[0] * plane[1]))
+    grad, y, dwh, sum_down, *_ = pl.pallas_call(
         functools.partial(mlp_kernel, (row_count, col_count), early, wide),
         out_shape=[
             jax.ShapeDtypeStruct((rows, width), f32),
             jax.ShapeDtypeStruct(shape, bf16),
             jax.ShapeDtypeStruct(wh_shape, bf16),
-            jax.ShapeDtypeStruct(wd.shape, bf16),
+            jax.ShapeDtypeStruct((deep, hidden), f32),
+        ]
+        + [
+            jax.ShapeDtypeStruct(held, bf16)
+            for held in InnerSum.held_shapes(plane, deep, hidden, chunk)
         ],
         in_specs=[ANY] * 5,
-        out_specs=[vmem, ANY, ANY, ANY],
+        out_specs=[ANY] * 7,
         scratch_shapes=[
             pltpu.VMEM(shape, bf16),
             pltpu.VMEM(shape, bf16),
@@ -807,13 +860,15 @@
             pltpu.VMEM((col_count, rows, hidden), bf16),
             pltpu.VMEM((col_count, rows, 2 * hidden), bf16),
             pltpu.VMEM(shape, bf16),
-            pltpu.VMEM((2, rows, width), bf16),
+            pltpu.VMEM((rows, width), bf16),
             pltpu.VMEM((width // wide, 2, steps, rows, wide), bf16),
+            pltpu.VMEM((2, rows, wide), f32),
+            pltpu.VMEM((2, deep, chunk), f32),
             pltpu.SemaphoreType.DMA((col_count,)),
+            pltpu.SemaphoreType.DMA((tiles, 2)),
             pltpu.SemaphoreType.DMA((tiles,)),
-            pltpu.SemaphoreType.DMA((tiles,)),
-            pltpu.SemaphoreType.DMA((2,)),
-            pltpu.SemaphoreType.DMA((2, width // 256)),
+            pltpu.SemaphoreType.DMA,
+            pltpu.SemaphoreType.DMA((width // 256,)),
             pltpu.SemaphoreType.DMA((width // wide, 2, steps)),
             pltpu.SemaphoreType.DMA((width // wide, 2, steps)),
             pltpu.SemaphoreType.DMA((2, steps)),
@@ -821,7 +876,10 @@
             pltpu.SemaphoreType.DMA(plane_sems),
             pltpu.SemaphoreType.DMA(plane_sems),
             pltpu.SemaphoreType.DMA,
-        ],
+            pltpu.SemaphoreType.DMA((2,)),
+        ]
+        + inner_sems
+        + InnerSumInPlace.stage_scratch(plane, deep, chunk),
         compiler_params=pltpu.CompilerParams(
             collective_id=collective_id, has_side_effects=True, vmem_limit_bytes=63 << 20
         ),
@@ -832,15 +890,15 @@
         ),
         name="feed_forward",
     )(hn, dy.reshape(shape), wh, wh_own, wd)
-    return grad, y.reshape(total, width), dwh, dwd
+    return grad, y.reshape(total, width), dwh, sum_down
 
 
 class PlaneSum:
-    def __init__(self, place, acc, held_core, held_second, held_first, sems):
-        self.place, self.acc = place, acc
-        self.held = (held_first, held_second, held_core)
+    def __init__(self, place, block, held_second, held_first, sems, stage=None):
+        self.place, self.block = place, block
+        self.held = (held_first, held_second)
         self.sends, self.recvs = sems
-        self.half_deep = acc.shape[1] // 2
+        self.stage = stage
 
     @staticmethod
     def counts_of(sizes):
@@ -862,33 +920,49 @@
     def part(self, half, i, j):
         first, second = self.axes(half)
         at = self.place.moved(second, j, self.place.moved(first, i))
-        return self.acc.at[
-            self.place.chip_of(at), pl.ds(half * self.half_deep, self.half_deep)
-        ]
+        return self.block(self.place.chip_of(at), half)
+
+    def number(self, half, kind, step, i):
+        return (step - 1) * self.counts(half)[0] + i if kind == 1 else step - 1
 
     def copy(self, half, kind, step, i):
         np_, nq = self.counts(half)
+        number = self.number(half, kind, step, i)
         if kind == 1:
-            number = (step - 1) * np_ + i
-            source = self.part(half, i, nq - step)
-            target = self.held[1].at[half, number]
-            sem = number
+            source, sem = self.part(half, i, nq - step), number
         else:
-            source = self.part(half, np_ - step, 0)
-            target = self.held[0].at[half, step - 1]
-            sem = (nq - 1) * np_ + step - 1
+            source, sem = self.part(half, np_ - step, 0), (nq - 1) * np_ + number
+        target = self.held[kind].at[half, number]
         device = self.place.device(self.axes(half)[1 if kind == 1 else 0], 1)
         return remote(source, target, self.sends.at[half, sem], self.recvs.at[half, sem], device)
 
-    def add(self, half, kind, step, i):
-        np_, nq = self.counts(half)
-        self.copy(half, kind, step, i).wait_recv()
-        if kind == 1:
-            add_rows(
-                self.part(half, i, nq - step - 1), self.held[1].at[half, (step - 1) * np_ + i]
-            )
-        else:
-            add_rows(self.part(half, np_ - step - 1, 0), self.held[0].at[half, step - 1])
+    def bring(self, half, kind, step, i):
+        number = self.number(half, kind, step, i)
+        return pltpu.make_async_copy(
+            self.held[kind].at[half, number],
+            self.stage[kind].at[half, number],
+            self.stage[2 + kind].at[half, number],
+        )
+
+    def add(self, pieces):
+        if self.stage is not None:
+            for piece in pieces:
+                self.copy(*piece).wait_recv()
+                self.bring(*piece).start()
+        for half, kind, step, i in pieces:
+            np_, nq = self.counts(half)
+            if self.stage is None:
+                self.copy(half, kind, step, i).wait_recv()
+                held = self.held[kind]
+            else:
+                self.bring(half, kind, step, i).wait()
+                held = self.stage[kind]
+            if kind == 1:
+                target = self.part(half, i, nq - step - 1)
+            else:
+                target = self.part(half, np_ - step - 1, 0)
+            add_rows(target, held.at[half, self.number(half, kind, step, i)])
+            yield half, i
 
     def first(self):
         for half in (0, 1):
@@ -900,22 +974,26 @@
     def second(self):
         for half in (0, 1):
             np_, nq = self.counts(half)
-            for step in range(1, nq):
-                for i in range(np_ - 1, -1, -1):
-                    self.add(half, 1, step, i)
-                    if step < nq - 1:
-                        self.copy(half, 1, step + 1, i).start()
-                    elif i == np_ - 1 and np_ > 1:
-                        self.copy(half, 0, 1, 0).start()
             if nq == 1 and np_ > 1:
                 self.copy(half, 0, 1, 0).start()
+        for step in range(1, max(self.place.sizes[:2])):
+            pieces = []
+            for half in (0, 1):
+                np_, nq = self.counts(half)
+                if step < nq:
+                    pieces += [(half, 1, step, i) for i in range(np_ - 1, -1, -1)]
+            for half, i in self.add(pieces):
+                np_, nq = self.counts(half)
+                if step < nq - 1:
+                    self.copy(half, 1, step + 1, i).start()
+                elif i == np_ - 1 and np_ > 1:
+                    self.copy(half, 0, 1, 0).start()
 
     def third(self):
-        for half in (0, 1):
-            np_, _ = self.counts(half)
-            for step in range(1, np_):
-                self.add(half, 0, step, 0)
-                if step < np_ - 1:
+        for step in range(1, max(self.place.sizes[:2])):
+            pieces = [(half, 0, step, 0) for half in (0, 1) if step < self.counts(half)[0]]
+            for half, _ in self.add(pieces):
+                if step < self.counts(half)[0] - 1:
                     self.copy(half, 0, step + 1, 0).start()
 
     def finish(self):
@@ -928,6 +1006,11 @@
                 self.copy(half, 0, step, 0).wait_send()
 
 
+def halves_of(acc):
+    half = acc.shape[1] // 2
+    return lambda chip, number: acc.at[chip, pl.ds(number * half, half)]
+
+
 def core_rows(place, chip, step, deep):
     cores = place.sizes[2]
     row = chip * cores + lax.rem(place.at[2] + step, cores)
@@ -938,49 +1021,69 @@
     def __init__(self, place, count, terms, target, refs):
         self.place, self.count, self.terms, self.target = place, count, terms, target
         self.acc, self.core_held, self.second, self.first, self.staged = refs[:5]
-        self.load_sems, self.core_sems, self.plane_sems, self.out_sems = refs[5:]
+        self.load_sems, self.core_sems, self.plane_sems, self.out_sems = refs[5:9]
         self.ahead = min(3, self.count)
+        self.chips, self.deep = self.core_held.shape[1:3]
+        self.stage = None
+
+    @staticmethod
+    def held_shapes(sizes, deep, width, chunk):
+        na, nb, _ = sizes
+        firsts, seconds = PlaneSum.counts_of(sizes)
+        return [
+            (width // chunk, na * nb, deep, chunk),
+            (width // chunk, 2, max(seconds, 1), deep // 2, chunk),
+            (width // chunk, 2, max(firsts, 1), deep // 2, chunk),
+        ]
+
+    @staticmethod
+    def sems(sizes, count):
+        return [
+            pltpu.SemaphoreType.DMA((2, count)),
+            pltpu.SemaphoreType.DMA((2, count, 2, max(PlaneSum.sem_count(sizes), 1))),
+            pltpu.SemaphoreType.DMA((2,)),
+        ]
 
     @staticmethod
     def scratch(sizes, deep, width, chunk):
-        na, nb, _ = sizes
+        shapes = InnerSum.held_shapes(sizes, deep, width, chunk)
         count = width // chunk
-        firsts, seconds = PlaneSum.counts_of(sizes)
-        sems = (2, count, 2, max(PlaneSum.sem_count(sizes), 1))
-        return [
-            pltpu.VMEM((count, na * nb, deep, chunk), bf16),
-            pltpu.VMEM((count, na * nb, deep, chunk), bf16),
-            pltpu.VMEM((count, 2, max(seconds, 1), deep // 2, chunk), bf16),
-            pltpu.VMEM((count, 2, max(firsts, 1), deep // 2, chunk), bf16),
-            pltpu.VMEM((2, deep, chunk), f32),
-            pltpu.SemaphoreType.DMA((count,)),
-            pltpu.SemaphoreType.DMA((2, count)),
-            pltpu.SemaphoreType.DMA(sems),
-            pltpu.SemaphoreType.DMA((2,)),
-        ]
+        return (
+            [pltpu.VMEM(shape, bf16) for shape in shapes[:1] + shapes]
+            + [pltpu.VMEM((2, deep, chunk), f32), pltpu.SemaphoreType.DMA((count,))]
+            + InnerSum.sems(sizes, count)
+        )
 
     def load(self, e):
         source = self.terms(e, self.place.at[2])
         return pltpu.make_async_copy(source, self.acc.at[e], self.load_sems.at[e])
 
-    def share(self, e):
-        other = lax.rem(self.place.at[2] + 1, self.place.sizes[2])
-        return remote(
-            self.terms(e, other),
-            self.core_held.at[e],
-            self.core_sems.at[0, e],
-            self.core_sems.at[1, e],
-            self.place.device(2, 1),
-        )
+    def other(self):
+        return lax.rem(self.place.at[2] + 1, self.place.sizes[2])
+
+    def shares(self, e):
+        return [
+            remote(
+                self.terms(e, self.other()),
+                self.core_held.at[e],
+                self.core_sems.at[0, e],
+                self.core_sems.at[1, e],
+                self.place.device(2, 1),
+            )
+        ]
+
+    def block(self, e, chip):
+        return self.acc.at[e, chip]
 
     def inside(self, e):
+        half = self.deep // 2
         return PlaneSum(
             self.place,
-            self.acc.at[e],
-            self.core_held.at[e],
+            lambda chip, number: self.block(e, chip).at[pl.ds(number * half, half)],
             self.second.at[e],
             self.first.at[e],
             (self.plane_sems.at[0, e], self.plane_sems.at[1, e]),
+            self.stage,
         )
 
     def out_copy(self, e):
@@ -992,19 +1095,26 @@
     def prepare(self, e):
         self.load(e).start()
         if self.place.sizes[2] > 1:
-            self.share(e).start()
+            for share in self.shares(e):
+                share.start()
 
     def begin(self):
         for e in range(self.ahead):
             self.prepare(e)
 
+    def ready(self, e):
+        self.load(e).wait()
+        if self.place.sizes[2] > 1:
+            for share in self.shares(e):
+                share.wait_recv()
+        return self.core_held.at[e]
+
     def start(self, e):
         when(e + self.ahead < self.count, lambda: self.prepare(e + self.ahead))
-        self.load(e).wait()
+        held = self.ready(e)
         if self.place.sizes[2] > 1:
-            self.share(e).wait_recv()
-            for chip in range(self.acc.shape[1]):
-                add_rows(self.acc.at[e, chip], self.core_held.at[e, chip])
+            for chip in range(self.chips):
+                add_rows(self.block(e, chip), held.at[chip])
         self.inside(e).first()
 
     def middle(self, e):
@@ -1014,14 +1124,14 @@
         self.inside(e).third()
         when(e >= 2, lambda: self.out_copy(e - 2).wait())
         slot = lax.rem(e, 2)
-        own = self.acc.at[e, self.place.chip_of(self.place.at)]
+        own = self.block(e, self.place.chip_of(self.place.at))
         self.staged[slot] = own[...].astype(f32)
         self.out_copy(e).start()
 
     def tick(self, t):
-        when(t < self.count, lambda: self.start(t))
-        when((t >= 1) & (t - 1 < self.count), lambda: self.middle(t - 1))
-        when((t >= 2) & (t - 2 < self.count), lambda: self.close(t - 2))
+        for lag, action in ((0, self.start), (LAG, self.middle), (2 * LAG, self.close)):
+            e = t - lag
+            when((e >= 0) & (e < self.count), functools.partial(action, e))
 
     def finish(self):
         for e in range(max(self.count - 2, 0), self.count):
@@ -1029,11 +1139,74 @@
 
         def done(e, carry):
             if self.place.sizes[2] > 1:
-                self.share(e).wait_send()
+                for share in self.shares(e):
+                    share.wait_send()
             self.inside(e).finish()
             return carry
 
         lax.fori_loop(0, self.count, done, 0)
+
+
+class InnerSumInPlace(InnerSum):
+    def __init__(self, place, terms, target, chunk, refs, stage):
+        self.place, self.terms, self.target, self.chunk = place, terms, target, chunk
+        self.core_held, self.second, self.first, self.staged = refs[:4]
+        self.core_sems, self.plane_sems, self.out_sems = refs[4:]
+        self.count = terms.shape[1] // chunk
+        self.ahead = self.count
+        self.chips, self.deep = self.core_held.shape[1:3]
+        self.core_stage, self.core_stage_sem = stage[:2]
+        self.stage = stage[2:]
+
+    @staticmethod
+    def stage_scratch(sizes, deep, chunk):
+        shapes = InnerSum.held_shapes(sizes, deep, chunk, chunk)
+        return [
+            pltpu.VMEM(shapes[0][1:], bf16),
+            pltpu.SemaphoreType.DMA,
+            pltpu.VMEM(shapes[2][1:], bf16),
+            pltpu.VMEM(shapes[1][1:], bf16),
+            pltpu.SemaphoreType.DMA(shapes[2][1:3]),
+            pltpu.SemaphoreType.DMA(shapes[1][1:3]),
+        ]
+
+    def rows(self, e, chip, core):
+        row = chip * self.place.sizes[2] + core
+        return self.terms.at[
+            pl.ds(pl.multiple_of(row * self.deep, self.deep), self.deep),
+            pl.ds(pl.multiple_of(e * self.chunk, self.chunk), self.chunk),
+        ]
+
+    def block(self, e, chip):
+        return self.rows(e, chip, self.place.at[2])
+
+    def shares(self, e):
+        return [
+            remote(
+                self.rows(e, chip, self.other()),
+                self.core_held.at[e, chip],
+                self.core_sems.at[0, e, chip],
+                self.core_sems.at[1, e, chip],
+                self.place.device(2, 1),
+            )
+            for chip in range(self.chips)
+        ]
+
+    def prepare(self, e):
+        if self.place.sizes[2] > 1:
+            for share in self.shares(e):
+                share.start()
+
+    def ready(self, e):
+        if self.place.sizes[2] > 1:
+            for share in self.shares(e):
+                share.wait_recv()
+            copy = pltpu.make_async_copy(
+                self.core_held.at[e], self.core_stage, self.core_stage_sem
+            )
+            copy.start()
+            copy.wait()
+        return self.core_stage
 
 
 class SmallSum:
@@ -1114,41 +1287,54 @@
         self.total[...] = total
 
 
-def sum_kernel(sizes, count, chunk, *refs):
+def norm_rows(dxn, x, dh, gain, out, part):
+    rows, width = x.shape
+    piece = 32
+
+    def body(n, carry):
+        at = pl.ds(pl.multiple_of(n * piece, piece), piece)
+        values = x[at].astype(f32)
+        scale = lax.rsqrt(jnp.mean(values * values, axis=1, keepdims=True) + epsilon)
+        grad = dxn[at]
+        weighted = grad * gain[...]
+        inner = jnp.mean(weighted * values, axis=1, keepdims=True)
+        result = dh[at] + scale * weighted - values * (scale * scale * scale) * inner
+        out[at] = result.astype(out.dtype)
+        part[0:1] += jnp.sum(grad * values * scale, axis=0, keepdims=True)
+        return carry
+
+    part[0:1] = jnp.zeros((1, width), f32)
+    lax.fori_loop(0, rows // piece, body, 0)
+
+
+def add_out(hidden, term, out):
+    rows = hidden.shape[0]
+    piece = 32
+
+    def body(n, carry):
+        at = pl.ds(pl.multiple_of(n * piece, piece), piece)
+        out[at] = (hidden[at] + term[at].astype(f32)).astype(out.dtype)
+        return carry
+
+    lax.fori_loop(0, rows // piece, body, 0)
+
+
+def sum_kernel(sizes, count, *refs):
     row_count, col_count = sizes
     place = Place(row_count, col_count)
     cores = place.sizes[2]
     lefts, rights = refs[: cores * count], refs[cores * count : 2 * cores * count]
     refs = refs[2 * cores * count :]
-    inner_terms, act_terms, small = refs[:3]
-    outs = refs[3 : 3 + count]
-    inner_out, act_out, small_out = refs[3 + count : 6 + count]
-    refs = refs[6 + count :]
+    dxn, x, dh, gain, hidden, out_sum, mid_part = refs[:7]
+    outs = refs[7 : 8 + count]
+    tokens_out, block_out, small_out = refs[8 + count : 11 + count]
+    refs = refs[11 + count :]
     per = [refs[7 * n : 7 * n + 7] for n in range(count)]
-
-    def inner_columns(e):
-        return pl.ds(pl.multiple_of(e * chunk, chunk), chunk)
-
-    inner = InnerSum(
-        place,
-        inner_out.shape[1] // chunk,
-        lambda e, core: inner_terms.at[:, core, :, inner_columns(e)],
-        lambda e: inner_out.at[:, inner_columns(e)],
-        refs[7 * count : 7 * count + 9],
-    )
-    act_held, load_sems, out_sems, ps, pr, zs, zr = refs[7 * count + 9 : 7 * count + 16]
-    ring_held, line_held, ring_sems, line_sems, chip_sems = refs[7 * count + 16 :]
-    token_rows = act_out.shape[0]
+    load_sems, out_sems, ps, pr, zs, zr = refs[7 * count : 7 * count + 6]
+    ring_held, line_held, ring_sems, line_sems, chip_sems, small = refs[7 * count + 6 :]
 
     entries = [(n, nearby(place, k)) for k in range(col_count - 1, -1, -1) for n in range(count)]
 
-    acts = LineSum(
-        place,
-        lambda j: act_terms.at[pl.ds(pl.multiple_of(j * token_rows, token_rows), token_rows)],
-        act_held,
-        zs.at[count],
-        zr.at[count],
-    )
     acc = [per[n][0] for n in range(count)]
     lines = [
         LineSum(
@@ -1186,21 +1372,18 @@
     for copy in loads():
         copy.start()
     place.greet(True, True)
-    inner.begin()
-    act_order = [nearby(place, k) for k in range(col_count - 1, 0, -1)]
-    act_early, act_late = list(act_order), list(act_order)
-    acts.early(act_early.pop(0), True) if act_early else None
     smalls = SmallSum(place, small, small_out, ring_held, line_held, ring_sems, line_sems)
-    smalls.begin()
-    stages = list(smalls.stages)
+    stages = [functools.partial(norm_rows, dxn, x, dh, gain, tokens_out, small)]
+    stages += [functools.partial(add_out, hidden, out_sum, block_out), smalls.begin]
+    stages += smalls.stages
+    small[1:2] = mid_part[...]
     for copy in loads():
         copy.wait()
 
     def inside(n, col):
         return PlaneSum(
             place,
-            acc[n].at[col],
-            None,
+            halves_of(acc[n].at[col]),
             per[n][1].at[col],
             per[n][2].at[col],
             (ps.at[n, col], pr.at[n, col]),
@@ -1208,12 +1391,9 @@
 
     parts = [inside(n, col) for n, col in entries]
     final = len(entries) - count
-    total = len(entries) + inner.count
+    total = len(entries)
 
     def start(number):
-        if number >= len(entries):
-            inner.start(number - len(entries))
-            return
         n, col = entries[number]
         left, right = per[n][5], per[n][6]
         deep = acc[n].shape[2]
@@ -1226,79 +1406,66 @@
         lax.fori_loop(0, acc[n].shape[1], chip_rows, 0)
         parts[number].first()
 
-    def middle(number):
-        if number >= len(entries):
-            inner.middle(number - len(entries))
-        else:
-            parts[number].second()
-
-    def out_copy(n):
-        return pltpu.make_async_copy(per[n][4], outs[n], out_sems.at[n])
+    split = outs[0].shape[1]
+
+    def out_copies(n):
+        if n > 0:
+            return [pltpu.make_async_copy(per[n][4], outs[n + 1], out_sems.at[n + 1])]
+        rest = pl.ds(split, outs[1].shape[1])
+        return [
+            pltpu.make_async_copy(per[0][4].at[:, pl.ds(0, split)], outs[0], out_sems.at[0]),
+            pltpu.make_async_copy(per[0][4].at[:, rest], outs[1], out_sems.at[1]),
+        ]
 
     def close(number):
-        if number >= len(entries):
-            inner.close(number - len(entries))
-            if number == len(entries) + 1 or total == len(entries) + 1:
-                finish_lines()
-            return
         parts[number].third()
         n, col = entries[number]
         if number < final:
             lines[n].early(col, True)
-        if number >= 2 * count:
-            waiting.pop(0)()
-
-    waiting = [functools.partial(lines[n].late, col, True) for n, col in entries[:final]]
+            if number >= count:
+                lines[n].late(entries[number - count][1], True)
+            if number >= final - count:
+                lines[n].late(col, True)
 
     def finish_lines():
-        while waiting:
-            waiting.pop(0)()
         for n in range(count):
             lines[n].last(per[n][4])
-            out_copy(n).start()
-
-    for number in range(total + 2):
+            for copy in out_copies(n):
+                copy.start()
+
+    for number in range(total + 2 * LAG):
         if number < total:
             start(number)
-        if 1 <= number <= total:
-            middle(number - 1)
-        if 2 <= number:
-            close(number - 2)
-        if act_early and number % 2 == 1:
-            acts.early(act_early.pop(0), True)
-        if act_late and number >= 3 and number % 2 == 1:
-            acts.late(act_late.pop(0), True)
-        if stages:
-            stages.pop(0)()
+        if LAG <= number < total + LAG:
+            parts[number - LAG].second()
+        if 2 * LAG <= number:
+            close(number - 2 * LAG)
+        if number >= 1:
+            for stage in stages[:2]:
+                stage()
+            del stages[:2]
     for stage in stages:
         stage()
-    for col in act_early:
-        acts.early(col, True)
-    for col in act_late:
-        acts.late(col, True)
-    acts.last(act_out)
+    finish_lines()
     for n in range(count):
-        out_copy(n).wait()
+        for copy in out_copies(n):
+            copy.wait()
     for part in parts:
         part.finish()
-    inner.finish()
-    for line in lines + [acts]:
+    for line in lines:
         line.finish()
 
 
-def sum_all(lefts, rights, inner_terms, act_terms, small, row_count, col_count, act_type):
+def sum_all(lefts, rights, split, extras, row_count, col_count):
     count = len(rights)
     sizes = plane_sizes(row_count)
     na, nb, nk = sizes
     chips = na * nb
-    tokens = lefts[0][0].shape[0]
+    tokens, model = lefts[0][0].shape
     deep = lefts[0][0].shape[1] // row_count
     steps = max(col_count - 1, 1)
     firsts, seconds = PlaneSum.counts_of(sizes)
     widths = [right[0].shape[2] for right in rights]
-    token_rows = act_terms.shape[0] // col_count
-    inner_width = inner_terms.shape[1]
-    chunk = min(512, inner_width)
     scratch = []
     for width in widths:
         scratch += [
@@ -1310,48 +1477,46 @@
             pltpu.VMEM((nk * tokens, chips * deep), bf16),
             pltpu.VMEM((col_count, nk * tokens, width), bf16),
         ]
-    scratch += InnerSum.scratch(sizes, deep, inner_width, chunk)
     plane_sems = (count, col_count, 2, max(PlaneSum.sem_count(sizes), 1))
     scratch += [
-        pltpu.VMEM((2, steps, token_rows, act_terms.shape[1]), bf16),
         pltpu.SemaphoreType.DMA((2, count * nk)),
-        pltpu.SemaphoreType.DMA((count,)),
+        pltpu.SemaphoreType.DMA((count + 1,)),
         pltpu.SemaphoreType.DMA(plane_sems),
         pltpu.SemaphoreType.DMA(plane_sems),
-        pltpu.SemaphoreType.DMA((count + 1, 2, steps)),
-        pltpu.SemaphoreType.DMA((count + 1, 2, steps)),
-        pltpu.VMEM((3, max(sizes)) + small.shape, f32),
-        pltpu.VMEM((col_count,) + small.shape, f32),
+        pltpu.SemaphoreType.DMA((count, 2, steps)),
+        pltpu.SemaphoreType.DMA((count, 2, steps)),
+        pltpu.VMEM((3, max(sizes), 2, model), f32),
+        pltpu.VMEM((col_count, 2, model), f32),
         pltpu.SemaphoreType.DMA((2, 3, max(max(sizes) - 1, 1))),
         pltpu.SemaphoreType.DMA((2, 2, steps)),
         pltpu.SemaphoreType.DMA((count, chips)),
+        pltpu.VMEM((2, model), f32),
     ]
+    outs = [split, widths[0] - split] + widths[1:]
     vmem = pl.BlockSpec(memory_space=pltpu.VMEM)
     flops = sum(2 * nk * tokens * chips * deep * width * col_count for width in widths)
     return pl.pallas_call(
-        functools.partial(sum_kernel, (row_count, col_count), count, chunk),
-        out_shape=[jax.ShapeDtypeStruct((deep, width), f32) for width in widths]
+        functools.partial(sum_kernel, (row_count, col_count), count),
+        out_shape=[jax.ShapeDtypeStruct((deep, width), f32) for width in outs]
         + [
-            jax.ShapeDtypeStruct((deep, inner_width), f32),
-            jax.ShapeDtypeStruct((token_rows, act_terms.shape[1]), act_type),
-            jax.ShapeDtypeStruct(small.shape, f32),
+            jax.ShapeDtypeStruct((tokens, model), bf16),
+            jax.ShapeDtypeStruct((tokens, model), bf16),
+            jax.ShapeDtypeStruct((2, model), f32),
         ],
-        in_specs=[ANY] * (2 * count * nk) + [ANY, vmem, vmem],
-        out_specs=[ANY] * (count + 1) + [vmem, vmem],
+        in_specs=[ANY] * (2 * count * nk) + [vmem] * 7,
+        out_specs=[ANY] * (count + 1) + [vmem] * 3,
         scratch_shapes=scratch,
         compiler_params=pltpu.CompilerParams(
             collective_id=1, has_side_effects=True, vmem_limit_bytes=63 << 20
         ),
         cost_estimate=pl.CostEstimate(
-            flops=flops, bytes_accessed=inner_terms.size * 2, transcendentals=0
+            flops=flops, bytes_accessed=flops // 256, transcendentals=0
         ),
         name="sum_weights",
     )(
         *[left for pair in lefts for left in pair],
         *[right for pair in rights for right in pair],
-        inner_terms.reshape(chips, nk, deep, inner_width),
-        act_terms,
-        small,
+        *extras,
     )
 
 
@@ -1394,9 +1559,10 @@
 
 
 def attend_kernel(sizes, heads, group, back, *refs):
-    xn, x, wf_in, wo_in, bias, cosq, sinq, coskv, sinkv, gain, tiles = refs[:11]
+    xn, x, wf_in, wo_in, bias, cosq, sinq, coskv, sinkv, gain, tiles_in = refs[:11]
     q_out, kv_out, mixed_out, lse_out, full_tiles, hidden, hn = refs[11:18]
-    q, kv, mixed, lse, wf, wo, w_sems, o_sems, sends, recvs, t_sems, ps, pr = refs[18:]
+    q, kv, mixed, lse, wf, wo, w_sems, o_sems, sends, recvs, t_sems, ps, pr = refs[18:31]
+    tiles, tiles_sem = refs[31:]
     place = Place(*sizes)
     cols, col = place.cols, place.col
     tokens = xn.shape[0]
@@ -1410,9 +1576,20 @@
             pltpu.make_async_copy(wo_in.at[z], wo.at[z], w_sems.at[1, z]),
         )
 
-    for number in (0, 1):
-        for z in range(cols):
-            weight_copies(z)[number].start()
+    count, _, tile = tiles.shape
+    tile = tile // 2
+    hidden_units = tiles_in.shape[1] // 2
+    fetches = [
+        pltpu.make_async_copy(
+            tiles_in.at[:, pl.ds(number * hidden_units + f * tile, tile)],
+            tiles.at[f, :, pl.ds(number * tile, tile)],
+            tiles_sem.at[f, number],
+        )
+        for f in range(count)
+        for number in (0, 1)
+    ]
+    for fetch in fetches:
+        fetch.start()
     for step in range(1, back + 1):
 
         @pl.when(col < step)
@@ -1429,15 +1606,20 @@
         )
         for f in range(tiles.shape[0])
     ]
-    for keep in keeps:
-        keep.start()
     place.greet(True, True)
+    for fetch in fetches:
+        fetch.wait()
     parts = [
         tile_gather(place, full_tiles.at[f], tiles.at[f], ps.at[f], pr.at[f])
         for f in range(tiles.shape[0])
     ]
     for part in parts:
         part.first()
+    for number in (0, 1):
+        for z in range(cols):
+            weight_copies(z)[number].start()
+    for keep in keeps:
+        keep.start()
 
     def hop(z, step):
         source = kv.at[z, pl.ds((back - step + 1) * tokens, tokens)]
@@ -1548,8 +1730,9 @@
 
 
 def attend(
-    xn, x, wf, wo, bias, tables, gain, tiles, heads, group, back, row_count, col_count, cid
+    xn, x, wf, wo, bias, tables, gain, tiles, count, tile, heads, group, back, sizes, cid
 ):
+    row_count, col_count = sizes
     tokens, width = xn.shape
     query_width = heads * HD
     kv_shape = (col_count, (back + 1) * tokens, heads // group * LANES)
@@ -1557,7 +1740,6 @@
     lse_shape = (col_count, heads, tokens)
     vmem = pl.BlockSpec(memory_space=pltpu.VMEM)
     keys = (back + 1) * tokens
-    count = tiles.shape[0]
     plane_sems = (count, 2, PlaneGather.sem_count(plane_sizes(row_count)))
     return pl.pallas_call(
         functools.partial(attend_kernel, (row_count, col_count), heads, group, back),
@@ -1566,11 +1748,11 @@
             jax.ShapeDtypeStruct(kv_shape, bf16),
             jax.ShapeDtypeStruct(q_shape, bf16),
             jax.ShapeDtypeStruct(lse_shape, f32),
-            jax.ShapeDtypeStruct((count, row_count * tiles.shape[1], tiles.shape[2]), bf16),
+            jax.ShapeDtypeStruct((count, row_count * tiles.shape[0], 2 * tile), bf16),
             jax.ShapeDtypeStruct((tokens, width), f32),
             jax.ShapeDtypeStruct((tokens, width), bf16),
         ],
-        in_specs=[vmem, vmem, ANY, ANY] + [vmem] * 7,
+        in_specs=[vmem, vmem, ANY, ANY] + [vmem] * 6 + [ANY],
         out_specs=[ANY] * 5 + [vmem] * 2,
         scratch_shapes=[
             pltpu.VMEM(q_shape, bf16),
@@ -1586,6 +1768,8 @@
             pltpu.SemaphoreType.DMA((count,)),
             pltpu.SemaphoreType.DMA(plane_sems),
             pltpu.SemaphoreType.DMA(plane_sems),
+            pltpu.VMEM((count, tiles.shape[0], 2 * tile), bf16),
+            pltpu.SemaphoreType.DMA((count, 2)),
         ],
         compiler_params=pltpu.CompilerParams(
             collective_id=cid, has_side_effects=True, vmem_limit_bytes=56 << 20
@@ -1757,7 +1941,7 @@
         return carry
 
     lax.fori_loop(0, cols, one_col, 0)
-    ticks = list(range(cols * pairs, inner.count + 2))
+    ticks = list(range(cols * pairs, inner.count + 2 * LAG))
     for z in range(cols, cols + back):
         if ticks:
             inner.tick(ticks.pop(0))
@@ -1970,8 +2154,7 @@
     tile = min(512, hidden)
     tiles = hidden // tile
     early = max(tiles // 2, 1)
-    hidden_tiles = jnp.transpose(hidden_weight.reshape(deep, 2, tiles, tile), (2, 0, 1, 3))
-    hidden_tiles = hidden_tiles.reshape(tiles, deep, 2 * tile)
+    hidden_flat = hidden_weight.reshape(deep, 2 * hidden)
 
     inputs = tokens.astype(f32)
     normal_in, scale_in = normalize(inputs, gain_first)
@@ -1992,26 +2175,28 @@
         bias,
         tables,
         gain_second[None],
-        hidden_tiles[:early],
+        hidden_flat,
+        early,
+        tile,
         heads,
         group,
         back,
-        row_count,
-        col_count,
+        (row_count, col_count),
         4,
     )
     scale_mid = lax.rsqrt(jnp.mean(hidden_in * hidden_in, axis=1, keepdims=True) + epsilon)
 
-    grad_mid, out_terms, grad_hidden_part, grad_down_part = mlp(
+    grad_mid, out_terms, grad_hidden_part, sum_down = mlp(
         normal_mid,
         rows_grad,
         early_tiles,
-        hidden_tiles[early:],
+        hidden_flat,
         full_down,
         row_count,
         col_count,
         3,
     )
+    out_sum = lax.psum_scatter(out_terms, "col", scatter_dimension=0, tiled=True)
     back_mid, gain_mid_part = norm_back(grad_mid, hidden_in, scale_mid, gain_second)
     grad_hidden_in = out_grad.astype(f32) + back_mid
     grad_low = grad_hidden_in.astype(bf16)
@@ -2035,27 +2220,31 @@
             5,
         )
     )
-    back_in, gain_in_part = norm_back(grad_in, inputs, scale_in, gain_first)
-    grad_tokens = (grad_hidden_in + back_in).astype(bf16)
-    gain_parts = jnp.concatenate([gain_in_part, gain_mid_part]).reshape(-1, 128)
     lefts = [
         (normal_in, normal_sib)[:cores],
         (grad_low, grad_low_sib)[:cores],
     ]
     rights = [(grad_first, grad_first_sib)[:cores], (mixed, mixed_sib)[:cores]]
-    sum_first, sum_output, sum_down, out_sum, gain_sums = sum_all(
-        lefts, rights, grad_down_part, out_terms, gain_parts, row_count, col_count, f32
+    extras = (
+        grad_in,
+        tokens,
+        grad_hidden_in,
+        gain_first[None],
+        hidden_in,
+        out_sum,
+        gain_mid_part[None],
     )
-    block_out = hidden_in + out_sum
-    gain_in_sum, gain_mid_sum = gain_sums.reshape(2, width)
+    sum_query, sum_keyvalue, sum_output, grad_tokens, block_out, gain_sums = sum_all(
+        lefts, rights, query_width, extras, row_count, col_count
+    )
     return (
-        block_out.astype(bf16),
+        block_out,
         grad_tokens,
-        gain_in_sum,
-        sum_first[:, :query_width],
-        sum_first[:, query_width:].reshape(deep, pairs, 2 * HD),
+        gain_sums[0],
+        sum_query,
+        sum_keyvalue.reshape(deep, pairs, 2 * HD),
         sum_output,
-        gain_mid_sum,
+        gain_sums[1],
         sum_hidden.reshape(deep, 2, hidden),
         sum_down,
     )

time: 619 us -> 598 us (0.966)
  Pallas kernels: 570 us -> 539 us
  between operations: 1.13 us -> 14.7 us
  other arithmetic: 24.8 us -> 14.9 us
    pallas_call x1, Pallas kernels: 140 us -> 108 us  [sum_all(): pl.pallas_call(functools.partial(sum_kernel, (row_count, col_count), coun...]
    unnamed x35 -> x29, local copies, waits for them, and re-layouts: 2.59 us -> 13 us
    convert_element_type x2 -> x0, other arithmetic: 6.73 us -> none  [the longest x1 3.53 us: shards(): block_out.astype(bf16)]
  transfers between devices with their start and end apart: 0 -> 1, of which waited for: 0 -> 1; matrix products, arithmetic and copies ran while one was open for 0% -> 2% of each run, Pallas kernels for 0% -> 14%
where the time goes in v6:
time: 598 us; the launch traced here: 593 us
  Pallas kernels  539 us (90%)
  local copies, waits for them, and re-layouts  23.1 us (4%)
  other arithmetic  14.9 us (2%)
  between operations  14.7 us (2%)
    pallas_call x1, Pallas kernels, mlp(): pl.pallas_call(functools.partial(mlp_kernel, (row_count, col_count), earl...  165 us
    pallas_call x1, Pallas kernels, gather_all(): pl.pallas_call(functools.partial(gather_kernel, (row_count, col_count), c...  140 us
    pallas_call x1, Pallas kernels, sum_all(): pl.pallas_call(functools.partial(sum_kernel, (row_count, col_count), coun...  108 us
    pallas_call x1, Pallas kernels, attend_back(): pl.pallas_call(functools.partial(attend_back_kernel, sizes, heads, group,...  82.2 us
    pallas_call x1, Pallas kernels, attend(): pl.pallas_call(functools.partial(attend_kernel, (row_count, col_count), h...  43.7 us
    unnamed x29, local copies, waits for them, and re-layouts  13 us
  transfers between devices with their start and end apart: 1, of which 1 were waited for; matrix products, arithmetic and copies ran while one was open for 2% of the time, Pallas kernels for 14%

profile of v6, /device:TPU:0, one launch (start us, length us, event | category | flops | bytes accessed | tf_op | source)
XLA Modules:
  0.0 592.7 jit_solution(13279991487584728278)
XLA Ops:
  7.3 0.8 reduce-window.8
  8.1 0.7 select_reduce_fusion
  9.2 0.9 copy.22
  10.2 0.7 convert_element_type.25
  10.9 1.5 fusion
  12.4 1.3 convert_element_type.30
  13.7 3.9 copy.20
  17.6 0.5 fusion.9
  18.1 0.8 pad_maximum_fusion.refs_0_
  18.9 1.3 fusion.2.refs_0_.refs_1_
  20.2 1.0 fusion.4.refs_4_
  21.2 140.2 %gather_weights.1 = (bf16[4,2048,768]{2,1,0:T(8,128)(2,1)}, bf16[4,2048,512]{2,1,0:T(8,128)(2,1)}, bf16[2048,2048]{1,0:T(8,128)(2,1)}, bf16[1024,2048]{1,0:T(8,128)(2,1)}) custom-call(bf16[256,768]{1,0:T(8,128)(2,1)} %pad_maximum_fusion.refs_0_, bf16[256,512]{1,0:T(8,128)(2,1)} %refs_1_.2, bf16[256,2048]{1,0:T(8,128)(2,1)} %refs_2_.1, bf16[256,2048]{1,0:T(8,128)(2,1)} %refs_3_.1), custom_call_target="tpu_custom_call" | custom-call | bytes 20971520 | tf_op jit(solution)/shard_map/gather_weights/pallas_call | solution.py:387
  161.5 1.1 fusion.7
  162.6 43.7 %attend.1 = (bf16[4,256,512]{2,1,0:T(8,128)(2,1)}, bf16[4,768,256]{2,1,0:T(8,128)(2,1)}, bf16[4,256,512]{2,1,0:T(8,128)(2,1)}, f32[4,8,256]{2,1,0:T(8,128)}, bf1...) custom-call(bf16[256,2048]{1,0:T(8,128)(2,1)} %fusion.2.refs_0_.refs_1_, ...), custom_call_target="tpu_custom_call" | custom-call | flops 6979321856 | bytes 20971520 | tf_op jit(solution)/shard_map/attend/pallas_call | solution.py:1744
  206.3 165.2 %feed_forward.1 = (f32[256,2048]{1,0:T(8,128)}, bf16[4,256,2048]{2,1,0:T(8,128)(2,1)}, bf16[4,2048,1024]{2,1,0:T(8,128)(2,1)}, f32[256,2048]{1,0:T(8,128)}, bf16...) custom-call(bf16[256,2048]{1,0:T(8,128)(2,1)} %get-tuple-element.40.refs_0_,, ...), custom_call_target="tpu_custom_call" | custom-call | flops 77309411328 | bytes 50331648 | tf_op jit(solution)/shard_map/feed_forward/pallas_call | solution.py:841
  371.5 1.5 copy-done
  373.1 0.2 multiply_reduce_fusion.2
  373.3 0.4 copy-done.2
  373.7 1.2 multiply_reduce_fusion
  374.9 1.1 fusion.6.refs_3_
  376.1 2.3 fusion.13
  378.4 82.2 %attend_back.1 = (f32[256,2048]{1,0:T(8,128)}, bf16[4,256,768]{2,1,0:T(8,128)(2,1)}, f32[256,4096]{1,0:T(8,128)}, bf16[256,1024]{1,0:T(8,128)(2,1)}, bf16[256,10...) custom-call(bf16[256,2048]{1,0:T(8,128)(2,1)} %get-tuple-element.73.refs_0_.refs_2_, ...), custom_call_target="tpu_custom_call" | custom-call | flops 9395240960 | bytes 37748736 | tf_op jit(solution)/shard_map/attend_back/pallas_call | solution.py:1984
  460.6 6.6 %reshape.127 = f32[256,2,2048]{2,1,0:T(2,128)} reshape(f32[256,4096]{1,0:T(8,128)} %get-tuple-element.63) | data formatting | bytes 8388608 | tf_op jit(solution)/shard_map/reshape | solution.py:2248
  467.2 1.0 reduce-scatter.2.cloned.1.call-done.refs_13_
  468.2 107.6 %sum_weights.1 = (f32[256,512]{1,0:T(8,128)}, f32[256,256]{1,0:T(8,128)}, f32[256,512]{1,0:T(8,128)}, bf16[256,2048]{1,0:T(8,128)(2,1)}, bf16[256,2048]{1,0:T(8,128)(2,1)}, /*index=5*/f32[2,2048]{1,0:T(2,128)}) custom-call(bf16[256,2048]{1,0:T(8,128)(2,1)} %fusion.2.refs_0_.refs_1_, bf16[256,1024]{1,0:T(8,128)(2,1)} %get-tuple-element.50.refs_1_, ...), custom_call_target="tpu_custom_call" | custom-call | flops 5368709120 | bytes 20971520 | tf_op jit(solution)/shard_map/sum_weights/pallas_call | solution.py:1498
  575.8 1.9 reshape.126
  577.7 1.4 fusion.14
  579.1 2.4 copy.28
  581.4 1.0 copy.29
  582.4 0.8 copy.30
  583.2 0.8 copy.31
  584.0 1.3 copy.32
  (34 shorter events, 0.5 us)
Async XLA Ops:
  7.2 461.0 %reduce-scatter.2.cloned.1.call-start = ((), (), s32[]{:S(2)}) async-start(), calls=%async_computation.1 | async-start | bytes 5242880 | tf_op jit(solution)/shard_map/reduce_scatter | solution.py:2199
  10.9 8.1 %copy-start.10 = (f32[2048]{0:T(1024)}, f32[2048]{0:T(1024)S(1)}, u32[]{:S(2)}) copy-start(f32[2048]{0:T(1024)S(1)} %convert_element_type.25) | copy-start | bytes 24580
  13.7 4.5 copy-start.8
  13.7 5.2 copy-start.1
  371.5 1.6 copy-start
  371.5 2.2 copy-start.2
  371.5 2.2 copy-start.9
  373.7 2.4 copy-start.3
  575.8 5.7 copy-start.5
  579.1 3.3 copy-start.7
  581.4 1.8 copy-start.6
  581.4 2.6 copy-start.4
Sparse Core Ops, SparseCore 0:
  371.6 96.5 reduce-scatter.1

commit v7 on v6

--- a/solution.py
+++ b/solution.py
@@ -288,6 +288,7 @@
 def gather_kernel(sizes, count, inner, *refs):
     row_count, col_count = sizes
     every = count + inner
+    splits = min(2, col_count)
     own, own_act = refs[:every], refs[every]
     full, full_act = refs[every + 1 : 2 * every + 1], refs[2 * every + 1]
     local_sems, zs, zr, ps, pr = refs[2 * every + 2 :]
@@ -327,19 +328,23 @@
     def inside(n, col, near):
         deep = own[n].shape[0]
         half = deep // 2
+        wide = own[n].shape[1] // splits
+        columns = pl.ds(col * wide, wide) if n >= count else slice(None)
 
         def block(row, number):
             rows = pl.ds(row * deep + number * half, half)
-            return full[n].at[col, rows] if n < count else full[n].at[rows]
+            return full[n].at[col, rows] if n < count else full[n].at[rows, columns]
 
         def mine(number):
-            return own[n].at[pl.ds(number * half, half)] if near else block(place.row, number)
+            rows = pl.ds(number * half, half)
+            return own[n].at[rows, columns] if near else block(place.row, number)
 
         return PlaneGather(place, block, mine, ps.at[n, col], pr.at[n, col])
 
     entries = [(n, k) for k in range(col_count) for n in range(count)]
-    entries += [(n, 0) for n in range(count, every)]
     parts = [inside(n, nearby(place, k), k == 0) for n, k in entries]
+    entries += [(n, 0) for n in range(count, every) for _ in range(splits)]
+    parts += [inside(n, part, True) for n in range(count, every) for part in range(splits)]
     act_steps = list(range(1, col_count))
 
     def act_step():
@@ -575,11 +580,11 @@
 
 def mlp_kernel(sizes, early, wide, *refs):
     hn_own, dy_in, wh_in, wh_own, wd_in = refs[:5]
-    grad_out, y_out, dwh_out, down_out, core_held, second_held, first_held = refs[5:12]
-    hn, dy, wh, wd, act, dgu, terms, staged, held, grad_staged, down_staged = refs[12:23]
-    token_sems, tile_sems, wd_sems, y_sem, dw_sems, sends, recvs = refs[23:30]
-    hs, hr, ps, pr, own_sem, grad_sems = refs[30:36]
-    inner_sems, inner_stage = refs[36:39], refs[39:]
+    grad_out, y_out, dwh_out, down_out = refs[5:9]
+    hn, dy, wh, wd, act, dgu, terms, staged, held, grad_staged, down_staged = refs[9:20]
+    token_sems, tile_sems, wd_sems, y_sem, dw_sems, sends, recvs = refs[20:27]
+    hs, hr, ps, pr, own_sem, grad_sems = refs[27:33]
+    first_held, inner_sems = refs[33], refs[34:]
     place = Place(*sizes)
     cols = place.cols
     width, hidden = wd.shape
@@ -764,10 +769,15 @@
         wd,
         lambda e: down_out.at[:, pl.ds(pl.multiple_of(e * chunk, chunk), chunk)],
         chunk,
-        (core_held, second_held, first_held, down_staged) + tuple(inner_sems),
-        inner_stage,
+        dy,
+        act,
+        first_held,
+        down_staged,
+        inner_sems,
     )
     inner.begin()
+    inner.tick(0)
+    inner.tick(1)
     grad(0)
     beside = []
     for number in ((1, 3) + (2,) * strips)[:strips]:
@@ -782,14 +792,14 @@
             right = dgu[:, :, span].reshape(cols * tokens, 2 * tile)
             wh[f, at] = dot_tokens(left, right).astype(bf16)
         pltpu.make_async_copy(wh.at[:, at], dwh_out.at[:, at], dw_sems.at[n]).start()
-        inner.tick(n)
+        inner.tick(n + 2)
         for number, some in enumerate(beside):
             for call in some:
                 pl.when(n == number)(functools.partial(do_late, call))
         return carry
 
     lax.fori_loop(0, strips, hidden_strip, 0)
-    for t in range(strips, inner.count + 2 * LAG):
+    for t in range(strips + 2, inner.count + 2 * LAG):
         inner.tick(t)
     while calls:
         next_late()
@@ -838,20 +848,16 @@
     count = hidden // chunk
     inner_sems = InnerSum.sems(plane, count)
     inner_sems[0] = pltpu.SemaphoreType.DMA((2, count, plane[0] * plane[1]))
-    grad, y, dwh, sum_down, *_ = pl.pallas_call(
+    grad, y, dwh, sum_down = pl.pallas_call(
         functools.partial(mlp_kernel, (row_count, col_count), early, wide),
         out_shape=[
             jax.ShapeDtypeStruct((rows, width), f32),
             jax.ShapeDtypeStruct(shape, bf16),
             jax.ShapeDtypeStruct(wh_shape, bf16),
             jax.ShapeDtypeStruct((deep, hidden), f32),
-        ]
-        + [
-            jax.ShapeDtypeStruct(held, bf16)
-            for held in InnerSum.held_shapes(plane, deep, hidden, chunk)
         ],
         in_specs=[ANY] * 5,
-        out_specs=[ANY] * 7,
+        out_specs=[ANY] * 4,
         scratch_shapes=[
             pltpu.VMEM(shape, bf16),
             pltpu.VMEM(shape, bf16),
@@ -878,8 +884,9 @@
             pltpu.SemaphoreType.DMA,
             pltpu.SemaphoreType.DMA((2,)),
         ]
+        + [pltpu.VMEM(InnerSum.held_shapes(plane, deep, hidden, chunk)[2], bf16)]
         + inner_sems
-        + InnerSumInPlace.stage_scratch(plane, deep, chunk),
+        + [pltpu.SemaphoreType.REGULAR],
         compiler_params=pltpu.CompilerParams(
             collective_id=collective_id, has_side_effects=True, vmem_limit_bytes=63 << 20
         ),
@@ -894,11 +901,9 @@
 
 
 class PlaneSum:
-    def __init__(self, place, block, held_second, held_first, sems, stage=None):
-        self.place, self.block = place, block
-        self.held = (held_first, held_second)
+    def __init__(self, place, block, held, sems):
+        self.place, self.block, self.held = place, block, held
         self.sends, self.recvs = sems
-        self.stage = stage
 
     @staticmethod
     def counts_of(sizes):
@@ -932,36 +937,19 @@
             source, sem = self.part(half, i, nq - step), number
         else:
             source, sem = self.part(half, np_ - step, 0), (nq - 1) * np_ + number
-        target = self.held[kind].at[half, number]
+        target = self.held(kind, half, number)
         device = self.place.device(self.axes(half)[1 if kind == 1 else 0], 1)
         return remote(source, target, self.sends.at[half, sem], self.recvs.at[half, sem], device)
 
-    def bring(self, half, kind, step, i):
-        number = self.number(half, kind, step, i)
-        return pltpu.make_async_copy(
-            self.held[kind].at[half, number],
-            self.stage[kind].at[half, number],
-            self.stage[2 + kind].at[half, number],
-        )
-
     def add(self, pieces):
-        if self.stage is not None:
-            for piece in pieces:
-                self.copy(*piece).wait_recv()
-                self.bring(*piece).start()
         for half, kind, step, i in pieces:
             np_, nq = self.counts(half)
-            if self.stage is None:
-                self.copy(half, kind, step, i).wait_recv()
-                held = self.held[kind]
-            else:
-                self.bring(half, kind, step, i).wait()
-                held = self.stage[kind]
+            self.copy(half, kind, step, i).wait_recv()
             if kind == 1:
                 target = self.part(half, i, nq - step - 1)
             else:
                 target = self.part(half, np_ - step - 1, 0)
-            add_rows(target, held.at[half, self.number(half, kind, step, i)])
+            add_rows(target, self.held(kind, half, self.number(half, kind, step, i)))
             yield half, i
 
     def first(self):
@@ -1006,6 +994,10 @@
                 self.copy(half, 0, step, 0).wait_send()
 
 
+def landing(first, second):
+    return lambda kind, half, number: (first, second)[kind].at[half, number]
+
+
 def halves_of(acc):
     half = acc.shape[1] // 2
     return lambda chip, number: acc.at[chip, pl.ds(number * half, half)]
@@ -1024,7 +1016,12 @@
         self.load_sems, self.core_sems, self.plane_sems, self.out_sems = refs[5:9]
         self.ahead = min(3, self.count)
         self.chips, self.deep = self.core_held.shape[1:3]
-        self.stage = None
+
+    def held(self, e):
+        return landing(self.first.at[e], self.second.at[e])
+
+    def core_block(self, e, chip):
+        return self.core_held.at[e, chip]
 
     @staticmethod
     def held_shapes(sizes, deep, width, chunk):
@@ -1045,12 +1042,12 @@
         ]
 
     @staticmethod
-    def scratch(sizes, deep, width, chunk):
+    def scratch(sizes, deep, width, chunk, staged):
         shapes = InnerSum.held_shapes(sizes, deep, width, chunk)
         count = width // chunk
         return (
             [pltpu.VMEM(shape, bf16) for shape in shapes[:1] + shapes]
-            + [pltpu.VMEM((2, deep, chunk), f32), pltpu.SemaphoreType.DMA((count,))]
+            + [pltpu.VMEM(staged, f32), pltpu.SemaphoreType.DMA((count,))]
             + InnerSum.sems(sizes, count)
         )
 
@@ -1080,10 +1077,8 @@
         return PlaneSum(
             self.place,
             lambda chip, number: self.block(e, chip).at[pl.ds(number * half, half)],
-            self.second.at[e],
-            self.first.at[e],
+            self.held(e),
             (self.plane_sems.at[0, e], self.plane_sems.at[1, e]),
-            self.stage,
         )
 
     def out_copy(self, e):
@@ -1107,14 +1102,13 @@
         if self.place.sizes[2] > 1:
             for share in self.shares(e):
                 share.wait_recv()
-        return self.core_held.at[e]
 
     def start(self, e):
         when(e + self.ahead < self.count, lambda: self.prepare(e + self.ahead))
-        held = self.ready(e)
+        self.ready(e)
         if self.place.sizes[2] > 1:
             for chip in range(self.chips):
-                add_rows(self.block(e, chip), held.at[chip])
+                add_rows(self.block(e, chip), self.core_block(e, chip))
         self.inside(e).first()
 
     def middle(self, e):
@@ -1133,8 +1127,11 @@
             e = t - lag
             when((e >= 0) & (e < self.count), functools.partial(action, e))
 
+    def last_outs(self):
+        return range(max(self.count - 2, 0), self.count)
+
     def finish(self):
-        for e in range(max(self.count - 2, 0), self.count):
+        for e in self.last_outs():
             self.out_copy(e).wait()
 
         def done(e, carry):
@@ -1147,44 +1144,67 @@
         lax.fori_loop(0, self.count, done, 0)
 
 
+class PairSum(InnerSum):
+    def out_copy(self, f):
+        return pltpu.make_async_copy(self.staged.at[0], self.target(f), self.out_sems.at[0])
+
+    def close(self, e):
+        self.inside(e).third()
+        f, part = e // 2, lax.rem(e, 2)
+        when((part == 0) & (f >= 1), lambda: self.out_copy(f - 1).wait())
+        own = self.block(e, self.place.chip_of(self.place.at))
+        for number in (0, 1):
+
+            @pl.when(part == number)
+            def _(number=number):
+                self.staged[0, :, number, :] = own[...].astype(f32)
+
+        when(part == 1, lambda: self.out_copy(f).start())
+
+    def last_outs(self):
+        return range(self.count // 2 - 1, self.count // 2)
+
+
 class InnerSumInPlace(InnerSum):
-    def __init__(self, place, terms, target, chunk, refs, stage):
+    def __init__(self, place, terms, target, chunk, core_land, land, first, staged, sems):
         self.place, self.terms, self.target, self.chunk = place, terms, target, chunk
-        self.core_held, self.second, self.first, self.staged = refs[:4]
-        self.core_sems, self.plane_sems, self.out_sems = refs[4:]
+        self.core_land, self.land, self.first, self.staged = core_land, land, first, staged
+        self.core_sems, self.plane_sems, self.out_sems, self.free_sem = sems
         self.count = terms.shape[1] // chunk
         self.ahead = self.count
-        self.chips, self.deep = self.core_held.shape[1:3]
-        self.core_stage, self.core_stage_sem = stage[:2]
-        self.stage = stage[2:]
-
-    @staticmethod
-    def stage_scratch(sizes, deep, chunk):
-        shapes = InnerSum.held_shapes(sizes, deep, chunk, chunk)
-        return [
-            pltpu.VMEM(shapes[0][1:], bf16),
-            pltpu.SemaphoreType.DMA,
-            pltpu.VMEM(shapes[2][1:], bf16),
-            pltpu.VMEM(shapes[1][1:], bf16),
-            pltpu.SemaphoreType.DMA(shapes[2][1:3]),
-            pltpu.SemaphoreType.DMA(shapes[1][1:3]),
-        ]
+        self.chips = place.sizes[0] * place.sizes[1]
+        self.deep = terms.shape[0] // place.rows
+
+    def columns(self, e):
+        return pl.ds(pl.multiple_of(e * self.chunk, self.chunk), self.chunk)
 
     def rows(self, e, chip, core):
         row = chip * self.place.sizes[2] + core
         return self.terms.at[
-            pl.ds(pl.multiple_of(row * self.deep, self.deep), self.deep),
-            pl.ds(pl.multiple_of(e * self.chunk, self.chunk), self.chunk),
+            pl.ds(pl.multiple_of(row * self.deep, self.deep), self.deep), self.columns(e)
         ]
 
     def block(self, e, chip):
         return self.rows(e, chip, self.place.at[2])
+
+    def core_block(self, e, chip):
+        return self.core_land.at[chip, :, self.columns(e)]
+
+    def held(self, e):
+        half_deep = self.deep // 2
+
+        def place_of(kind, half, number):
+            if kind == 0:
+                return self.first.at[e, half, number]
+            return self.land.at[number, pl.ds(half * half_deep, half_deep), self.columns(e)]
+
+        return place_of
 
     def shares(self, e):
         return [
             remote(
                 self.rows(e, chip, self.other()),
-                self.core_held.at[e, chip],
+                self.core_block(e, chip),
                 self.core_sems.at[0, e, chip],
                 self.core_sems.at[1, e, chip],
                 self.place.device(2, 1),
@@ -1197,16 +1217,20 @@
             for share in self.shares(e):
                 share.start()
 
+    def begin(self):
+        peers = [axis for axis in range(3) if self.place.sizes[axis] > 1]
+        for axis in peers:
+            pl.semaphore_signal(
+                self.free_sem, inc=1, device_id=self.place.device(axis, -1), device_id_type=MESH
+            )
+        if peers:
+            pl.semaphore_wait(self.free_sem, len(peers))
+        super().begin()
+
     def ready(self, e):
         if self.place.sizes[2] > 1:
             for share in self.shares(e):
                 share.wait_recv()
-            copy = pltpu.make_async_copy(
-                self.core_held.at[e], self.core_stage, self.core_stage_sem
-            )
-            copy.start()
-            copy.wait()
-        return self.core_stage
 
 
 class SmallSum:
@@ -1298,24 +1322,12 @@
         grad = dxn[at]
         weighted = grad * gain[...]
         inner = jnp.mean(weighted * values, axis=1, keepdims=True)
-        result = dh[at] + scale * weighted - values * (scale * scale * scale) * inner
+        result = dh[at].astype(f32) + scale * weighted - values * (scale * scale * scale) * inner
         out[at] = result.astype(out.dtype)
         part[0:1] += jnp.sum(grad * values * scale, axis=0, keepdims=True)
         return carry
 
     part[0:1] = jnp.zeros((1, width), f32)
-    lax.fori_loop(0, rows // piece, body, 0)
-
-
-def add_out(hidden, term, out):
-    rows = hidden.shape[0]
-    piece = 32
-
-    def body(n, carry):
-        at = pl.ds(pl.multiple_of(n * piece, piece), piece)
-        out[at] = (hidden[at] + term[at].astype(f32)).astype(out.dtype)
-        return carry
-
     lax.fori_loop(0, rows // piece, body, 0)
 
 
@@ -1325,10 +1337,10 @@
     cores = place.sizes[2]
     lefts, rights = refs[: cores * count], refs[cores * count : 2 * cores * count]
     refs = refs[2 * cores * count :]
-    dxn, x, dh, gain, hidden, out_sum, mid_part = refs[:7]
-    outs = refs[7 : 8 + count]
-    tokens_out, block_out, small_out = refs[8 + count : 11 + count]
-    refs = refs[11 + count :]
+    dxn, x, dh, gain, mid_part = refs[:5]
+    outs = refs[5 : 6 + count]
+    tokens_out, small_out = refs[6 + count : 8 + count]
+    refs = refs[8 + count :]
     per = [refs[7 * n : 7 * n + 7] for n in range(count)]
     load_sems, out_sems, ps, pr, zs, zr = refs[7 * count : 7 * count + 6]
     ring_held, line_held, ring_sems, line_sems, chip_sems, small = refs[7 * count + 6 :]
@@ -1374,8 +1386,7 @@
     place.greet(True, True)
     smalls = SmallSum(place, small, small_out, ring_held, line_held, ring_sems, line_sems)
     stages = [functools.partial(norm_rows, dxn, x, dh, gain, tokens_out, small)]
-    stages += [functools.partial(add_out, hidden, out_sum, block_out), smalls.begin]
-    stages += smalls.stages
+    stages += [smalls.begin] + smalls.stages
     small[1:2] = mid_part[...]
     for copy in loads():
         copy.wait()
@@ -1384,8 +1395,7 @@
         return PlaneSum(
             place,
             halves_of(acc[n].at[col]),
-            per[n][1].at[col],
-            per[n][2].at[col],
+            landing(per[n][2].at[col], per[n][1].at[col]),
             (ps.at[n, col], pr.at[n, col]),
         )
 
@@ -1500,11 +1510,10 @@
         out_shape=[jax.ShapeDtypeStruct((deep, width), f32) for width in outs]
         + [
             jax.ShapeDtypeStruct((tokens, model), bf16),
-            jax.ShapeDtypeStruct((tokens, model), bf16),
             jax.ShapeDtypeStruct((2, model), f32),
         ],
-        in_specs=[ANY] * (2 * count * nk) + [vmem] * 7,
-        out_specs=[ANY] * (count + 1) + [vmem] * 3,
+        in_specs=[ANY] * (2 * count * nk) + [vmem] * 5,
+        out_specs=[ANY] * (count + 1) + [vmem] * 2,
         scratch_shapes=scratch,
         compiler_params=pltpu.CompilerParams(
             collective_id=1, has_side_effects=True, vmem_limit_bytes=63 << 20
@@ -1784,28 +1793,28 @@
 
 
 def attend_back_kernel(sizes, heads, group, back, chunk, *refs):
-    dhb, xn, lse, bias, cosq, sinq, coskv, sinkv = refs[:8]
-    mixed_in, q_in, kv_in, wo_in, wf_in, terms = refs[8:14]
-    dxn, dqkv_out, sum_out, xn_sib, dhb_sib, mixed_sib, dqkv_sib = refs[14:21]
-    q, kv, wo, wf, dmix, dkv, dqkv, going, coming, dst, pst, rhs_q, rhs_o = refs[21:34]
-    in_sems, wo_sems, wf_sems, out_sems, pair_sems, row_sems, sends, recvs = refs[34:42]
+    grad_hn, hidden_in, dy, gain, xn, lse, bias, cosq, sinq, coskv, sinkv = refs[:11]
+    mixed_in, q_in, kv_in, wo_in, wf_in, terms = refs[11:17]
+    dxn, dh, dhb, mid_part = refs[17:21]
+    dqkv_out, sum_out, xn_sib, dhb_sib, mixed_sib, dqkv_sib = refs[21:27]
+    q, kv, wo, wf, dmix, dkv, dqkv, going, coming, dst, pst, rhs_q, rhs_o = refs[27:40]
+    in_sems, wo_sems, wf_sems, out_sems, pair_sems, row_sems, sends, recvs = refs[40:48]
     place = Place(*sizes)
     cols, col = place.cols, place.col
     cores = place.sizes[2]
     tokens = dhb.shape[0]
     query_width = heads * HD
     pairs = heads // group
-    hidden = sum_out.shape[1] // 2
-
-    def inner_target(e):
-        at = lax.rem(e, 2) * hidden + e // 2 * chunk
-        return sum_out.at[:, pl.ds(pl.multiple_of(at, chunk), chunk)]
+    hidden = sum_out.shape[2]
+
+    def inner_target(f):
+        return sum_out.at[:, :, pl.ds(pl.multiple_of(f * chunk, chunk), chunk)]
 
     def inner_terms(e, core):
         at = pl.multiple_of(lax.rem(e, 2) * chunk, chunk)
         return terms.at[e // 2, :, core, :, pl.ds(at, chunk)]
 
-    inner = InnerSum(place, 2 * hidden // chunk, inner_terms, inner_target, refs[42:])
+    inner = PairSum(place, 2 * hidden // chunk, inner_terms, inner_target, refs[48:])
 
     in_copies = [
         pltpu.make_async_copy(q_in, q, in_sems.at[0]),
@@ -1817,24 +1826,23 @@
         return pltpu.make_async_copy(wo_in.at[z], wo.at[slot], wo_sems.at[slot])
 
     def wf_copy(z):
-        slot = lax.rem(z, 2)
-        return pltpu.make_async_copy(wf_in.at[z], wf.at[slot], wf_sems.at[slot])
+        return pltpu.make_async_copy(wf_in.at[z], wf, wf_sems.at[0])
 
     wo_copy(0).start()
     for copy in in_copies:
         copy.start()
-    for z in range(min(2, cols)):
-        wf_copy(z).start()
+    wf_copy(0).start()
     place.greet(True, True)
 
     other = place.device(2, 1)
+    chips, deep = terms.shape[1], terms.shape[3]
     exchanges = []
     if cores > 1:
-        chips, deep = terms.shape[1], terms.shape[3]
         moves = [(mixed_in, mixed_sib)]
-        for chip in range(chips):
-            to, rows = pl.ds(chip * deep, deep), core_rows(place, chip, 1, deep)
-            moves += [(xn.at[:, rows], xn_sib.at[:, to]), (dhb.at[:, rows], dhb_sib.at[:, to])]
+        for source, target in ((xn, xn_sib), (dhb, dhb_sib)):
+            for chip in range(chips):
+                to, rows = pl.ds(chip * deep, deep), core_rows(place, chip, 1, deep)
+                moves.append((source.at[:, rows], target.at[:, to]))
         exchanges = [
             remote(source, target, pair_sems.at[0, n], pair_sems.at[1, n], other)
             for n, (source, target) in enumerate(moves)
@@ -1847,7 +1855,11 @@
         return pltpu.make_async_copy(dqkv.at[z], dqkv_out.at[z], out_sems.at[z])
 
     inner.begin()
-    for exchange in exchanges:
+    for exchange in exchanges[: 1 + chips]:
+        exchange.start()
+    norm_rows(grad_hn, hidden_in, dy, gain, dh, mid_part)
+    dhb[...] = dh[...].astype(bf16)
+    for exchange in exchanges[1 + chips :]:
         exchange.start()
     dxn[...] = jnp.zeros_like(dxn)
     for copy in in_copies:
@@ -1894,8 +1906,8 @@
         if cores > 1:
             row_exchange(z).start()
         wf_copy(z).wait()
-        dxn[...] += against(dqkv[z], wf[lax.rem(z, 2)])
-        when(z + 2 < cols, lambda: wf_copy(z + 2).start())
+        dxn[...] += against(dqkv[z], wf[...])
+        when(z + 1 < cols, lambda: wf_copy(z + 1).start())
 
     def halos(z):
         for step in range(1, back + 1):
@@ -1963,12 +1975,12 @@
 
 
 def attend_back(
-    dhb, xn, lse, bias, tables, mixed, q, kv, wo, wf, terms, group, sizes, cid
+    mid, xn, lse, bias, tables, mixed, q, kv, wo, wf, terms, group, sizes, cid
 ):
     row_count, col_count = sizes
     plane = plane_sizes(row_count)
     chips = plane[0] * plane[1]
-    tokens, width = dhb.shape
+    tokens, width = xn.shape
     heads = lse.shape[1]
     back = kv.shape[1] // tokens - 1
     pairs = heads // group
@@ -1985,20 +1997,23 @@
         functools.partial(attend_back_kernel, sizes, heads, group, back, chunk),
         out_shape=[
             jax.ShapeDtypeStruct((tokens, width), f32),
+            jax.ShapeDtypeStruct((tokens, width), f32),
+            jax.ShapeDtypeStruct((tokens, width), bf16),
+            jax.ShapeDtypeStruct((1, width), f32),
             jax.ShapeDtypeStruct(row_shape, bf16),
-            jax.ShapeDtypeStruct((deep, inner_width), f32),
+            jax.ShapeDtypeStruct((deep, 2, tiles * chunk), f32),
             jax.ShapeDtypeStruct((tokens, chips * deep), bf16),
             jax.ShapeDtypeStruct((tokens, chips * deep), bf16),
             jax.ShapeDtypeStruct(mixed.shape, bf16),
             jax.ShapeDtypeStruct(row_shape, bf16),
         ],
-        in_specs=[vmem] * 8 + [ANY] * 6,
-        out_specs=[vmem] + [ANY] * 6,
+        in_specs=[vmem] * 11 + [ANY] * 6,
+        out_specs=[vmem] * 4 + [ANY] * 6,
         scratch_shapes=[
             pltpu.VMEM(q.shape, bf16),
             pltpu.VMEM(kv.shape, bf16),
             pltpu.VMEM((2,) + wo.shape[1:], bf16),
-            pltpu.VMEM((2,) + wf.shape[1:], bf16),
+            pltpu.VMEM(wf.shape[1:], bf16),
             pltpu.VMEM((tokens, heads * HD), bf16),
             pltpu.VMEM(kv.shape, f32),
             pltpu.VMEM(row_shape, bf16),
@@ -2017,7 +2032,7 @@
             pltpu.SemaphoreType.DMA((max(back, 1), col_count)),
             pltpu.SemaphoreType.DMA((max(back, 1), col_count)),
         ]
-        + InnerSum.scratch(plane, deep, inner_width, chunk),
+        + InnerSum.scratch(plane, deep, inner_width, chunk, (1, deep, 2, chunk)),
         compiler_params=pltpu.CompilerParams(
             collective_id=cid, has_side_effects=True, vmem_limit_bytes=62 << 20
         ),
@@ -2028,7 +2043,7 @@
         ),
         name="attend_back",
     )(
-        dhb,
+        *mid,
         xn,
         lse,
         bias,
@@ -2069,15 +2084,6 @@
 def normalize(values, gain):
     scale = lax.rsqrt(jnp.mean(values * values, axis=1, keepdims=True) + epsilon)
     return ((values * scale * gain).astype(bf16), scale)
-
-
-def norm_back(grad_in, values, scale, gain):
-    weighted = grad_in * gain
-    inner_sum = jnp.mean(weighted * values, axis=1, keepdims=True)
-    return (
-        scale * weighted - values * (scale * scale * scale) * inner_sum,
-        jnp.sum(grad_in * values * scale, axis=0),
-    )
 
 
 def against(left, right):
@@ -2184,8 +2190,6 @@
         (row_count, col_count),
         4,
     )
-    scale_mid = lax.rsqrt(jnp.mean(hidden_in * hidden_in, axis=1, keepdims=True) + epsilon)
-
     grad_mid, out_terms, grad_hidden_part, sum_down = mlp(
         normal_mid,
         rows_grad,
@@ -2197,14 +2201,11 @@
         3,
     )
     out_sum = lax.psum_scatter(out_terms, "col", scatter_dimension=0, tiled=True)
-    back_mid, gain_mid_part = norm_back(grad_mid, hidden_in, scale_mid, gain_second)
-    grad_hidden_in = out_grad.astype(f32) + back_mid
-    grad_low = grad_hidden_in.astype(bf16)
     cores = plane_sizes(row_count)[2]
     tables_back = (tables[0], -tables[1], tables[2], -tables[3])
-    grad_in, grad_first, sum_hidden, normal_sib, grad_low_sib, mixed_sib, grad_first_sib = (
+    grad_in, grad_hidden_in, grad_low, gain_mid_part, grad_first, sum_hidden, *siblings = (
         attend_back(
-            grad_low,
+            (grad_mid, hidden_in, out_grad, gain_second[None]),
             normal_in,
             lse,
             bias.T,
@@ -2220,6 +2221,7 @@
             5,
         )
     )
+    normal_sib, grad_low_sib, mixed_sib, grad_first_sib = siblings
     lefts = [
         (normal_in, normal_sib)[:cores],
         (grad_low, grad_low_sib)[:cores],
@@ -2230,13 +2232,13 @@
         tokens,
         grad_hidden_in,
         gain_first[None],
-        hidden_in,
-        out_sum,
-        gain_mid_part[None],
+        gain_mid_part,
     )
-    sum_query, sum_keyvalue, sum_output, grad_tokens, block_out, gain_sums = sum_all(
+    sum_query, sum_keyvalue, sum_output, grad_tokens, gain_sums = sum_all(
         lefts, rights, query_width, extras, row_count, col_count
     )
+    out_sum, gain_sums = lax.optimization_barrier((out_sum, gain_sums))
+    block_out = (hidden_in + out_sum.astype(f32)).astype(bf16)
     return (
         block_out,
         grad_tokens,
@@ -2245,7 +2247,7 @@
         sum_keyvalue.reshape(deep, pairs, 2 * HD),
         sum_output,
         gain_sums[1],
-        sum_hidden.reshape(deep, 2, hidden),
+        sum_hidden,
         sum_down,
     )
 

time: 598 us -> 584 us (0.977)
  local copies, waits for them, and re-layouts: 23.1 us -> 14.8 us
    reshape x1 -> x0, local copies, waits for them, and re-layouts: 6.57 us -> none  [shards(): sum_hidden.reshape(deep, 2, hidden)]
    unnamed x29 -> x27, local copies, waits for them, and re-layouts: 13 us -> 12.1 us
  transfers between devices with their start and end apart: 1 -> 1, of which waited for: 1 -> 0; matrix products, arithmetic and copies ran while one was open for 2% -> 1% of each run, Pallas kernels for 14% -> 33%
where the time goes in v7:
time: 584 us; the launch traced here: 579 us
  Pallas kernels  536 us (92%)
  local copies, waits for them, and re-layouts  14.8 us (3%)
  between operations  14.4 us (2%)
  other arithmetic  13.7 us (2%)
    pallas_call x1, Pallas kernels, mlp(): pl.pallas_call(functools.partial(mlp_kernel, (row_count, col_count), earl...  162 us
    pallas_call x1, Pallas kernels, gather_all(): pl.pallas_call(functools.partial(gather_kernel, (row_count, col_count), c...  140 us
    pallas_call x1, Pallas kernels, sum_all(): pl.pallas_call(functools.partial(sum_kernel, (row_count, col_count), coun...  106 us
    pallas_call x1, Pallas kernels, attend_back(): pl.pallas_call(functools.partial(attend_back_kernel, sizes, heads, group,...  85.5 us
    pallas_call x1, Pallas kernels, attend(): pl.pallas_call(functools.partial(attend_kernel, (row_count, col_count), h...  43.5 us
    unnamed x27, local copies, waits for them, and re-layouts  12.1 us
  transfers between devices with their start and end apart: 1, of which 0 were waited for; matrix products, arithmetic and copies ran while one was open for 1% of the time, Pallas kernels for 33%

profile of v7, /device:TPU:0, one launch (start us, length us, event | category | flops | bytes accessed | tf_op | source)
XLA Modules:
  0.0 579.4 jit_solution(5715314787024462241)
XLA Ops:
  7.3 0.8 reduce-window.8
  8.1 0.7 select_reduce_fusion
  8.9 0.1 pad.3.clone
  8.9 0.1 pad.6.clone
  9.0 0.1 dynamic-slice_convert_fusion
  9.2 0.1 pad_dynamic-slice_fusion
  9.2 0.9 copy.22
  10.2 0.7 convert_element_type.23
  10.9 1.5 fusion
  12.4 3.9 copy.20
  16.3 0.6 broadcast_in_dim.64
  16.9 0.5 fusion.9
  17.5 0.8 pad_maximum_fusion.refs_0_
  18.3 1.3 fusion.2.refs_0_.refs_4_
  19.5 1.0 fusion.4.refs_4_
  20.5 140.0 %gather_weights.1 = (bf16[4,2048,768]{2,1,0:T(8,128)(2,1)}, bf16[4,2048,512]{2,1,0:T(8,128)(2,1)}, bf16[2048,2048]{1,0:T(8,128)(2,1)}, bf16[1024,2048]{1,0:T(8,128)(2,1)}) custom-call(bf16[256,768]{1,0:T(8,128)(2,1)} %pad_maximum_fusion.refs_0_, bf16[256,512]{1,0:T(8,128)(2,1)} %refs_1_.2, bf16[256,2048]{1,0:T(8,128)(2,1)} %refs_2_.2, bf16[256,2048]{1,0:T(8,128)(2,1)} %refs_2_.3), custom_call_target="tpu_custom_call" | custom-call | bytes 20971520 | tf_op jit(solution)/shard_map/gather_weights/pallas_call | solution.py:392
  160.5 1.1 fusion.7
  161.6 43.5 %attend.1 = (bf16[4,256,512]{2,1,0:T(8,128)(2,1)}, bf16[4,768,256]{2,1,0:T(8,128)(2,1)}, bf16[4,256,512]{2,1,0:T(8,128)(2,1)}, f32[4,8,256]{2,1,0:T(8,128)}, bf1...) custom-call(bf16[256,2048]{1,0:T(8,128)(2,1)} %fusion.2.refs_0_.refs_4_, ...), custom_call_target="tpu_custom_call" | custom-call | flops 6979321856 | bytes 20971520 | tf_op jit(solution)/shard_map/attend/pallas_call | solution.py:1753
  205.1 161.9 %feed_forward.1 = (f32[256,2048]{1,0:T(8,128)}, bf16[4,256,2048]{2,1,0:T(8,128)(2,1)}, bf16[4,2048,1024]{2,1,0:T(8,128)(2,1)}, f32[256,2048]{1,0:T(8,128)}) custom-call(bf16[256,2048]{1,0:T(8,128)(2,1)} %get-tuple-element.44.refs_0_, bf16[4,256,2048]{2,1,0:T(8,128)(2,1)} %bitcast.31, bf16[2,2048,1024]{2,1,0:T(8,128)(2,1)} %get-tuple-element.46.refs_2_, ...), custom_call_target="tpu_custom_call" | custom-call | flops 77309411328 | bytes 50331648 | tf_op jit(solution)/shard_map/feed_forward/pallas_call | solution.py:851
  367.1 1.2 fusion.6.refs_6_
  368.2 85.5 %attend_back.1 = (f32[256,2048]{1,0:T(8,128)}, f32[256,2048]{1,0:T(8,128)}, bf16[256,2048]{1,0:T(8,128)(2,1)}, f32[1,2048]{1,0:T(1,128)}, bf16[4,256,768]{2,1,0:...) custom-call(f32[256,2048]{1,0:T(8,128)} %get-tuple-element.49.refs_0, ...), custom_call_target="tpu_custom_call" | custom-call | flops 9395240960 | bytes 37748736 | tf_op jit(solution)/shard_map/attend_back/pallas_call | solution.py:1996
  453.8 105.5 %sum_weights.1 = (f32[256,512]{1,0:T(8,128)}, f32[256,256]{1,0:T(8,128)}, f32[256,512]{1,0:T(8,128)}, bf16[256,2048]{1,0:T(8,128)(2,1)}, f32[2,2048]{1,0:T(2,128)}) custom-call(bf16[256,2048]{1,0:T(8,128)(2,1)} %fusion.2.refs_0_.refs_4_, bf16[256,1024]{1,0:T(8,128)(2,1)} %get-tuple-element.55.refs_1_, bf16[256,2048]{1,0:T(8,128)(2,1)} %get-tuple-element.56.refs_2_, ...), custom_call_target="tpu_custom_call" | custom-call | flops 5368709120 | bytes 20971520 | tf_op jit(solution)/shard_map/sum_weights/pallas_call | solution.py:1508
  559.3 1.8 reshape.104
  561.1 3.3 add_convert_fusion
  564.4 0.6 fusion.13
  565.0 1.0 copy.28
  565.9 0.8 copy.29
  566.7 0.8 copy.30
  567.5 0.3 copy-done.1
  567.8 2.1 copy.31
  570.0 1.0 copy-done.2
  570.9 1.3 copy.32
  (27 shorter events, 0.2 us)
Async XLA Ops:
  7.2 553.9 %reduce-scatter.2.cloned.1.call-start = ((), (), s32[]{:S(2)}) async-start(), calls=%async_computation.1 | async-start | bytes 5242880 | tf_op jit(solution)/shard_map/reduce_scatter | solution.py:2203
  10.9 7.4 %copy-start.7 = (f32[2048]{0:T(1024)}, f32[2048]{0:T(1024)S(1)}, u32[]{:S(2)}) copy-start(f32[2048]{0:T(1024)S(1)} %convert_element_type.23) | copy-start | bytes 24580
  12.4 3.9 copy-start.9
  12.4 5.1 copy-start.6
  12.4 5.8 %copy-start = (bf16[256,2048]{1,0:T(8,128)(2,1)S(1)}, bf16[256,2048]{1,0:T(8,128)(2,1)}, u32[]{:S(2)}) copy-start(bf16[256,2048]{1,0:T(8,128)(2,1)} %refs_9_.1) | copy-start | bytes 3145732
  561.1 3.3 copy-start.8
  561.1 3.9 copy-start.3
  561.1 4.9 copy-start.5
  561.1 5.7 copy-start.4
  565.0 2.9 copy-start.1
  567.8 3.1 copy-start.2
Sparse Core Ops, SparseCore 0:
  367.2 96.0 reduce-scatter.1

commit v8 on v7

--- a/solution.py
+++ b/solution.py
@@ -799,7 +799,7 @@
         return carry
 
     lax.fori_loop(0, strips, hidden_strip, 0)
-    for t in range(strips + 2, inner.count + 2 * LAG):
+    for t in range(strips + 2, inner.count + 2 * inner.lag):
         inner.tick(t)
     while calls:
         next_late()
@@ -1010,6 +1010,8 @@
 
 
 class InnerSum:
+    lag = LAG
+
     def __init__(self, place, count, terms, target, refs):
         self.place, self.count, self.terms, self.target = place, count, terms, target
         self.acc, self.core_held, self.second, self.first, self.staged = refs[:5]
@@ -1123,7 +1125,8 @@
         self.out_copy(e).start()
 
     def tick(self, t):
-        for lag, action in ((0, self.start), (LAG, self.middle), (2 * LAG, self.close)):
+        steps = ((0, self.start), (self.lag, self.middle), (2 * self.lag, self.close))
+        for lag, action in steps:
             e = t - lag
             when((e >= 0) & (e < self.count), functools.partial(action, e))
 
@@ -1166,6 +1169,8 @@
 
 
 class InnerSumInPlace(InnerSum):
+    lag = LAG + 1
+
     def __init__(self, place, terms, target, chunk, core_land, land, first, staged, sems):
         self.place, self.terms, self.target, self.chunk = place, terms, target, chunk
         self.core_land, self.land, self.first, self.staged = core_land, land, first, staged

time: 584 us -> 587 us (level)
    pallas_call x1, Pallas kernels: 106 us -> 112 us  [sum_all(): pl.pallas_call(functools.partial(sum_kernel, (row_count, col_count), coun...]
  transfers between devices with their start and end apart: 1 -> 1, of which waited for: 0 -> 0; matrix products, arithmetic and copies ran while one was open for 1% -> 1% of each run, Pallas kernels for 33% -> 34%
where the time goes in v8:
time: 587 us; the launch traced here: 583 us
  Pallas kernels  540 us (92%)
  local copies, waits for them, and re-layouts  14.8 us (3%)
  between operations  14.4 us (2%)
  other arithmetic  13.7 us (2%)
    pallas_call x1, Pallas kernels, mlp(): pl.pallas_call(functools.partial(mlp_kernel, (row_count, col_count), earl...  157 us
    pallas_call x1, Pallas kernels, gather_all(): pl.pallas_call(functools.partial(gather_kernel, (row_count, col_count), c...  140 us
    pallas_call x1, Pallas kernels, sum_all(): pl.pallas_call(functools.partial(sum_kernel, (row_count, col_count), coun...  112 us
    pallas_call x1, Pallas kernels, attend_back(): pl.pallas_call(functools.partial(attend_back_kernel, sizes, heads, group,...  87.1 us
    pallas_call x1, Pallas kernels, attend(): pl.pallas_call(functools.partial(attend_kernel, (row_count, col_count), h...  43.5 us
    unnamed x27, local copies, waits for them, and re-layouts  12.1 us
  transfers between devices with their start and end apart: 1, of which 0 were waited for; matrix products, arithmetic and copies ran while one was open for 1% of the time, Pallas kernels for 34%

profile of v8, /device:TPU:0, one launch (start us, length us, event | category | flops | bytes accessed | tf_op | source)
XLA Modules:
  0.0 582.6 jit_solution(10648347539615644836)
XLA Ops:
  7.3 0.8 reduce-window.8
  8.1 0.7 select_reduce_fusion
  8.9 0.1 pad.3.clone
  8.9 0.1 pad.6.clone
  9.0 0.1 dynamic-slice_convert_fusion
  9.2 0.1 pad_dynamic-slice_fusion
  9.2 0.9 copy.22
  10.2 0.7 convert_element_type.23
  10.9 1.5 fusion
  12.4 3.9 copy.20
  16.3 0.6 broadcast_in_dim.64
  16.9 0.5 fusion.9
  17.5 0.8 pad_maximum_fusion.refs_0_
  18.3 1.3 fusion.2.refs_0_.refs_4_
  19.5 1.0 fusion.4.refs_4_
  20.5 140.0 %gather_weights.1 = (bf16[4,2048,768]{2,1,0:T(8,128)(2,1)}, bf16[4,2048,512]{2,1,0:T(8,128)(2,1)}, bf16[2048,2048]{1,0:T(8,128)(2,1)}, bf16[1024,2048]{1,0:T(8,128)(2,1)}) custom-call(bf16[256,768]{1,0:T(8,128)(2,1)} %pad_maximum_fusion.refs_0_, bf16[256,512]{1,0:T(8,128)(2,1)} %refs_1_.2, bf16[256,2048]{1,0:T(8,128)(2,1)} %refs_2_.2, bf16[256,2048]{1,0:T(8,128)(2,1)} %refs_2_.3), custom_call_target="tpu_custom_call" | custom-call | bytes 20971520 | tf_op jit(solution)/shard_map/gather_weights/pallas_call | solution.py:392
  160.5 1.1 fusion.7
  161.6 43.5 %attend.1 = (bf16[4,256,512]{2,1,0:T(8,128)(2,1)}, bf16[4,768,256]{2,1,0:T(8,128)(2,1)}, bf16[4,256,512]{2,1,0:T(8,128)(2,1)}, f32[4,8,256]{2,1,0:T(8,128)}, bf1...) custom-call(bf16[256,2048]{1,0:T(8,128)(2,1)} %fusion.2.refs_0_.refs_4_, ...), custom_call_target="tpu_custom_call" | custom-call | flops 6979321856 | bytes 20971520 | tf_op jit(solution)/shard_map/attend/pallas_call | solution.py:1758
  205.1 156.9 %feed_forward.1 = (f32[256,2048]{1,0:T(8,128)}, bf16[4,256,2048]{2,1,0:T(8,128)(2,1)}, bf16[4,2048,1024]{2,1,0:T(8,128)(2,1)}, f32[256,2048]{1,0:T(8,128)}) custom-call(bf16[256,2048]{1,0:T(8,128)(2,1)} %get-tuple-element.44.refs_0_, bf16[4,256,2048]{2,1,0:T(8,128)(2,1)} %bitcast.31, bf16[2,2048,1024]{2,1,0:T(8,128)(2,1)} %get-tuple-element.46.refs_2_, ...), custom_call_target="tpu_custom_call" | custom-call | flops 77309411328 | bytes 50331648 | tf_op jit(solution)/shard_map/feed_forward/pallas_call | solution.py:851
  362.0 1.2 fusion.6.refs_6_
  363.1 87.1 %attend_back.1 = (f32[256,2048]{1,0:T(8,128)}, f32[256,2048]{1,0:T(8,128)}, bf16[256,2048]{1,0:T(8,128)(2,1)}, f32[1,2048]{1,0:T(1,128)}, bf16[4,256,768]{2,1,0:...) custom-call(f32[256,2048]{1,0:T(8,128)} %get-tuple-element.49.refs_0, ...), custom_call_target="tpu_custom_call" | custom-call | flops 9395240960 | bytes 37748736 | tf_op jit(solution)/shard_map/attend_back/pallas_call | solution.py:2001
  450.3 112.3 %sum_weights.1 = (f32[256,512]{1,0:T(8,128)}, f32[256,256]{1,0:T(8,128)}, f32[256,512]{1,0:T(8,128)}, bf16[256,2048]{1,0:T(8,128)(2,1)}, f32[2,2048]{1,0:T(2,128)}) custom-call(bf16[256,2048]{1,0:T(8,128)(2,1)} %fusion.2.refs_0_.refs_4_, bf16[256,1024]{1,0:T(8,128)(2,1)} %get-tuple-element.55.refs_1_, bf16[256,2048]{1,0:T(8,128)(2,1)} %get-tuple-element.56.refs_2_, ...), custom_call_target="tpu_custom_call" | custom-call | flops 5368709120 | bytes 20971520 | tf_op jit(solution)/shard_map/sum_weights/pallas_call | solution.py:1513
  562.5 1.8 reshape.104
  564.3 3.3 add_convert_fusion
  567.6 0.6 fusion.13
  568.2 1.0 copy.28
  569.2 0.8 copy.29
  570.0 0.8 copy.30
  570.8 0.3 copy-done.1
  571.1 2.1 copy.31
  573.2 1.0 copy-done.2
  574.2 1.3 copy.32
  (27 shorter events, 0.2 us)
Async XLA Ops:
  7.2 557.2 %reduce-scatter.2.cloned.1.call-start = ((), (), s32[]{:S(2)}) async-start(), calls=%async_computation.1 | async-start | bytes 5242880 | tf_op jit(solution)/shard_map/reduce_scatter | solution.py:2208
  10.9 7.4 %copy-start.7 = (f32[2048]{0:T(1024)}, f32[2048]{0:T(1024)S(1)}, u32[]{:S(2)}) copy-start(f32[2048]{0:T(1024)S(1)} %convert_element_type.23) | copy-start | bytes 24580
  12.4 3.9 copy-start.9
  12.4 5.1 copy-start.6
  12.4 5.8 %copy-start = (bf16[256,2048]{1,0:T(8,128)(2,1)S(1)}, bf16[256,2048]{1,0:T(8,128)(2,1)}, u32[]{:S(2)}) copy-start(bf16[256,2048]{1,0:T(8,128)(2,1)} %refs_9_.1) | copy-start | bytes 3145732
  564.3 3.3 copy-start.8
  564.3 3.9 copy-start.3
  564.3 4.9 copy-start.5
  564.3 5.7 copy-start.4
  568.2 2.9 copy-start.1
  571.1 3.1 copy-start.2
Sparse Core Ops, SparseCore 0:
  362.1 100.7 reduce-scatter.1
